TPU v7x, 32 devices: a whole 2x2x4 slice. The times are simulated.
32 devices in a mesh: wide: 8 (over z, x), narrow: 4 (over y, core).
Axes of the slice: x: 2, y: 2, z: 4, core: 2. Of those that a mesh axis runs over, the one named last changes fastest.
Arguments:
- tokens: bfloat16 [64, 1024, 768], P(('wide', 'narrow')), may hold values from -6 to 6
- item_ids: int32 [64], P(('wide', 'narrow')), may hold values from 0 to 63, as said below
- w_mem: bfloat16 [768, 2304], P(('wide', 'narrow')), may hold values from -0.21875 to 0.21875
- w_qkv: bfloat16 [768, 2304], P(('wide', 'narrow')), may hold values from -0.21875 to 0.21875
- w_out: bfloat16 [768, 768], P(('wide', 'narrow')), may hold values from -6 to 6
- w_up: bfloat16 [768, 3072], P(('wide', 'narrow')), may hold values from -0.21875 to 0.21875
- w_down: bfloat16 [3072, 768], P(('wide', 'narrow')), may hold values from -0.109375 to 0.109375
- mem_tokens: bfloat16 [16, 768], replicated, may hold values from -6 to 6
- gains: bfloat16 [2, 768], replicated, may hold values from 0.5 to 1.5
- w_beta: bfloat16 [768], replicated, may hold values from -0.21875 to 0.21875
- out_grad: bfloat16 [64, 1024, 768], P(('wide', 'narrow')), may hold values from -6 to 6
Outputs:
- block_out: bfloat16 [64, 1024, 768], P(('wide', 'narrow'))
- grad_tokens: float32 [64, 1024, 768], P(('wide', 'narrow'))
- grad_w_mem: float32 [768, 2304], P(('wide', 'narrow'))
- grad_w_qkv: float32 [768, 2304], P(('wide', 'narrow'))
- grad_w_out: float32 [768, 768], P(('wide', 'narrow'))
- grad_w_up: float32 [768, 3072], P(('wide', 'narrow'))
- grad_w_down: float32 [3072, 768], P(('wide', 'narrow'))
- grad_mem_tokens: float32 [16, 768], replicated
- grad_gains: float32 [2, 768], replicated
- grad_w_beta: float32 [768], replicated
Inputs may be any that keep to these rules, and one draw needn't show every extreme that they name: `item_ids`: A segment's number is the index, counted from 0 over all 64 segments, of the first segment of its item; an item's segments are consecutive and lie in one group of 2; every group begins a new item; an item has 1 to 2 segments.
All inputs are finite; a program needn't handle non-finite values.
Results may differ from a plain program's by a relative error of at most 0.017.
Values may be sent and summed in bfloat16 or wider, within the bound.
A program may use at most 448 MiB of HBM per device.

v0:
```python
import jax
import jax.numpy as jnp
from jax import lax
from jax.sharding import PartitionSpec as P

HD = 64


highest = lax.Precision.HIGHEST
eps_norm = 1e-05
score_scale = 0.125


def product(left, right):
    return jnp.dot(left, right, preferred_element_type=jnp.float32)


def contract_rows(left, right):
    return lax.dot_general(
        left, right, (((0,), (0,)), ((), ())), preferred_element_type=jnp.float32
    )


def contract_cols(left, right):
    return lax.dot_general(
        left, right, (((1,), (1,)), ((), ())), preferred_element_type=jnp.float32
    )


def layer_norm(values, gain):
    average = jnp.mean(values, axis=-1, keepdims=True)
    centered = values - average
    spread = jnp.mean(centered * centered, axis=-1, keepdims=True)
    return centered * lax.rsqrt(spread + eps_norm) * gain


def feature_map(values):
    softer = jax.nn.softplus(values)
    return jnp.concatenate(
        [softer * jnp.roll(softer, offset, axis=-1) for offset in (1, 2, 3)], axis=-1
    )


def gelu_tanh(values):
    return jax.nn.gelu(values, approximate=True)


def normalized(numerator, phi_rows, normalizer):
    return numerator / (1.0 + jnp.dot(phi_rows, normalizer, precision=highest))[:, None]


def write_terms(mem_out, w_beta, values, recall, phi_keys, normalizer):
    beta = jax.nn.sigmoid(jnp.dot(mem_out, w_beta, precision=highest))
    recalled = normalized(recall, phi_keys, normalizer)
    delta = beta[:, None] * (values - recalled)
    grown = jnp.dot(beta, phi_keys, precision=highest)
    return (delta, grown)


def accumulate(total, term):
    if total is None:
        return term
    return total + term


def query_blocks(rows, seg_rows):
    half = seg_rows // 2
    return [(0, half, half), (half, rows - half, rows)]


def masked_scores(queries, keys_all, start):
    count = queries.shape[1]
    reach = keys_all.shape[1]
    raw = (
        jnp.einsum("hqd,hkd->hqk", queries, keys_all, preferred_element_type=jnp.float32)
        * score_scale
    )
    positions = lax.broadcasted_iota(jnp.int32, (count, reach), 0) + start
    columns = lax.broadcasted_iota(jnp.int32, (count, reach), 1)
    return jnp.where((positions >= columns)[None], raw, -1e30)


def heads_first(block, width):
    rows = block.shape[0]
    return block.reshape(rows, width // HD, HD).transpose(1, 0, 2)


def rows_first(block):
    heads, rows, size = block.shape
    return block.transpose(1, 0, 2).reshape(rows, heads * size)


def split_heads(qkv_low, width):
    queries = heads_first(qkv_low[:, :width], width)
    keys_all = heads_first(qkv_low[:, width : 2 * width], width)
    values_all = heads_first(qkv_low[:, 2 * width :], width)
    return (queries, keys_all, values_all)


def add_prefix(total, part):
    reach = part.shape[1]
    if total is None:
        return part
    if reach == total.shape[1]:
        return total + part
    return jnp.concatenate([total[:, :reach] + part, total[:, reach:]], axis=1)


def forward_segment(full, inputs, memory, normalizer, reads, writes):
    w_mem, w_qkv, w_out, w_up, w_down, mem_tokens, gains, w_beta = full
    seg_rows, width = inputs.shape
    first = jnp.concatenate([inputs, mem_tokens], axis=0)
    rows = first.shape[0]
    memory_low = memory.astype(jnp.bfloat16)
    kept = {"first": first, "memory_low": memory_low}
    if reads:
        query_mem = product(first, w_mem[:, :width])
        phi_query, phi_query_pull = jax.vjp(feature_map, query_mem)
        phi_query_low = phi_query.astype(jnp.bfloat16)
        numerator = product(phi_query_low, memory_low)
        read_out, read_pull = jax.vjp(normalized, numerator, phi_query, normalizer)
        states_one = first.astype(jnp.float32) + read_out
        kept["phi_query_pull"] = phi_query_pull
        kept["phi_query_low"] = phi_query_low
        kept["read_pull"] = read_pull
    else:
        states_one = first.astype(jnp.float32)
    normed_one, norm_one_pull = jax.vjp(layer_norm, states_one, gains[0].astype(jnp.float32))
    normed_one_low = normed_one.astype(jnp.bfloat16)
    qkv_low = product(normed_one_low, w_qkv).astype(jnp.bfloat16)
    queries, keys_all, values_all = split_heads(qkv_low, width)
    attended_parts = []
    log_totals = []
    for start, count, reach in query_blocks(rows, seg_rows):
        masked = masked_scores(queries[:, start : start + count], keys_all[:, :reach], start)
        peak = jnp.max(masked, axis=-1, keepdims=True)
        log_total = peak + jnp.log(jnp.sum(jnp.exp(masked - peak), axis=-1, keepdims=True))
        probs_low = jnp.exp(masked - log_total).astype(jnp.bfloat16)
        attended_parts.append(
            jnp.einsum(
                "hqk,hkd->hqd", probs_low, values_all[:, :reach], preferred_element_type=jnp.float32
            )
        )
        log_totals.append(log_total)
    attended_low = rows_first(jnp.concatenate(attended_parts, axis=1)).astype(jnp.bfloat16)
    states_two = states_one + product(attended_low, w_out)
    normed_two, norm_two_pull = jax.vjp(layer_norm, states_two, gains[1].astype(jnp.float32))
    normed_two_low = normed_two.astype(jnp.bfloat16)
    upward = product(normed_two_low, w_up)
    activated, gelu_pull = jax.vjp(gelu_tanh, upward)
    activated_low = activated.astype(jnp.bfloat16)
    states_three = states_two + product(activated_low, w_down)
    output = states_three[:seg_rows].astype(jnp.bfloat16)
    kept.update(
        {
            "norm_one_pull": norm_one_pull,
            "normed_one_low": normed_one_low,
            "qkv_low": qkv_low,
            "log_totals": log_totals,
            "attended_low": attended_low,
            "norm_two_pull": norm_two_pull,
            "normed_two_low": normed_two_low,
            "gelu_pull": gelu_pull,
            "activated_low": activated_low,
        }
    )
    if writes:
        mem_out = states_three[seg_rows:]
        mem_out_low = mem_out.astype(jnp.bfloat16)
        key_value = product(mem_out_low, w_mem[:, width:])
        phi_keys, phi_keys_pull = jax.vjp(feature_map, key_value[:, :width])
        phi_keys_low = phi_keys.astype(jnp.bfloat16)
        recall = product(phi_keys_low, memory_low)
        (delta, grown), write_pull = jax.vjp(
            write_terms,
            mem_out,
            w_beta.astype(jnp.float32),
            key_value[:, width:],
            recall,
            phi_keys,
            normalizer,
        )
        delta_low = delta.astype(jnp.bfloat16)
        memory = memory + contract_rows(phi_keys_low, delta_low)
        normalizer = normalizer + grown
        kept["mem_out_low"] = mem_out_low
        kept["phi_keys_pull"] = phi_keys_pull
        kept["phi_keys_low"] = phi_keys_low
        kept["write_pull"] = write_pull
        kept["delta_low"] = delta_low
    return (output, memory, normalizer, kept)


def backward_segment(full, kept, seg_grad, grad_memory, grad_normal, reads, writes, totals):
    w_mem, w_qkv, w_out, w_up, w_down, mem_tokens, gains, w_beta = full
    seg_rows, width = seg_grad.shape
    rows = seg_rows + mem_tokens.shape[0]
    grad_states = jnp.concatenate(
        [seg_grad, jnp.zeros((rows - seg_rows, width), jnp.float32)], axis=0
    )
    grad_memory_low = None
    if writes:
        grad_increment = grad_memory.astype(jnp.bfloat16)
        grad_phi_keys = contract_cols(kept["delta_low"], grad_increment)
        grad_delta = product(kept["phi_keys_low"], grad_increment)
        grad_mem_out, grad_beta_w, grad_values, grad_recall, grad_phi_part, grad_normal_part = kept[
            "write_pull"
        ]((grad_delta, grad_normal))
        grad_recall_low = grad_recall.astype(jnp.bfloat16)
        grad_phi_keys = (
            grad_phi_keys + grad_phi_part + contract_cols(grad_recall_low, kept["memory_low"])
        )
        grad_memory_low = contract_rows(kept["phi_keys_low"], grad_recall_low)
        (grad_key,) = kept["phi_keys_pull"](grad_phi_keys)
        grad_kv_low = jnp.concatenate([grad_key, grad_values], axis=1).astype(jnp.bfloat16)
        totals["mem_kv"] = accumulate(
            totals["mem_kv"], contract_rows(kept["mem_out_low"], grad_kv_low)
        )
        grad_mem_rows = grad_mem_out + contract_cols(grad_kv_low, w_mem[:, width:])
        grad_states = jnp.concatenate(
            [grad_states[:seg_rows], grad_states[seg_rows:] + grad_mem_rows], axis=0
        )
        totals["beta"] = accumulate(totals["beta"], grad_beta_w)
        grad_normal = grad_normal + grad_normal_part
    grad_down_low = grad_states.astype(jnp.bfloat16)
    totals["down"] = accumulate(totals["down"], contract_rows(kept["activated_low"], grad_down_low))
    grad_activated = contract_cols(grad_down_low, w_down)
    (grad_upward,) = kept["gelu_pull"](grad_activated)
    grad_upward_low = grad_upward.astype(jnp.bfloat16)
    totals["up"] = accumulate(totals["up"], contract_rows(kept["normed_two_low"], grad_upward_low))
    grad_normed_two = contract_cols(grad_upward_low, w_up)
    grad_states_two, grad_gain_two = kept["norm_two_pull"](grad_normed_two)
    grad_states = grad_states + grad_states_two
    grad_attn_low = grad_states.astype(jnp.bfloat16)
    totals["out"] = accumulate(totals["out"], contract_rows(kept["attended_low"], grad_attn_low))
    grad_attended = heads_first(contract_cols(grad_attn_low, w_out).astype(jnp.bfloat16), width)
    queries, keys_all, values_all = split_heads(kept["qkv_low"], width)
    grad_query_parts = []
    grad_keys = None
    grad_values_all = None
    pairs = list(zip(query_blocks(rows, seg_rows), kept["log_totals"]))
    for (start, count, reach), log_total in reversed(pairs):
        block_queries = queries[:, start : start + count]
        block_keys = keys_all[:, :reach]
        masked = masked_scores(block_queries, block_keys, start)
        probs = jnp.exp(masked - log_total)
        probs_low = probs.astype(jnp.bfloat16)
        block_grad = grad_attended[:, start : start + count]
        grad_probs = jnp.einsum(
            "hqd,hkd->hqk", block_grad, values_all[:, :reach], preferred_element_type=jnp.float32
        )
        grad_values_all = add_prefix(
            grad_values_all,
            jnp.einsum("hqk,hqd->hkd", probs_low, block_grad, preferred_element_type=jnp.float32),
        )
        inner = jnp.sum(grad_probs * probs, axis=-1, keepdims=True)
        grad_raw_low = (probs * (grad_probs - inner) * score_scale).astype(jnp.bfloat16)
        grad_query_parts.insert(
            0,
            jnp.einsum(
                "hqk,hkd->hqd", grad_raw_low, block_keys, preferred_element_type=jnp.float32
            ),
        )
        grad_keys = add_prefix(
            grad_keys,
            jnp.einsum(
                "hqk,hqd->hkd", grad_raw_low, block_queries, preferred_element_type=jnp.float32
            ),
        )
    grad_queries = jnp.concatenate(grad_query_parts, axis=1)
    grad_qkv_low = jnp.concatenate(
        [rows_first(grad_queries), rows_first(grad_keys), rows_first(grad_values_all)], axis=1
    ).astype(jnp.bfloat16)
    totals["qkv"] = accumulate(totals["qkv"], contract_rows(kept["normed_one_low"], grad_qkv_low))
    grad_normed_one = contract_cols(grad_qkv_low, w_qkv)
    grad_states_one, grad_gain_one = kept["norm_one_pull"](grad_normed_one)
    grad_states = grad_states + grad_states_one
    totals["gains"] = accumulate(totals["gains"], jnp.stack([grad_gain_one, grad_gain_two]))
    if reads:
        grad_numerator, grad_phi_query, grad_normal_read = kept["read_pull"](grad_states)
        grad_numerator_low = grad_numerator.astype(jnp.bfloat16)
        grad_phi_query = grad_phi_query + contract_cols(grad_numerator_low, kept["memory_low"])
        grad_memory_low = accumulate(
            grad_memory_low, contract_rows(kept["phi_query_low"], grad_numerator_low)
        )
        (grad_query_mem,) = kept["phi_query_pull"](grad_phi_query)
        grad_query_low = grad_query_mem.astype(jnp.bfloat16)
        totals["mem_q"] = accumulate(totals["mem_q"], contract_rows(kept["first"], grad_query_low))
        grad_first = grad_states + contract_cols(grad_query_low, w_mem[:, :width])
        grad_normal = grad_normal + grad_normal_read
    else:
        grad_first = grad_states
    totals["tokens"] = accumulate(totals["tokens"], grad_first[seg_rows:])
    if grad_memory_low is not None:
        grad_memory = grad_memory + grad_memory_low
    return (grad_first[:seg_rows], grad_memory, grad_normal, totals)


def on_device(
    tokens, item_ids, w_mem, w_qkv, w_out, w_up, w_down, mem_tokens, gains, w_beta, out_grad
):
    gathered = (
        lax.all_gather(w_mem, ("wide", "narrow"), axis=0, tiled=True),
        lax.all_gather(w_qkv, ("wide", "narrow"), axis=0, tiled=True),
        lax.all_gather(w_out, ("wide", "narrow"), axis=0, tiled=True),
        lax.all_gather(w_up, ("wide", "narrow"), axis=0, tiled=True),
        lax.all_gather(w_down, ("wide", "narrow"), axis=0, tiled=True),
    )
    full = (
        gathered[0],
        gathered[1],
        gathered[2],
        gathered[3],
        gathered[4],
        mem_tokens,
        gains,
        w_beta,
    )
    slots, seg_rows, width = tokens.shape
    same_item = item_ids[1:] == item_ids[:-1]
    flags = jnp.concatenate(
        [jnp.zeros((1,), jnp.float32), jnp.where(same_item, 1.0, 0.0).astype(jnp.float32)]
    )
    memory = jnp.zeros((3 * width, width), jnp.float32)
    normalizer = jnp.zeros((3 * width,), jnp.float32)
    outputs = []
    kept_all = []
    for slot in range(slots):
        memory = memory * flags[slot]
        normalizer = normalizer * flags[slot]
        output, memory, normalizer, kept = forward_segment(
            full, tokens[slot], memory, normalizer, slot > 0, slot + 1 < slots
        )
        outputs.append(output)
        kept_all.append(kept)
    gathered = (
        lax.all_gather(w_mem, ("wide", "narrow"), axis=0, tiled=True),
        lax.all_gather(w_qkv, ("wide", "narrow"), axis=0, tiled=True),
        lax.all_gather(w_out, ("wide", "narrow"), axis=0, tiled=True),
        lax.all_gather(w_up, ("wide", "narrow"), axis=0, tiled=True),
        lax.all_gather(w_down, ("wide", "narrow"), axis=0, tiled=True),
    )
    full = (
        gathered[0],
        gathered[1],
        gathered[2],
        gathered[3],
        gathered[4],
        mem_tokens,
        gains,
        w_beta,
    )
    totals = {
        "mem_q": None,
        "mem_kv": None,
        "qkv": None,
        "out": None,
        "up": None,
        "down": None,
        "tokens": None,
        "gains": None,
        "beta": None,
    }
    grad_memory = jnp.zeros((3 * width, width), jnp.float32)
    grad_normal = jnp.zeros((3 * width,), jnp.float32)
    grad_inputs = [None] * slots
    for slot in reversed(range(slots)):
        grad_in, grad_memory, grad_normal, totals = backward_segment(
            full,
            kept_all[slot],
            out_grad[slot].astype(jnp.float32),
            grad_memory,
            grad_normal,
            slot > 0,
            slot + 1 < slots,
            totals,
        )
        grad_memory = grad_memory * flags[slot]
        grad_normal = grad_normal * flags[slot]
        grad_inputs[slot] = grad_in
    mem_query = (
        totals["mem_q"] if totals["mem_q"] is not None else jnp.zeros((width, width), jnp.float32)
    )
    mem_pair = (
        totals["mem_kv"]
        if totals["mem_kv"] is not None
        else jnp.zeros((width, 2 * width), jnp.float32)
    )
    beta_total = totals["beta"] if totals["beta"] is not None else jnp.zeros((width,), jnp.float32)
    mem_total = jnp.concatenate([mem_query, mem_pair], axis=1)
    summed = (
        lax.psum_scatter(mem_total, ("wide", "narrow"), scatter_dimension=0, tiled=True),
        lax.psum_scatter(totals["qkv"], ("wide", "narrow"), scatter_dimension=0, tiled=True),
        lax.psum_scatter(totals["out"], ("wide", "narrow"), scatter_dimension=0, tiled=True),
        lax.psum_scatter(totals["up"], ("wide", "narrow"), scatter_dimension=0, tiled=True),
        lax.psum_scatter(totals["down"], ("wide", "narrow"), scatter_dimension=0, tiled=True),
    )
    small_sums = lax.psum((totals["tokens"], totals["gains"], beta_total), ("wide", "narrow"))
    return (
        jnp.stack(outputs),
        jnp.stack(grad_inputs),
        summed[0],
        summed[1],
        summed[2],
        summed[3],
        summed[4],
        small_sums[0],
        small_sums[1],
        small_sums[2],
    )


def solution(mesh):
    in_specs = (
        P(("wide", "narrow"), None, None),
        P(("wide", "narrow")),
        P(("wide", "narrow"), None),
        P(("wide", "narrow"), None),
        P(("wide", "narrow"), None),
        P(("wide", "narrow"), None),
        P(("wide", "narrow"), None),
        P(),
        P(),
        P(),
        P(("wide", "narrow"), None, None),
    )
    out_specs = (
        P(("wide", "narrow"), None, None),
        P(("wide", "narrow"), None, None),
        P(("wide", "narrow"), None),
        P(("wide", "narrow"), None),
        P(("wide", "narrow"), None),
        P(("wide", "narrow"), None),
        P(("wide", "narrow"), None),
        P(),
        P(),
        P(),
    )
    return jax.shard_map(
        on_device, mesh=mesh, in_specs=in_specs, out_specs=out_specs, check_vma=False
    )
```

profile of v0, /device:TPU:0, one launch (start us, length us, event | category | flops | bytes accessed | tf_op | source)
XLA Modules:
  0.0 1588.1 jit_solution(18157704289271722582)
XLA Ops:
  22.8 51.0 %all-gather.6.cloned.1.call-done = bf16[768,2304]{1,0:T(8,128)(2,1)} async-done(((bf16[24,2304]{1,0:T(8,128)(2,1)}), bf16[768,2304]{1,0:T(8,128)(2,1)}) %all-gather.6.cloned.1.call-update) | async-done | bytes 3538960 | tf_op jit(solution)/shard_map/all_gather | solution.py:304
  92.2 14.7 fusion.320
  110.9 24.8 %all-gather.14.cloned.1.call-done = bf16[768,2304]{1,0:T(8,128)(2,1)} async-done(((bf16[24,2304]{1,0:T(8,128)(2,1)}), bf16[768,2304]{1,0:T(8,128)(2,1)}) %all-gather.14.cloned.1.call-update) | async-done | bytes 3538960 | tf_op jit(solution)/shard_map/all_gather | solution.py:303
  149.3 11.8 exponential_reduce_fusion.1
  161.2 8.7 convolution_convert_fusion.5
  169.8 12.6 fusion.141
  203.8 53.1 %all-gather.10.cloned.1.call-done = bf16[768,3072]{1,0:T(8,128)(2,1)} async-done(((bf16[24,3072]{1,0:T(8,128)(2,1)}), bf16[768,3072]{1,0:T(8,128)(2,1)}) %all-gather.10.cloned.1.call-update) | async-done | bytes 4718608 | tf_op jit(solution)/shard_map/all_gather | solution.py:306
  256.8 11.3 fusion.306
  268.2 53.8 %all-gather.12.cloned.1.call-done = bf16[3072,768]{1,0:T(8,128)(2,1)} async-done(((bf16[96,768]{1,0:T(8,128)(2,1)}), bf16[3072,768]{1,0:T(8,128)(2,1)}) %all-gather.12.cloned.1.call-update) | async-done | bytes 4718608 | tf_op jit(solution)/shard_map/all_gather | solution.py:307
  322.0 11.9 convolution_add_fusion.6
  338.5 8.3 fusion.166
  347.4 8.4 fusion.316
  375.5 13.9 fusion.322
  395.6 11.9 exponential_reduce_fusion
  412.1 11.9 fusion.144
  430.3 8.5 fusion.308
  438.8 16.1 %fusion.27 = bf16[1040,3072]{1,0:T(8,128)(2,1)S(1)} fusion(f32[1040,3072]{1,0:T(8,128)} %fusion.308, bf16[3072,768]{1,0:T(8,128)(2,1)} %all-gather.12.cloned.1.call-done, bf16[1024,768]{1,0:T(8,128)(2,1)S(1)} %copy-done.41), kind=kOutput, calls=%fused_computation.38 | convolution fusion | flops 4971233280 | bytes 25460736 | tf_op jit(solution)/shard_map/dot_general | solution.py:25
  454.9 10.9 multiply_reduce_fusion.5
  480.7 11.6 fusion.185
  492.2 58.3 %fusion.150 = bf16[12,528,64]{1,2,0:T(8,128)(2,1)} fusion(bf16[12,1040,64]{1,2,0:T(8,128)(2,1)} %bitcast.168, f32[12,528,1040]{2,1,0:T(8,128)} %fusion.185, f32[12,528,1040]{2,1,0:T(8,128)} %get-tuple-element.74, f32[12,528]{1,0:T(8,128)} %copy-done.104), kind=kOutput, calls=%fused_computation.211 | convolution fusion | flops 889987264 | bytes 55149312 | tf_op jit(solution)/shard_map/hqk,hkd->hqd/dot_general | solution.py:260
  550.6 59.4 %fusion.37 = f32[12,1040,64]{1,2,0:T(8,128)} fusion(f32[12,528,1040]{2,1,0:T(8,128)} %fusion.185, f32[12,528,1040]{2,1,0:T(8,128)} %get-tuple-element.74, f32[12,528]{1,0:T(8,128)} %copy-done.104, bf16[12,1040,64]{1,2,0:T(8,128)(2,1)S(1)} %bitcast.176), kind=kOutput, calls=%fused_computation.61 | convolution fusion | flops 889581760 | bytes 121044992 | tf_op jit(solution)/shard_map/hqk,hqd->hkd/dot_general | solution.py:266
  610.0 20.4 %fusion.157 = bf16[12,512,64]{1,2,0:T(8,128)(2,1)} fusion(f32[12,512,512]{1,2,0:T(8,128)} %fusion.197, f32[12,512,512]{1,2,0:T(8,128)} %copy-done.5, f32[12,512]{1,0:T(8,128)} %copy-done.148, pred[512,512]{0,1:T(8,128)(4,1)} %copy-done.38, bf16[12,1040,64]{1,2,0:T(8,128)(2,1)} %bitcast.169), kind=kOutput, calls=%fused_computation.212 | convolution fusion | flops 437656064 | bytes 52494336 | tf_op jit(solution)/shard_map/hqk,hkd->hqd/dot_general | solution.py:260
  630.4 21.6 %fusion.140 = bf16[12,512,64]{1,2,0:T(8,128)(2,1)} fusion(f32[12,1040,64]{1,2,0:T(8,128)} %fusion.37, f32[12,512,512]{1,2,0:T(8,128)} %fusion.197, f32[12,512,512]{1,2,0:T(8,128)} %copy-done.5, f32[12,512]{1,0:T(8,128)} %copy-done.148, pred[512,512]{0,1:T(8,128)(4,1)} %copy-done.38, bf16[12,1040,64]{1,2,0:T(8,128)(2,1)S(1)} %bitcast.177), kind=kOutput, calls=%fused_computation.202 | convolution fusion | flops 438049280 | bytes 54067200 | tf_op jit(solution)/shard_map/hqk,hqd->hkd/dot_general | solution.py:266
  653.7 11.5 fusion.101
  707.9 16.4 %fusion.20 = bf16[1040,3072]{1,0:T(8,128)(2,1)} fusion(f32[1040,3072]{1,0:T(8,128)} %fusion.306, bf16[3072,768]{1,0:T(8,128)(2,1)} %all-gather.12.cloned.1.call-done, f32[16,768]{1,0:T(8,128)S(1)} %fusion.163, f32[1024,768]{1,0:T(8,128)S(1)} %copy-done.31), kind=kOutput, calls=%fused_computation.31 | convolution fusion | flops 4974428160 | bytes 27082752 | tf_op jit(solution)/shard_map/dot_general | solution.py:25
  724.4 10.6 multiply_reduce_fusion.4
  750.2 11.6 fusion.182
  761.8 58.0 %fusion.147 = bf16[12,528,64]{1,2,0:T(8,128)(2,1)} fusion(bf16[12,1040,64]{1,2,0:T(8,128)(2,1)} %bitcast.164, f32[12,528,1040]{2,1,0:T(8,128)} %fusion.182, f32[12,528,1040]{2,1,0:T(8,128)} %get-tuple-element.63, f32[12,528]{1,0:T(8,128)} %copy-done.103), kind=kOutput, calls=%fused_computation.210 | convolution fusion | flops 889987264 | bytes 55149312 | tf_op jit(solution)/shard_map/hqk,hkd->hqd/dot_general | solution.py:260
  819.8 59.2 %fusion.43 = f32[12,1040,64]{1,2,0:T(8,128)} fusion(f32[12,528,1040]{2,1,0:T(8,128)} %fusion.182, f32[12,528,1040]{2,1,0:T(8,128)} %get-tuple-element.63, f32[12,528]{1,0:T(8,128)} %copy-done.103, bf16[12,1040,64]{1,2,0:T(8,128)(2,1)S(1)} %bitcast.172), kind=kOutput, calls=%fused_computation.63 | convolution fusion | flops 889581760 | bytes 121044992 | tf_op jit(solution)/shard_map/hqk,hqd->hkd/dot_general | solution.py:266
  879.0 20.8 %fusion.160 = bf16[12,512,64]{1,2,0:T(8,128)(2,1)} fusion(f32[12,512,512]{1,2,0:T(8,128)} %fusion.194, f32[12,512,512]{1,2,0:T(8,128)} %copy-done.4, f32[12,512]{1,0:T(8,128)} %copy-done.146, pred[512,512]{0,1:T(8,128)(4,1)} %copy-done.38, bf16[12,1040,64]{1,2,0:T(8,128)(2,1)} %bitcast.165), kind=kOutput, calls=%fused_computation.213 | convolution fusion | flops 437656064 | bytes 52494336 | tf_op jit(solution)/shard_map/hqk,hkd->hqd/dot_general | solution.py:260
  899.8 21.3 %fusion.138 = bf16[12,512,64]{1,2,0:T(8,128)(2,1)} fusion(f32[12,1040,64]{1,2,0:T(8,128)} %fusion.43, f32[12,512,512]{1,2,0:T(8,128)} %fusion.194, f32[12,512,512]{1,2,0:T(8,128)} %copy-done.4, f32[12,512]{1,0:T(8,128)} %copy-done.146, pred[512,512]{0,1:T(8,128)(4,1)} %copy-done.38, bf16[12,1040,64]{1,2,0:T(8,128)(2,1)S(1)} %bitcast.173), kind=kOutput, calls=%fused_computation.198 | convolution fusion | flops 438049280 | bytes 54067200 | tf_op jit(solution)/shard_map/hqk,hqd->hkd/dot_general | solution.py:266
  922.8 11.7 fusion.105
  934.5 7.5 fusion.137
  955.2 8.2 fusion.125
  963.5 11.3 convolution_add_fusion.1
  975.5 7.3 convolution_add_fusion
  999.7 8.6 fusion.118
  1015.9 10.1 fusion.175
  1026.0 13.4 convolution_add_fusion.2
  1041.3 9.1 fusion.307
  1050.4 12.7 convolution_add_fusion.3
  1063.1 9.2 fusion.114
  1081.7 41.4 %all-reduce.13 = (f32[16,768]{1,0:T(8,128)}, f32[2,768]{1,0:T(2,128)}, f32[768]{0:T(1024)}) all-reduce(f32[16,768]{1,0:T(8,128)S(1)} %slice_add_fusion.5, f32[2,768]{1,0:T(2,128)S(1)} %maximum_add_fusion, f32[768]{0:T(1024)S(1)} %convolution_reduce_fusion.1), channel_id=1, replica_groups=mesh['wide'=8,'narrow'=4] {'wide','narrow'}, use_global_device_ids=true, to_apply=%region_36.37 | all-reduce | flops 14592 | bytes 116736 | tf_op jit(solution)/shard_map/psum | solution.py:398
  1125.2 11.7 fusion.312
  1144.7 28.5 %reduce-scatter.8.cloned.1.call-done = f32[24,2304]{1,0:T(8,128)} async-done(((f32[768,2304]{1,0:T(8,128)}), f32[24,2304]{1,0:T(8,128)}) %reduce-scatter.8.cloned.1.call-update) | async-done | bytes 221200 | tf_op jit(solution)/shard_map/reduce_scatter | solution.py:393
  1173.1 124.6 %reduce-scatter.6.cloned.1.call-done = f32[24,2304]{1,0:T(8,128)} async-done(((f32[768,2304]{1,0:T(8,128)}), f32[24,2304]{1,0:T(8,128)}) %reduce-scatter.6.cloned.1.call-update) | async-done | bytes 221200 | tf_op jit(solution)/shard_map/reduce_scatter | solution.py:392
  1297.8 142.2 %reduce-scatter.14.cloned.1.call-done = f32[96,768]{1,0:T(8,128)} async-done(((f32[3072,768]{1,0:T(8,128)}), f32[96,768]{1,0:T(8,128)}) %reduce-scatter.14.cloned.1.call-update) | async-done | bytes 294928 | tf_op jit(solution)/shard_map/reduce_scatter | solution.py:396
  1440.0 141.1 %reduce-scatter.12.cloned.1.call-done = f32[24,3072]{1,0:T(8,128)} async-done(((f32[768,3072]{1,0:T(8,128)}), f32[24,3072]{1,0:T(8,128)}) %reduce-scatter.12.cloned.1.call-update) | async-done | bytes 294928 | tf_op jit(solution)/shard_map/reduce_scatter | solution.py:395
  (517 shorter events, 247.0 us)
Async XLA Ops:
  7.2 66.6 %all-gather.6.cloned.1.call-start = ((), (), s32[]{:S(2)}) async-start(), calls=%async_computation.5 | async-start | bytes 3649536 | tf_op jit(solution)/shard_map/all_gather | solution.py:304
  7.9 127.8 %all-gather.14.cloned.1.call-start = ((), (), s32[]{:S(2)}) async-start(), calls=%async_computation.9 | async-start | bytes 3649536 | tf_op jit(solution)/shard_map/all_gather | solution.py:303
  8.7 182.9 %all-gather.8.cloned.1.call-start = ((), (), s32[]{:S(2)}) async-start(), calls=%async_computation.6 | async-start | bytes 1216512 | tf_op jit(solution)/shard_map/all_gather | solution.py:305
  9.4 247.4 %all-gather.10.cloned.1.call-start = ((), (), s32[]{:S(2)}) async-start(), calls=%async_computation.7 | async-start | bytes 4866048 | tf_op jit(solution)/shard_map/all_gather | solution.py:306
  10.0 312.0 %all-gather.12.cloned.1.call-start = ((), (), s32[]{:S(2)}) async-start(), calls=%async_computation.8 | async-start | bytes 4866048 | tf_op jit(solution)/shard_map/all_gather | solution.py:307
  10.6 1134.1 %reduce-scatter.10.cloned.1.call-start = ((), (), s32[]{:S(2)}) async-start(), calls=%async_computation.12 | async-start | bytes 2433024 | tf_op jit(solution)/shard_map/reduce_scatter | solution.py:394
  10.7 396.8 %copy-start.38 = (pred[512,512]{0,1:T(8,128)(4,1)}, pred[512,512]{0,1:T(8,128)(4,1)S(1)}, u32[]{:S(2)}) copy-start(pred[512,512]{0,1:T(8,128)(4,1)S(1)} %iota_compare_fusion.1) | copy-start | bytes 786436
  16.1 57.7 %copy-start.7 = (bf16[1024,768]{1,0:T(8,128)(2,1)}, bf16[1024,768]{1,0:T(8,128)(2,1)S(1)}, u32[]{:S(2)}) copy-start(bf16[1024,768]{1,0:T(8,128)(2,1)S(1)} %get-tuple-element.50) | copy-start | bytes 4718596
  16.4 57.4 %copy-start.112 = (f32[1040]{0:T(1024)}, f32[1040]{0:T(1024)S(1)}, u32[]{:S(2)}) copy-start(f32[1040]{0:T(1024)S(1)} %broadcast_multiply_fusion.5) | copy-start | bytes 12484
  17.1 56.7 %copy-start.130 = (f32[1040]{0:T(1024)}, f32[1040]{0:T(1024)S(1)}, u32[]{:S(2)}) copy-start(f32[1040]{0:T(1024)S(1)} %fusion.233) | copy-start | bytes 12484
  17.1 340.4 %copy-start.135 = (f32[768]{0:T(1024)}, f32[768]{0:T(1024)S(1)}, u32[]{:S(2)}) copy-start(f32[768]{0:T(1024)S(1)} %get-tuple-element.21) | copy-start | bytes 9220
  17.1 448.8 %copy-start.87 = (f32[768]{0:T(1024)}, f32[768]{0:T(1024)S(1)}, u32[]{:S(2)}) copy-start(f32[768]{0:T(1024)S(1)} %get-tuple-element.20) | copy-start | bytes 9220
  92.2 14.7 copy-start.4
  141.4 56.5 %copy-start = (f32[1040,768]{1,0:T(8,128)}, f32[1040,768]{1,0:T(8,128)S(1)}, u32[]{:S(2)}) copy-start(f32[1040,768]{1,0:T(8,128)S(1)} %get-tuple-element.70) | copy-start | bytes 9584644
  149.2 11.9 copy-start.146
  149.3 11.8 copy-start.106
  149.3 11.9 copy-start.10
  195.7 61.2 %copy-start.84 = (f32[1040]{0:T(1024)}, f32[1040]{0:T(1024)S(1)}, u32[]{:S(2)}) copy-start(f32[1040]{0:T(1024)S(1)} %broadcast_multiply_fusion.4) | copy-start | bytes 12484
  197.9 59.0 %copy-start.90 = (f32[1040]{0:T(1024)}, f32[1040]{0:T(1024)S(1)}, u32[]{:S(2)}) copy-start(f32[1040]{0:T(1024)S(1)} %fusion.234) | copy-start | bytes 12484
  256.8 65.2 %copy-start.13 = (f32[1040,768]{1,0:T(8,128)S(1)}, f32[1040,768]{1,0:T(8,128)}, u32[]{:S(2)}) copy-start(f32[1040,768]{1,0:T(8,128)} %copy-done.12) | copy-start | bytes 9584644
  322.0 11.9 copy-start.74
  322.0 16.4 %copy-start.54 = (f32[1040,768]{1,0:T(8,128)S(1)}, f32[1040,768]{1,0:T(8,128)}, u32[]{:S(2)}) copy-start(f32[1040,768]{1,0:T(8,128)} %get-tuple-element.46) | copy-start | bytes 9584644
  334.8 12.0 copy-start.95
  334.8 12.0 copy-start.97
  334.8 12.0 copy-start.99
  375.5 13.9 copy-start.5
  392.8 14.7 copy-start.148
  395.6 13.0 copy-start.6
  429.7 36.2 %copy-start.2 = (f32[1040,768]{1,0:T(8,128)}, f32[1040,768]{1,0:T(8,128)S(1)}, u32[]{:S(2)}) copy-start(f32[1040,768]{1,0:T(8,128)S(1)} %get-tuple-element.78) | copy-start | bytes 9584644
  429.7 36.2 %copy-start.108 = (f32[1040]{0:T(1024)}, f32[1040]{0:T(1024)S(1)}, u32[]{:S(2)}) copy-start(f32[1040]{0:T(1024)S(1)} %broadcast_multiply_fusion.2) | copy-start | bytes 12484
  430.3 35.6 %copy-start.110 = (f32[1040]{0:T(1024)}, f32[1040]{0:T(1024)S(1)}, u32[]{:S(2)}) copy-start(f32[1040]{0:T(1024)S(1)} %fusion.236) | copy-start | bytes 12484
  467.2 217.5 %copy-start.144 = (f32[1040]{0:T(1024)}, f32[1040]{0:T(1024)S(1)}, u32[]{:S(2)}) copy-start(f32[1040]{0:T(1024)S(1)} %negate_multiply_fusion.3) | copy-start | bytes 12484
  492.2 58.3 %copy-start.37 = (bf16[1040,768]{0,1:T(8,128)(2,1)S(1)}, bf16[1040,768]{0,1:T(8,128)(2,1)}, u32[]{:S(2)}) copy-start(bf16[1040,768]{0,1:T(8,128)(2,1)} %copy.42) | copy-start | bytes 4792324
  653.7 11.5 copy-start.39
  706.7 17.6 %copy-start.166 = (f32[16]{0:T(128)}, f32[16]{0:T(128)S(1)}, u32[]{:S(2)}) copy-start(f32[16]{0:T(128)S(1)} %fusion.170) | copy-start | bytes 196
  707.6 28.6 %copy-start.139 = (f32[16,768]{1,0:T(8,128)}, f32[16,768]{1,0:T(8,128)S(1)}, u32[]{:S(2)}) copy-start(f32[16,768]{1,0:T(8,128)S(1)} %fusion.163) | copy-start | bytes 147460
  707.9 16.4 %copy-start.14 = (f32[1040,768]{1,0:T(8,128)S(1)}, f32[1040,768]{1,0:T(8,128)}, u32[]{:S(2)}) copy-start(f32[1040,768]{1,0:T(8,128)} %copy-done.12) | copy-start | bytes 9584644
  707.9 16.4 %copy-start.85 = (f32[1040]{0:T(1024)S(1)}, f32[1040]{0:T(1024)}, u32[]{:S(2)}) copy-start(f32[1040]{0:T(1024)} %copy-done.84) | copy-start | bytes 12484
  707.9 16.4 %copy-start.88 = (f32[768]{0:T(1024)S(1)}, f32[768]{0:T(1024)}, u32[]{:S(2)}) copy-start(f32[768]{0:T(1024)} %copy-done.87) | copy-start | bytes 9220
  707.9 16.4 %copy-start.91 = (f32[1040]{0:T(1024)S(1)}, f32[1040]{0:T(1024)}, u32[]{:S(2)}) copy-start(f32[1040]{0:T(1024)} %copy-done.90) | copy-start | bytes 12484
  761.8 58.0 %copy-start.36 = (bf16[1040,768]{0,1:T(8,128)(2,1)S(1)}, bf16[1040,768]{0,1:T(8,128)(2,1)}, u32[]{:S(2)}) copy-start(bf16[1040,768]{0,1:T(8,128)(2,1)} %copy.38) | copy-start | bytes 4792324
  922.7 11.7 copy-start.40
  922.8 11.7 copy-start.147
  948.9 224.2 %reduce-scatter.8.cloned.1.call-start = ((), (), s32[]{:S(2)}) async-start(), calls=%async_computation.11 | async-start | bytes 7299072 | tf_op jit(solution)/shard_map/reduce_scatter | solution.py:393
  950.5 12.9 copy-start.70
  974.8 322.9 %reduce-scatter.6.cloned.1.call-start = ((), (), s32[]{:S(2)}) async-start(), calls=%async_computation.10 | async-start | bytes 7299072 | tf_op jit(solution)/shard_map/reduce_scatter | solution.py:392
  1015.6 424.4 %reduce-scatter.14.cloned.1.call-start = ((), (), s32[]{:S(2)}) async-start(), calls=%async_computation.14 | async-start | bytes 9732096 | tf_op jit(solution)/shard_map/reduce_scatter | solution.py:396
  1039.4 541.7 %reduce-scatter.12.cloned.1.call-start = ((), (), s32[]{:S(2)}) async-start(), calls=%async_computation.13 | async-start | bytes 9732096 | tf_op jit(solution)/shard_map/reduce_scatter | solution.py:395
  (138 other events, 674.9 us)
Sparse Core Ops, SparseCore 0:
  10.9 62.8 all-gather.5
  76.7 58.9 all-gather.13
  138.6 52.9 all-gather.7
  194.3 62.4 all-gather.9
  259.6 62.3 all-gather.11
  949.0 97.7 reduce-scatter.9
  1054.0 119.0 reduce-scatter.7
  1179.4 118.3 reduce-scatter.5
  1305.3 134.7 reduce-scatter.13
  1446.3 134.7 reduce-scatter.11
where the time goes:
time: 1600 us; the launch traced here: 1590 us
  matrix products  737 us (46%)
  waiting for transfers between devices  629 us (39%)
  other arithmetic  83.7 us (5%)
  local copies, waits for them, and re-layouts  78.7 us (5%)
  blocking collectives  41.4 us (3%)
  between operations  18.1 us (1%)
    dot_general x4, matrix products, backward_segment(): jnp.einsum('hqk,hqd->hkd', grad_raw_low, block_queries, preferred_element...  162 us
    dot_general x4, matrix products, backward_segment(): jnp.einsum('hqk,hkd->hqd', grad_raw_low, block_keys, preferred_element_ty...  158 us
    reduce_scatter x1, waiting for transfers between devices, on_device(): lax.psum_scatter(totals['down'], ('wide', 'narrow'), scatter_dimension=0,...  142 us
    reduce_scatter x1, waiting for transfers between devices, on_device(): lax.psum_scatter(totals['up'], ('wide', 'narrow'), scatter_dimension=0, t...  141 us
    reduce_scatter x1, waiting for transfers between devices, on_device(): lax.psum_scatter(mem_total, ('wide', 'narrow'), scatter_dimension=0, tile...  125 us
    dot_general x12, matrix products, contract_rows(): lax.dot_general(left, right, (((0,), (0,)), ((), ())), preferred_element_...  87.8 us
    dot_general x13, matrix products, contract_cols(): lax.dot_general(left, right, (((1,), (1,)), ((), ())), preferred_element_...  86.5 us
    dot_general x13, matrix products, product(): return jnp.dot(left, right, preferred_element_type=jnp.float32)  80.3 us
  transfers between devices with their start and end apart: 10, of which 9 were waited for; matrix products, arithmetic and copies ran while one was open for 17% of the time, Pallas kernels for 0%

commit v1 on v0

v1 whole, which is shorter than its diff:
```python
import functools

import jax
import jax.numpy as jnp
from jax import lax
from jax.experimental import pallas as pl
from jax.experimental.pallas import tpu as pltpu
from jax.sharding import PartitionSpec as P

HD = 64
PAIR = 2 * HD
AXES = ("wide", "narrow")
eps_norm = 1e-05
score_scale = 0.125
gelu_c = 0.7978845608028654
gelu_a = 0.044715
f32 = jnp.float32
low_type = jnp.bfloat16
VMEM_BYTES = 60 * 2**20


def nn(left, right):
    return lax.dot_general(left, right, (((1,), (0,)), ((), ())), preferred_element_type=f32)


def nt(left, right):
    return lax.dot_general(left, right, (((1,), (1,)), ((), ())), preferred_element_type=f32)


def tn(left, right):
    return lax.dot_general(left, right, (((0,), (0,)), ((), ())), preferred_element_type=f32)


def low(values):
    return values.astype(low_type)


def split(values):
    high = low(values)
    return high, low(values - high.astype(f32))


def row_chunk(rows):
    for count in (208, 256, 128, 80, 64, 16):
        if rows % count == 0:
            return count
    return rows


def over_rows(rows, body):
    count = row_chunk(rows)

    @pl.loop(0, rows // count)
    def _(step):
        body(pl.ds(pl.multiple_of(step * count, count), count))


def normal_form(values):
    average = jnp.mean(values, axis=-1, keepdims=True)
    centered = values - average
    spread = jnp.mean(centered * centered, axis=-1, keepdims=True)
    inverse = lax.rsqrt(spread + eps_norm)
    return centered * inverse, inverse


def norm_back(grad, unit, inverse, gain):
    scaled = grad * gain
    mean_grad = jnp.mean(scaled, axis=-1, keepdims=True)
    mean_unit = jnp.mean(scaled * unit, axis=-1, keepdims=True)
    return inverse * (scaled - mean_grad - unit * mean_unit)


def softplus(values):
    return jnp.maximum(values, 0.0) + jnp.log1p(jnp.exp(-jnp.abs(values)))


def feature_parts(softer):
    return [softer * pltpu.roll(softer, offset, 1) for offset in (1, 2, 3)]


def feature_back(grads, softer, values):
    width = softer.shape[1]
    total = None
    for offset, grad in zip((1, 2, 3), grads):
        term = grad * pltpu.roll(softer, offset, 1) + pltpu.roll(grad * softer, width - offset, 1)
        total = term if total is None else total + term
    return total * jax.nn.sigmoid(values)


def whole(shape, memory=None):
    zeros = (0,) * len(shape)
    return pl.BlockSpec(shape, lambda *_: zeros, pipeline_mode=pl.Buffered(1))


def result(shape):
    zeros = (0,) * len(shape)
    return pl.BlockSpec(shape, lambda *_: zeros)


def params(**extra):
    return pltpu.CompilerParams(vmem_limit_bytes=VMEM_BYTES, **extra)


def shaped(shape, dtype):
    return jax.ShapeDtypeStruct(shape, dtype)


def load_first(tokens_ref, mem_ref, first_ref):
    seg_rows = tokens_ref.shape[0]
    first_ref[:seg_rows, :] = tokens_ref[...]
    first_ref[seg_rows:, :] = mem_ref[...]


def enter_kernel(tokens_ref, mem_ref, gains_ref, w_ref, normed_ref, qkv_ref, first_ref):
    @pl.when(pl.program_id(0) == 0)
    def _():
        load_first(tokens_ref, mem_ref, first_ref)

        def chunk(at):
            unit, _ = normal_form(first_ref[at, :].astype(f32))
            normed_ref[at, :] = low(unit * gains_ref[0:1, :])

        over_rows(first_ref.shape[0], chunk)

    qkv_ref[0] = low(nn(normed_ref[...], w_ref[...]))


def enter_read_kernel(
    tokens_ref,
    mem_ref,
    gains_ref,
    w_ref,
    w_query_ref,
    phi_keys_ref,
    delta_ref,
    beta_ref,
    normed_ref,
    qkv_ref,
    states_ref,
    query_ref,
    match_ref,
    first_ref,
):
    @pl.when(pl.program_id(0) == 0)
    def _():
        load_first(tokens_ref, mem_ref, first_ref)
        width = first_ref.shape[1]
        delta_twice = jnp.concatenate([delta_ref[...], delta_ref[...]], axis=0)

        def chunk(at):
            first = first_ref[at, :]
            query = nn(first, w_query_ref[...])
            query_ref[at, :] = query
            parts = feature_parts(softplus(query))
            match = None
            for index, part in enumerate(parts):
                term = nt(low(part), phi_keys_ref[:, index * width : (index + 1) * width])
                match = term if match is None else match + term
            match_ref[at, :] = match
            numerator = nn(jnp.concatenate(split(match), axis=1), delta_twice)
            below = 1.0 + jnp.sum(match * beta_ref[...], axis=1, keepdims=True)
            states = first.astype(f32) + numerator / below
            states_ref[at, :] = states
            unit, _ = normal_form(states)
            normed_ref[at, :] = low(unit * gains_ref[0:1, :])

        over_rows(first_ref.shape[0], chunk)

    qkv_ref[0] = low(nn(normed_ref[...], w_ref[...]))


def enter_segment(slot, tokens, mem_tokens, gains, w_qkv, w_mem, written):
    slots, seg_rows, width = tokens.shape
    mems = mem_tokens.shape[0]
    rows = seg_rows + mems
    parts = w_qkv.shape[1] // width
    in_specs = [
        pl.BlockSpec((None, seg_rows, width), lambda j: (slot, 0, 0), pipeline_mode=pl.Buffered(1)),
        whole((mems, width)),
        whole(gains.shape),
        pl.BlockSpec((width, width), lambda j: (0, j)),
    ]
    out_shape = [shaped((rows, width), low_type), shaped((parts, rows, width), low_type)]
    out_specs = [
        result((rows, width)),
        pl.BlockSpec((1, rows, width), lambda j: (j, 0, 0)),
    ]
    args = [tokens, mem_tokens, gains, w_qkv]
    body = enter_kernel
    macs = rows * width * width * parts
    if written is not None:
        body = enter_read_kernel
        args += [w_mem, written["phi_keys_low"], written["delta_low"], written["beta_row"]]
        in_specs += [whole((width, width))] + [whole(a.shape) for a in args[5:]]
        out_shape += [
            shaped((rows, width), f32),
            shaped((rows, width), f32),
            shaped((rows, mems), f32),
        ]
        out_specs += [result((rows, width)), result((rows, width)), result((rows, mems))]
        macs += rows * width * width
    return pl.pallas_call(
        body,
        grid=(parts,),
        in_specs=in_specs,
        out_specs=out_specs,
        out_shape=out_shape,
        scratch_shapes=[pltpu.VMEM((rows, width), low_type)],
        compiler_params=params(),
        cost_estimate=pl.CostEstimate(
            flops=2 * macs, bytes_accessed=20 * 2**20, transcendentals=0
        ),
        name="enter_read" if written is not None else "enter",
    )(*args)


def query_blocks(rows, seg_rows):
    step = 256 if seg_rows % 256 == 0 else seg_rows
    blocks = [(at, step) for at in range(0, seg_rows, step)]
    return blocks + [(seg_rows, rows - seg_rows)]


def packed_lanes(rows, seg_rows):
    places = []
    at = 0
    for _, count in query_blocks(rows, seg_rows):
        places.append(at)
        at += -(-2 * count // 128) * 128
    return places, at


def stack_heads(block):
    lanes = lax.broadcasted_iota(jnp.int32, block.shape, 1)
    zero = jnp.zeros_like(block)
    return jnp.concatenate(
        [jnp.where(lanes < HD, block, zero), jnp.where(lanes < HD, zero, block)], axis=0
    )


def merge_heads(stacked):
    count = stacked.shape[0] // 2
    lanes = lax.broadcasted_iota(jnp.int32, (count, stacked.shape[1]), 1)
    return jnp.where(lanes < HD, stacked[:count], stacked[count:])


def as_row(column):
    count = column.shape[0]
    return jnp.transpose(jnp.broadcast_to(column, (count, 128)))[0:1, :]


def attend_kernel(seg_rows, qkv_ref, attended_ref, log_ref):
    rows = qkv_ref.shape[1]
    places, _ = packed_lanes(rows, seg_rows)
    for (start, count), place in zip(query_blocks(rows, seg_rows), places):
        reach = start + count
        queries = stack_heads(qkv_ref[0, start:reach, :] * score_scale)
        raw = nt(queries, qkv_ref[1, :reach, :])
        place_of = lax.broadcasted_iota(jnp.int32, (2 * count, count), 0)
        place_of = jnp.where(place_of < count, place_of, place_of - count)
        allowed = place_of >= lax.broadcasted_iota(jnp.int32, (2 * count, count), 1)
        edge = jnp.where(allowed, raw[:, start:], -1e30)
        masked = jnp.concatenate([raw[:, :start], edge], axis=1) if start else edge
        peak = jnp.max(masked, axis=1, keepdims=True)
        grown = jnp.exp(masked - peak)
        total = jnp.sum(grown, axis=1, keepdims=True)
        probs = low(grown * (1.0 / total))
        mixed = merge_heads(nn(probs, qkv_ref[2, :reach, :]))
        attended_ref[start:reach, :] = low(mixed)
        log_row = as_row(peak + jnp.log(total))
        log_ref[0, 0:1, place : place + 2 * count] = log_row


def attend(qkv, seg_rows):
    parts, rows, width = qkv.shape
    _, lanes = packed_lanes(rows, seg_rows)
    pairs = width // PAIR
    return pl.pallas_call(
        functools.partial(attend_kernel, seg_rows),
        grid=(pairs,),
        in_specs=[pl.BlockSpec((parts, rows, PAIR), lambda h: (0, 0, h))],
        out_specs=[
            pl.BlockSpec((rows, PAIR), lambda h: (0, h)),
            pl.BlockSpec((1, 1, lanes), lambda h: (h, 0, 0)),
        ],
        out_shape=[shaped((rows, width), low_type), shaped((pairs, 1, lanes), f32)],
        compiler_params=params(),
        cost_estimate=pl.CostEstimate(
            flops=4 * rows * rows * width, bytes_accessed=7 * 2**20, transcendentals=0
        ),
        name="attend",
    )(qkv)


def attend_back_kernel(seg_rows, qkv_ref, grad_ref, attended_ref, log_ref, out_ref, keys_sum, values_sum):
    rows = qkv_ref.shape[1]
    places, _ = packed_lanes(rows, seg_rows)
    ones = jnp.ones((8, PAIR), f32)
    blocks = list(zip(query_blocks(rows, seg_rows), places))
    for order, ((start, count), place) in enumerate(reversed(blocks)):
        reach = start + count
        queries = stack_heads(qkv_ref[0, start:reach, :] * score_scale)
        grads = stack_heads(grad_ref[start:reach, :])
        mixed = attended_ref[start:reach, :].astype(f32)
        both = jnp.concatenate([mixed, mixed], axis=0) * grads.astype(f32)
        inner = lax.dot_general(
            ones,
            both,
            (((1,), (1,)), ((), ())),
            precision=lax.Precision.HIGHEST,
            preferred_element_type=f32,
        )[0:1, :]
        keys = qkv_ref[1, :reach, :]
        raw = nt(keys, queries)
        log_row = log_ref[0, 0:1, place : place + 2 * count]
        probs = jnp.exp(raw - log_row)
        place_of = lax.broadcasted_iota(jnp.int32, (count, 2 * count), 1)
        place_of = jnp.where(place_of < count, place_of, place_of - count)
        allowed = place_of >= lax.broadcasted_iota(jnp.int32, (count, 2 * count), 0)
        edge = jnp.where(allowed, probs[start:], 0.0)
        probs = jnp.concatenate([probs[:start], edge], axis=0) if start else edge
        grad_probs = nt(qkv_ref[2, :reach, :], grads)
        grad_raw = low(probs * (grad_probs - inner))
        value_part = nn(low(probs), grads)
        key_part = nn(grad_raw, queries)
        if order == 0:
            values_sum[...] = value_part
            keys_sum[...] = key_part
        else:
            values_sum[:reach, :] += value_part
            keys_sum[:reach, :] += key_part
        out_ref[0, start:reach, :] = low(merge_heads(tn(grad_raw, keys)) * score_scale)
    out_ref[1] = low(keys_sum[...])
    out_ref[2] = low(values_sum[...])


def attend_back(qkv, grad_attended, attended, logs, seg_rows):
    parts, rows, width = qkv.shape
    pairs = width // PAIR
    column = pl.BlockSpec((rows, PAIR), lambda h: (0, h))
    three = pl.BlockSpec((parts, rows, PAIR), lambda h: (0, 0, h))
    return pl.pallas_call(
        functools.partial(attend_back_kernel, seg_rows),
        grid=(pairs,),
        in_specs=[
            three,
            column,
            column,
            pl.BlockSpec((1,) + logs.shape[1:], lambda h: (h, 0, 0)),
        ],
        out_specs=three,
        out_shape=shaped((parts, rows, width), low_type),
        scratch_shapes=[pltpu.VMEM((rows, PAIR), f32), pltpu.VMEM((rows, PAIR), f32)],
        compiler_params=params(),
        cost_estimate=pl.CostEstimate(
            flops=10 * rows * rows * width, bytes_accessed=13 * 2**20, transcendentals=0
        ),
        name="attend_back",
    )(qkv, grad_attended, attended, logs)


def leave_kernel(
    reads, earlier, *refs
):
    if reads:
        (states_one_ref, *refs) = refs
    else:
        (tokens_ref, mem_ref, *refs) = refs
    (attended_ref, gains_ref, w_out_ref, w_up_ref, w_down_ref, *refs) = refs
    if earlier:
        refs = refs[1:]
    (out_ref, mem_out_ref, states_two_ref, normed_ref, upward_ref, sum_ref, *scratch) = refs
    rows, width = attended_ref.shape
    seg_rows = out_ref.shape[0]
    step = pl.program_id(0)

    @pl.when(step == 0)
    def _():
        if not reads:
            load_first(tokens_ref, mem_ref, scratch[0])

        def chunk(at):
            source = states_one_ref if reads else scratch[0]
            states = source[at, :].astype(f32) + nn(attended_ref[at, :], w_out_ref[...])
            states_two_ref[at, :] = states
            unit, _ = normal_form(states)
            normed_ref[at, :] = low(unit * gains_ref[1:2, :])
            sum_ref[at, :] = states

        over_rows(rows, chunk)

    def chunk(at):
        upward = nn(normed_ref[at, :], w_up_ref[...])
        upward_ref[at, :] = upward
        bent = jnp.tanh(upward * (gelu_c + gelu_c * gelu_a * (upward * upward)))
        active = low(upward * (0.5 + 0.5 * bent))
        sum_ref[at, :] += nn(active, w_down_ref[...])

    chunk(pl.ds(0, rows))

    @pl.when(step == pl.num_programs(0) - 1)
    def _():
        out_ref[...] = low(sum_ref[:seg_rows, :])
        mem_out_ref[...] = sum_ref[seg_rows:, :]


def leave_segment(slot, slots, seg_rows, start, attended, gains, w_out, w_up, w_down, earlier):
    rows, width = attended.shape
    hidden = w_up.shape[1]
    size = 512 if hidden % 512 == 0 else hidden
    reads = not isinstance(start, tuple)
    args = []
    in_specs = []
    scratch = [pltpu.VMEM((rows, width), f32)]
    if reads:
        args.append(start)
        in_specs.append(whole((rows, width)))
    else:
        tokens, mem_tokens = start
        args += [tokens, mem_tokens]
        in_specs += [
            pl.BlockSpec((None, seg_rows, width), lambda j: (slot, 0, 0), pipeline_mode=pl.Buffered(1)),
            whole(mem_tokens.shape),
        ]
        scratch.append(pltpu.VMEM((rows, width), low_type))
    args += [attended, gains, w_out, w_up, w_down]
    in_specs += [
        whole((rows, width)),
        whole(gains.shape),
        whole((width, width)),
        pl.BlockSpec((width, size), lambda j: (0, j)),
        pl.BlockSpec((size, width), lambda j: (j, 0)),
    ]
    aliases = {}
    if earlier is not None:
        aliases = {len(args): 0}
        args.append(earlier)
        in_specs.append(pl.BlockSpec(memory_space=pl.ANY))
    return pl.pallas_call(
        functools.partial(leave_kernel, reads, earlier is not None),
        grid=(hidden // size,),
        in_specs=in_specs,
        out_specs=[
            pl.BlockSpec((None, seg_rows, width), lambda j: (slot, 0, 0)),
            result((rows - seg_rows, width)),
            result((rows, width)),
            result((rows, width)),
            pl.BlockSpec((rows, size), lambda j: (0, j)),
        ],
        out_shape=[
            shaped((slots, seg_rows, width), low_type),
            shaped((rows - seg_rows, width), f32),
            shaped((rows, width), f32),
            shaped((rows, width), low_type),
            shaped((rows, hidden), f32),
        ],
        scratch_shapes=scratch,
        input_output_aliases=aliases,
        compiler_params=params(),
        cost_estimate=pl.CostEstimate(
            flops=2 * rows * width * (width + 2 * hidden), bytes_accessed=36 * 2**20, transcendentals=0
        ),
        name="leave",
    )(*args)


def beta_parts(mem_out, w_beta):
    column = jnp.sum(mem_out * w_beta, axis=1, keepdims=True)
    row = lax.dot_general(
        w_beta,
        mem_out,
        (((1,), (1,)), ((), ())),
        precision=lax.Precision.HIGHEST,
        preferred_element_type=f32,
    )
    return jax.nn.sigmoid(column), jax.nn.sigmoid(row)


def write_kernel(
    flag_ref,
    mem_out_ref,
    w_key_ref,
    w_value_ref,
    w_beta_ref,
    key_ref,
    value_ref,
    phi_ref,
    phi_rest_ref,
    delta_ref,
    beta_row_ref,
):
    flag = flag_ref[0]
    width = key_ref.shape[1]
    mem_out = mem_out_ref[...]
    mem_low = low(mem_out)
    key = nn(mem_low, w_key_ref[...])
    value = nn(mem_low, w_value_ref[...])
    key_ref[...] = key
    value_ref[...] = value
    for index, part in enumerate(feature_parts(softplus(key))):
        high, rest = split(part)
        phi_ref[:, index * width : (index + 1) * width] = high
        phi_rest_ref[:, index * width : (index + 1) * width] = rest
    beta, beta_row = beta_parts(mem_out, w_beta_ref[...])
    delta_ref[...] = low(low(beta * value).astype(f32) * flag)
    beta_row_ref[...] = beta_row * flag


def write_memory(flag, mem_out, w_mem, w_beta):
    mems, width = mem_out.shape
    names = ("key", "value", "phi_keys_low", "phi_keys_rest", "delta_low", "beta_row")
    out_shape = [
        shaped((mems, width), f32),
        shaped((mems, width), f32),
        shaped((mems, 3 * width), low_type),
        shaped((mems, 3 * width), low_type),
        shaped((mems, width), low_type),
        shaped((1, mems), f32),
    ]
    outs = pl.pallas_call(
        write_kernel,
        grid=(1,),
        in_specs=[
            pl.BlockSpec(memory_space=pltpu.SMEM),
            whole((mems, width)),
            pl.BlockSpec((width, width), lambda j: (0, 1)),
            pl.BlockSpec((width, width), lambda j: (0, 2)),
            whole((1, width)),
        ],
        out_specs=[result(s.shape) for s in out_shape],
        out_shape=out_shape,
        compiler_params=params(),
        name="write",
    )(flag, mem_out, w_mem, w_mem, w_beta)
    return dict(zip(names, outs))


def write_back_kernel(
    flag_ref,
    mem_out_ref,
    w_key_ref,
    w_value_ref,
    w_beta_ref,
    key_ref,
    value_ref,
    grad_delta_ref,
    grad_phi_ref,
    grad_normal_ref,
    grad_rows_ref,
    grad_w_ref,
    grad_beta_ref,
):
    flag = flag_ref[0]
    width = key_ref.shape[1]
    mem_out = mem_out_ref[...]
    mem_low = low(mem_out)
    w_beta = w_beta_ref[...]
    key = key_ref[...]
    value = value_ref[...]
    beta, _ = beta_parts(mem_out, w_beta)
    softer = softplus(key)
    parts = feature_parts(softer)
    grad_delta = grad_delta_ref[...] * flag
    grad_strength = jnp.sum(grad_delta * value, axis=1, keepdims=True)
    grads = []
    for index, part in enumerate(parts):
        at = slice(index * width, (index + 1) * width)
        grad_normal = grad_normal_ref[:, at] * flag
        grad_strength += jnp.sum(part * grad_normal, axis=1, keepdims=True)
        grads.append(grad_phi_ref[:, at] * flag + beta * grad_normal)
    grad_key = low(feature_back(grads, softer, key))
    grad_value = low(beta * grad_delta)
    grad_logit = grad_strength * beta * (1.0 - beta)
    grad_rows_ref[...] = (
        grad_logit * w_beta + nt(grad_key, w_key_ref[...]) + nt(grad_value, w_value_ref[...])
    )
    grad_beta_ref[...] = jnp.sum(grad_logit * mem_out, axis=0, keepdims=True)
    grad_w_ref[:, :width] = low(tn(mem_low, grad_key))
    grad_w_ref[:, width:] = low(tn(mem_low, grad_value))


def write_back(flag, mem_out, w_mem, w_beta, written, grad_delta, grad_phi, grad_normal):
    mems, width = mem_out.shape
    args = [flag, mem_out, w_mem, w_mem, w_beta, written["key"], written["value"]]
    args += [grad_delta, grad_phi, grad_normal]
    out_shape = [
        shaped((mems, width), f32),
        shaped((width, 2 * width), low_type),
        shaped((1, width), f32),
    ]
    return pl.pallas_call(
        write_back_kernel,
        grid=(1,),
        in_specs=[
            pl.BlockSpec(memory_space=pltpu.SMEM),
            whole((mems, width)),
            pl.BlockSpec((width, width), lambda j: (0, 1)),
            pl.BlockSpec((width, width), lambda j: (0, 2)),
        ]
        + [whole(a.shape) for a in args[4:]],
        out_specs=[result(s.shape) for s in out_shape],
        out_shape=out_shape,
        compiler_params=params(),
        name="write_back",
    )(*args)


def leave_back_kernel(writes, adds, *refs):
    (out_grad_ref, *refs) = refs
    if writes:
        (grad_rows_ref, *refs) = refs
    (
        states_two_ref,
        normed_ref,
        upward_ref,
        attended_ref,
        gains_ref,
        w_out_ref,
        w_up_ref,
        w_down_ref,
        *refs,
    ) = refs
    if adds:
        (up_in_ref, down_in_ref, out_in_ref, *refs) = refs
    (
        grad_states_ref,
        grad_attended_ref,
        grad_up_ref,
        grad_down_ref,
        grad_out_ref,
        grad_gain_ref,
        grad_low_ref,
        sum_ref,
        grad_two_ref,
    ) = refs
    rows, width = normed_ref.shape
    seg_rows = out_grad_ref.shape[0]
    step = pl.program_id(0)

    @pl.when(step == 0)
    def _():
        grad_low_ref[:seg_rows, :] = out_grad_ref[...]
        grad_states_ref[:seg_rows, :] = out_grad_ref[...].astype(f32)
        if writes:
            grad_low_ref[seg_rows:, :] = low(grad_rows_ref[...])
            grad_states_ref[seg_rows:, :] = grad_rows_ref[...]
        else:
            grad_low_ref[seg_rows:, :] = jnp.zeros((rows - seg_rows, width), low_type)
            grad_states_ref[seg_rows:, :] = jnp.zeros((rows - seg_rows, width), f32)
        sum_ref[...] = jnp.zeros_like(sum_ref)

    upward = upward_ref[...]
    square = upward * upward
    bent = jnp.tanh(upward * (gelu_c + gelu_c * gelu_a * square))
    half = 0.5 + 0.5 * bent
    active = upward * half
    slope = half + (active - active * half) * (2.0 * gelu_c + 6.0 * gelu_c * gelu_a * square)
    grad_low = grad_low_ref[...]
    grad_upward = low(nt(grad_low, w_down_ref[...]) * slope)
    grad_down = tn(low(active), grad_low)
    grad_up = tn(normed_ref[...], grad_upward)
    sum_ref[...] += nt(grad_upward, w_up_ref[...])
    if adds:
        grad_down += down_in_ref[...]
        grad_up += up_in_ref[...]
    grad_down_ref[...] = grad_down.astype(grad_down_ref.dtype)
    grad_up_ref[...] = grad_up.astype(grad_up_ref.dtype)

    @pl.when(step == pl.num_programs(0) - 1)
    def _():
        gain = gains_ref[1:2, :]
        grad_gain_ref[...] = jnp.zeros_like(grad_gain_ref)

        def chunk(at):
            unit, inverse = normal_form(states_two_ref[at, :])
            grad = sum_ref[at, :]
            grad_gain_ref[...] += jnp.sum(grad * unit, axis=0, keepdims=True)
            total = grad_states_ref[at, :] + norm_back(grad, unit, inverse, gain)
            grad_states_ref[at, :] = total
            total_low = low(total)
            grad_two_ref[at, :] = total_low
            grad_attended_ref[at, :] = low(nt(total_low, w_out_ref[...]))

        over_rows(rows, chunk)
        grad_out = tn(attended_ref[...], grad_two_ref[...])
        if adds:
            grad_out += out_in_ref[...]
        grad_out_ref[...] = grad_out.astype(grad_out_ref.dtype)


def leave_back(slot, out_grad, grad_rows, kept, gains, w_out, w_up, w_down, sums, grad_type):
    _, seg_rows, width = out_grad.shape
    rows = kept["normed_two"].shape[0]
    hidden = w_up.shape[1]
    size = 512 if hidden % 512 == 0 else hidden
    up_spec = pl.BlockSpec((width, size), lambda j: (0, j))
    down_spec = pl.BlockSpec((size, width), lambda j: (j, 0))
    args = [out_grad]
    in_specs = [
        pl.BlockSpec((None, seg_rows, width), lambda j: (slot, 0, 0), pipeline_mode=pl.Buffered(1))
    ]
    if grad_rows is not None:
        args.append(grad_rows)
        in_specs.append(whole(grad_rows.shape))
    args += [kept["states_two"], kept["normed_two"], kept["upward"], kept["attended"]]
    args += [gains, w_out, w_up, w_down]
    in_specs += [
        whole((rows, width)),
        whole((rows, width)),
        pl.BlockSpec((rows, size), lambda j: (0, j)),
        whole((rows, width)),
        whole(gains.shape),
        whole((width, width)),
        up_spec,
        down_spec,
    ]
    if sums is not None:
        args += [sums["up"], sums["down"], sums["out"]]
        in_specs += [up_spec, down_spec, whole((width, width))]
    return pl.pallas_call(
        functools.partial(leave_back_kernel, grad_rows is not None, sums is not None),
        grid=(hidden // size,),
        in_specs=in_specs,
        out_specs=[
            result((rows, width)),
            result((rows, width)),
            up_spec,
            down_spec,
            result((width, width)),
            result((1, width)),
        ],
        out_shape=[
            shaped((rows, width), f32),
            shaped((rows, width), low_type),
            shaped((width, hidden), grad_type),
            shaped((hidden, width), grad_type),
            shaped((width, width), grad_type),
            shaped((1, width), f32),
        ],
        scratch_shapes=[
            pltpu.VMEM((rows, width), low_type),
            pltpu.VMEM((rows, width), f32),
            pltpu.VMEM((rows, width), low_type),
        ],
        compiler_params=params(),
        cost_estimate=pl.CostEstimate(
            flops=4 * rows * width * (width + 2 * hidden), bytes_accessed=60 * 2**20, transcendentals=0
        ),
        name="leave_back",
    )(*args)


def enter_back_kernel(reads, adds, earlier, *refs):
    (tokens_ref, mem_ref, normed_ref, grad_qkv_ref, grad_states_ref, gains_ref, w_ref, *refs) = refs
    if reads:
        (
            states_ref,
            query_ref,
            match_ref,
            w_query_ref,
            phi_keys_ref,
            phi_rest_ref,
            delta_ref,
            beta_ref,
            *refs,
        ) = refs
    if adds:
        (w_in_ref, *refs) = refs
    if earlier:
        refs = refs[1:]
    (grad_tokens_ref, grad_mem_ref, grad_w_ref, grad_gain_ref, *refs) = refs
    if reads:
        (grad_w_query_ref, grad_delta_ref, grad_phi_ref, grad_normal_ref, *refs) = refs
    (first_ref, sum_ref, *refs) = refs
    rows, width = normed_ref.shape
    seg_rows = tokens_ref.shape[0]
    step = pl.program_id(0)

    @pl.when(step == 0)
    def _():
        load_first(tokens_ref, mem_ref, first_ref)
        sum_ref[...] = jnp.zeros_like(sum_ref)

    grad_part = grad_qkv_ref[0]
    sum_ref[...] += nt(grad_part, w_ref[...])
    grad_w = tn(normed_ref[...], grad_part)
    if adds:
        grad_w += w_in_ref[...]
    grad_w_ref[...] = grad_w.astype(grad_w_ref.dtype)

    @pl.when(step == pl.num_programs(0) - 1)
    def _():
        gain = gains_ref[0:1, :]
        grad_gain_ref[...] = jnp.zeros_like(grad_gain_ref)
        if reads:
            (grad_query_ref, packed_sum_ref, delta_sum_ref) = refs
            packed_sum_ref[...] = jnp.zeros_like(packed_sum_ref)
            delta_sum_ref[...] = jnp.zeros_like(delta_sum_ref)
            mems = delta_ref.shape[0]
            beta = beta_ref[...]
            basis = jnp.concatenate([phi_keys_ref[...], phi_keys_ref[...], phi_rest_ref[...]], axis=0)

        def chunk(at):
            first = first_ref[at, :].astype(f32)
            states = states_ref[at, :] if reads else first
            unit, inverse = normal_form(states)
            grad = sum_ref[at, :]
            grad_gain_ref[...] += jnp.sum(grad * unit, axis=0, keepdims=True)
            total = grad_states_ref[at, :] + norm_back(grad, unit, inverse, gain)
            if reads:
                match = match_ref[at, :]
                below = 1.0 + jnp.sum(match * beta, axis=1, keepdims=True)
                grad_num = low(total / below)
                grad_below = -jnp.sum(total * (states - first), axis=1, keepdims=True) / below
                pulled = nt(grad_num, delta_ref[...])
                spread_below = grad_below * beta
                both_high, both_low = split(pulled + spread_below)
                weights = jnp.concatenate([both_high, both_low, low(spread_below)], axis=1)
                query = query_ref[at, :]
                softer = softplus(query)
                parts = feature_parts(softer)
                grads = []
                packed = jnp.concatenate(
                    list(split(pulled))
                    + [low(jnp.broadcast_to(part, pulled.shape)) for part in (grad_below,)]
                    + [
                        low(
                            jnp.broadcast_to(
                                grad_below - low(grad_below).astype(f32), pulled.shape
                            )
                        )
                    ],
                    axis=1,
                )
                for index, part in enumerate(parts):
                    cols = slice(index * width, (index + 1) * width)
                    grads.append(nn(weights, basis[:, cols]))
                    packed_sum_ref[:, cols] += tn(packed, low(part))
                delta_sum_ref[...] += tn(jnp.concatenate(split(match), axis=1), grad_num)
                grad_query = low(feature_back(grads, softer, query))
                grad_query_ref[at, :] = grad_query
                total += nt(grad_query, w_query_ref[...])
            sum_ref[at, :] = total

        over_rows(rows, chunk)
        grad_tokens_ref[...] = sum_ref[:seg_rows, :]
        grad_mem_ref[...] = sum_ref[seg_rows:, :]
        if reads:
            grad_w_query_ref[...] = low(tn(first_ref[...], grad_query_ref[...]))
            grad_delta_ref[...] = delta_sum_ref[:mems, :] + delta_sum_ref[mems:, :]
            grad_phi_ref[...] = packed_sum_ref[:mems, :] + packed_sum_ref[mems : 2 * mems, :]
            grad_normal_ref[...] = (
                packed_sum_ref[2 * mems : 2 * mems + 1, :]
                + packed_sum_ref[3 * mems : 3 * mems + 1, :]
            )


def enter_back(
    slot, tokens, mem_tokens, kept, grad_qkv, grad_states, gains, w_qkv, w_mem, written, w_sum, earlier, grad_type
):
    slots, seg_rows, width = tokens.shape
    mems = mem_tokens.shape[0]
    rows = seg_rows + mems
    parts = grad_qkv.shape[0]
    reads = written is not None
    args = [tokens, mem_tokens, kept["normed_one"], grad_qkv, grad_states, gains, w_qkv]
    in_specs = [
        pl.BlockSpec((None, seg_rows, width), lambda j: (slot, 0, 0), pipeline_mode=pl.Buffered(1)),
        whole((mems, width)),
        whole((rows, width)),
        pl.BlockSpec((1, rows, width), lambda j: (j, 0, 0)),
        whole((rows, width)),
        whole(gains.shape),
        pl.BlockSpec((width, width), lambda j: (0, j)),
    ]
    scratch = [pltpu.VMEM((rows, width), low_type), pltpu.VMEM((rows, width), f32)]
    if reads:
        more = [written["phi_keys_low"], written["phi_keys_rest"]]
        more += [written["delta_low"], written["beta_row"]]
        args += [kept["states_one"], kept["query"], kept["match"], w_mem] + more
        in_specs += [whole((rows, width)), whole((rows, width)), whole((rows, mems)), whole((width, width))]
        in_specs += [whole(a.shape) for a in more]
        scratch += [
            pltpu.VMEM((rows, width), low_type),
            pltpu.VMEM((4 * mems, 3 * width), f32),
            pltpu.VMEM((2 * mems, width), f32),
        ]
    if w_sum is not None:
        args.append(w_sum)
        in_specs.append(pl.BlockSpec((width, width), lambda j: (0, j)))
    aliases = {}
    if earlier is not None:
        aliases = {len(args): 0}
        args.append(earlier)
        in_specs.append(pl.BlockSpec(memory_space=pl.ANY))
    out_specs = [
        pl.BlockSpec((None, seg_rows, width), lambda j: (slot, 0, 0)),
        result((mems, width)),
        pl.BlockSpec((width, width), lambda j: (0, j)),
        result((1, width)),
    ]
    out_shape = [
        shaped((slots, seg_rows, width), f32),
        shaped((mems, width), f32),
        shaped((width, parts * width), grad_type),
        shaped((1, width), f32),
    ]
    if reads:
        extra = [
            shaped((width, width), low_type),
            shaped((mems, width), f32),
            shaped((mems, 3 * width), f32),
            shaped((1, 3 * width), f32),
        ]
        out_shape += extra
        out_specs += [result(s.shape) for s in extra]
    return pl.pallas_call(
        functools.partial(enter_back_kernel, reads, w_sum is not None, earlier is not None),
        grid=(parts,),
        in_specs=in_specs,
        out_specs=out_specs,
        out_shape=out_shape,
        scratch_shapes=scratch,
        input_output_aliases=aliases,
        compiler_params=params(),
        cost_estimate=pl.CostEstimate(
            flops=4 * rows * width * width * (parts + 1), bytes_accessed=30 * 2**20, transcendentals=0
        ),
        name="enter_back",
    )(*args)


def gather_weights(shards):
    return [lax.all_gather(shard, AXES, axis=0, tiled=True) for shard in shards]


def scatter_sums(totals):
    return [
        lax.psum_scatter(total.astype(f32), AXES, scatter_dimension=0, tiled=True)
        for total in totals
    ]


def on_device(
    tokens, item_ids, w_mem, w_qkv, w_out, w_up, w_down, mem_tokens, gains, w_beta, out_grad
):
    slots, seg_rows, width = tokens.shape
    gains = gains.astype(f32)
    w_beta = w_beta.astype(f32).reshape(1, width)
    w_qkv, w_out, w_up, w_down, w_mem = gather_weights([w_qkv, w_out, w_up, w_down, w_mem])
    same_item = jnp.where(item_ids[1:] == item_ids[:-1], 1.0, 0.0).astype(f32)
    kept_all = []
    written = [None] * (slots + 1)
    out = None
    for slot in range(slots):
        kept = {}
        entered = enter_segment(slot, tokens, mem_tokens, gains, w_qkv, w_mem, written[slot])
        kept["normed_one"], kept["qkv"] = entered[:2]
        start = (tokens, mem_tokens)
        if written[slot] is not None:
            kept["states_one"], kept["query"], kept["match"] = entered[2:]
            start = kept["states_one"]
        kept["attended"], kept["logs"] = attend(kept["qkv"], seg_rows)
        out, mem_out, kept["states_two"], kept["normed_two"], kept["upward"] = leave_segment(
            slot, slots, seg_rows, start, kept["attended"], gains, w_out, w_up, w_down, out
        )
        kept["mem_out"] = mem_out
        if slot + 1 < slots:
            written[slot + 1] = write_memory(same_item[slot : slot + 1], mem_out, w_mem, w_beta)
        kept_all.append(kept)

    sums = None
    qkv_sum = None
    grad_tokens = None
    grad_mem_tokens = 0.0
    grad_gains = 0.0
    grad_beta = 0.0
    pulled = None
    for slot in reversed(range(slots)):
        kept = kept_all[slot]
        grad_type = f32 if slot else low_type
        grad_rows = None
        if slot + 1 < slots:
            grad_rows, w_pair_sum, grad_beta_part = write_back(
                same_item[slot : slot + 1], kept["mem_out"], w_mem, w_beta, written[slot + 1], *pulled
            )
            grad_beta += grad_beta_part
        grad_states, grad_attended, up_sum, down_sum, out_sum, gain_two = leave_back(
            slot, out_grad, grad_rows, kept, gains, w_out, w_up, w_down, sums, grad_type
        )
        sums = {"up": up_sum, "down": down_sum, "out": out_sum}
        grad_qkv = attend_back(kept["qkv"], grad_attended, kept["attended"], kept["logs"], seg_rows)
        grad_tokens, grad_mem, qkv_sum, gain_one, *extra = enter_back(
            slot,
            tokens,
            mem_tokens,
            kept,
            grad_qkv,
            grad_states,
            gains,
            w_qkv,
            w_mem,
            written[slot],
            qkv_sum,
            grad_tokens,
            grad_type,
        )
        if written[slot] is not None:
            w_query_sum, *pulled = extra
        grad_mem_tokens += grad_mem
        grad_gains += jnp.concatenate([gain_one, gain_two], axis=0)
    mem_sum = jnp.concatenate([w_query_sum, w_pair_sum], axis=1)
    summed = scatter_sums([mem_sum, qkv_sum, sums["out"], sums["up"], sums["down"]])
    small = lax.psum((grad_mem_tokens, grad_gains, grad_beta.reshape(width)), AXES)
    return (out, grad_tokens, *summed, *small)


def solution(mesh):
    split_rows = P(AXES, None)
    split_items = P(AXES, None, None)
    in_specs = (
        split_items,
        P(AXES),
        split_rows,
        split_rows,
        split_rows,
        split_rows,
        split_rows,
        P(),
        P(),
        P(),
        split_items,
    )
    out_specs = (
        split_items,
        split_items,
        split_rows,
        split_rows,
        split_rows,
        split_rows,
        split_rows,
        P(),
        P(),
        P(),
    )
    return jax.shard_map(
        on_device, mesh=mesh, in_specs=in_specs, out_specs=out_specs, check_vma=False
    )
```

time: 1600 us -> 1200 us (0.75)
  matrix products: 737 us -> 0 us
  Pallas kernels: 0 us -> 332 us
  waiting for transfers between devices: 629 us -> 771 us
  local copies, waits for them, and re-layouts: 78.7 us -> 3.36 us
  other arithmetic: 83.7 us -> 27.2 us
    dot_general x69 -> x0, matrix products: 737 us -> none  [the longest x4 162 us: backward_segment(): jnp.einsum('hqk,hqd->hkd', grad_raw_low, block_queries, preferred_element...]
    pallas_call x0 -> x14, Pallas kernels: none -> 332 us  [the longest x2 88.4 us: leave_back(): pl.pallas_call(functools.partial(leave_back_kernel, grad_rows is not None...]
    reduce_scatter x5, waiting for transfers between devices: 436 us -> 514 us  [scatter_sums(): lax.psum_scatter(total.astype(f32), AXES, scatter_dimension=0, tiled=True)]
    all_gather x5, waiting for transfers between devices: 189 us -> 254 us  [gather_weights(): return [lax.all_gather(shard, AXES, axis=0, tiled=True) for shard in shards]]
    reduce_sum x14 -> x0, other arithmetic: 41.9 us -> none  [the longest x4 31 us: forward_segment(): jnp.sum(jnp.exp(masked - peak), axis=-1, keepdims=True)]
    unnamed x353 -> x18, local copies, waits for them, and re-layouts: 28.9 us -> 0.79 us
    slice x19 -> x1, local copies, waits for them, and re-layouts: 28.1 us -> 1.31 us  [on_device(): same_item = jnp.where(item_ids[1:] == item_ids[:-1], 1.0, 0.0).astype(f32)]
  transfers between devices with their start and end apart: 10 -> 10, of which waited for: 9 -> 9; matrix products, arithmetic and copies ran while one was open for 17% -> 2% of each run, Pallas kernels for 0% -> 9%
where the time goes in v1:
time: 1200 us; the launch traced here: 1190 us
  waiting for transfers between devices  771 us (64%)
  Pallas kernels  332 us (28%)
  blocking collectives  39.8 us (3%)
  other arithmetic  27.2 us (2%)
  between operations  16.1 us (1%)
    reduce_scatter x5, waiting for transfers between devices, scatter_sums(): lax.psum_scatter(total.astype(f32), AXES, scatter_dimension=0, tiled=True)  514 us
    all_gather x5, waiting for transfers between devices, gather_weights(): return [lax.all_gather(shard, AXES, axis=0, tiled=True) for shard in shards]  254 us
    pallas_call x2, Pallas kernels, leave_back(): pl.pallas_call(functools.partial(leave_back_kernel, grad_rows is not None...  88.4 us
    pallas_call x2, Pallas kernels, attend_back(): pl.pallas_call(functools.partial(attend_back_kernel, seg_rows), grid=(pai...  67.2 us
    pallas_call x2, Pallas kernels, enter_back(): pl.pallas_call(functools.partial(enter_back_kernel, reads, w_sum is not N...  53.5 us
    pallas_call x2, Pallas kernels, leave_segment(): pl.pallas_call(functools.partial(leave_kernel, reads, earlier is not None...  44.9 us
    pallas_call x2, Pallas kernels, attend(): pl.pallas_call(functools.partial(attend_kernel, seg_rows), grid=(pairs,),...  43.2 us
    psum x1, blocking collectives, on_device(): lax.psum((grad_mem_tokens, grad_gains, grad_beta.reshape(width)), AXES)  39.8 us
  transfers between devices with their start and end apart: 10, of which 9 were waited for; matrix products, arithmetic and copies ran while one was open for 2% of the time, Pallas kernels for 9%

profile of v1, /device:TPU:0, one launch (start us, length us, event | category | flops | bytes accessed | tf_op | source)
XLA Modules:
  0.0 1190.0 jit_solution(14952097805374634006)
XLA Ops:
  7.2 0.0 all-gather.6.cloned.1.call-start
  7.2 0.7 all-gather.6.cloned.1.call-update
  7.9 0.0 all-gather.10.cloned.1.call-start
  8.0 0.7 all-gather.10.cloned.1.call-update
  8.7 0.0 all-gather.12.cloned.1.call-start
  8.7 0.7 all-gather.12.cloned.1.call-update
  9.4 0.0 all-gather.14.cloned.1.call-start
  9.4 0.5 all-gather.14.cloned.1.call-update
  10.0 0.0 all-gather.8.cloned.1.call-start
  10.0 0.5 all-gather.8.cloned.1.call-update
  10.6 0.0 reduce-scatter.10.cloned.1.call-start
  10.6 1.3 reshape.32.w_beta_ref
  11.9 1.3 convert_element_type.19.gains_ref.refs_3_.refs_2_.refs_5_.refs_6_
  13.1 1.3 fusion
  15.8 58.0 %all-gather.6.cloned.1.call-done.w_ref.refs_6_ = bf16[768,2304]{1,0:T(8,128)(2,1)} async-done(((bf16[24,2304]{1,0:T(8,128)(2,1)}), bf16[768,2304]{1,0:T(8,128)(2,1)}) %all-gather.6.cloned.1.call-update) | async-done | bytes 3538960 | tf_op jit(solution)/shard_map/all_gather | solution.py:933
  73.8 9.0 enter.1
  82.8 21.4 %attend.2 = (bf16[1040,768]{1,0:T(8,128)(2,1)}, f32[6,1,2176]{2,1,0:T(1,128)}) custom-call(bf16[3,1040,768]{2,1,0:T(8,128)(2,1)} %get-tuple-element.63.qkv_ref), custom_call_target="tpu_custom_call" | custom-call | flops 3322675200 | bytes 7340032 | tf_op jit(solution)/shard_map/attend/pallas_call | solution.py:277
  104.2 25.4 %all-gather.10.cloned.1.call-done.refs_4_.refs_3_.refs_6_.refs_7_ = bf16[768,768]{1,0:T(8,128)(2,1)} async-done(((bf16[24,768]{1,0:T(8,128)(2,1)}), bf16[768,768]{1,0:T(8,128)(2,1)}) %all-gather.10.cloned.1.call-update) | async-done | bytes 1179664 | tf_op jit(solution)/shard_map/all_gather | solution.py:933
  129.6 65.5 %all-gather.12.cloned.1.call-done.refs_5_.refs_4_.refs_7_.refs_8_ = bf16[768,3072]{1,0:T(8,128)(2,1)} async-done(((bf16[24,3072]{1,0:T(8,128)(2,1)}), bf16[768,3072]{1,0:T(8,128)(2,1)}) %all-gather.12.cloned.1.call-update) | async-done | bytes 4718608 | tf_op jit(solution)/shard_map/all_gather | solution.py:933
  195.1 65.2 %all-gather.14.cloned.1.call-done.refs_6_.refs_5_.refs_8_.refs_9_ = bf16[3072,768]{1,0:T(8,128)(2,1)} async-done(((bf16[96,768]{1,0:T(8,128)(2,1)}), bf16[3072,768]{1,0:T(8,128)(2,1)}) %all-gather.14.cloned.1.call-update) | async-done | bytes 4718608 | tf_op jit(solution)/shard_map/all_gather | solution.py:933
  260.3 22.2 %leave.2 = (bf16[2,1024,768]{2,1,0:T(8,128)(2,1)}, f32[16,768]{1,0:T(8,128)}, f32[1040,768]{1,0:T(8,128)}, bf16[1040,768]{1,0:T(8,128)(2,1)}, f32[1040,3072]{1,0:T(8,128)}) custom-call(bf16[2,1024,768]{2,1,0:T(8,128)(2,1)} %refs_0_.9, bf16[16,768]{1,0:T(8,128)(2,1)} %refs_1_.5, bf16[1040,768]{1,0:T(8,128)(2,1)} %get-tuple-element.64.refs_2_.refs_5_.attended_ref, ...), custom_call_target="tpu_custom_call" | custom-call | flops 11041505280 | bytes 37748736 | tf_op jit(solution)/shard_map/leave/pallas_call | solution.py:438
  282.5 39.5 %all-gather.8.cloned.1.call-done.w_key_ref.w_value_ref.w_query_ref.refs_10_ = bf16[768,2304]{1,0:T(8,128)(2,1)} async-done(((bf16[24,2304]{1,0:T(8,128)(2,1)}), bf16[768,2304]{1,0:T(8,128)(2,1)}) %all-gather.8.cloned.1.call-update) | async-done | bytes 3538960 | tf_op jit(solution)/shard_map/all_gather | solution.py:933
  322.0 2.8 write.1
  324.8 18.6 %enter_read.1 = (bf16[1040,768]{1,0:T(8,128)(2,1)}, bf16[3,1040,768]{2,1,0:T(8,128)(2,1)}, f32[1040,768]{1,0:T(8,128)}, f32[1040,768]{1,0:T(8,128)}, f32[1040,16]{1,0:T(8,128)}) custom-call(bf16[2,1024,768]{2,1,0:T(8,128)(2,1)} %refs_0_.9, bf16[16,768]{1,0:T(8,128)(2,1)} %refs_1_.5, f32[2,768]{1,0:T(2,128)} %convert_element_type.19.gains_ref.refs_3_.refs_2_.refs_5_.refs_6_, ...), custom_call_target="tpu_custom_call" | custom-call | flops 4907335680 | bytes 20971520 | tf_op jit(solution)/shard_map/enter_read/pallas_call | solution.py:202
  343.4 21.9 %attend.3 = (bf16[1040,768]{1,0:T(8,128)(2,1)}, f32[6,1,2176]{2,1,0:T(1,128)}) custom-call(bf16[3,1040,768]{2,1,0:T(8,128)(2,1)} %get-tuple-element.70.qkv_ref), custom_call_target="tpu_custom_call" | custom-call | flops 3322675200 | bytes 7340032 | tf_op jit(solution)/shard_map/attend/pallas_call | solution.py:277
  365.3 22.6 %leave.3 = (bf16[2,1024,768]{2,1,0:T(8,128)(2,1)}, f32[16,768]{1,0:T(8,128)}, f32[1040,768]{1,0:T(8,128)}, bf16[1040,768]{1,0:T(8,128)(2,1)}, f32[1040,3072]{1,0:T(8,128)}) custom-call(f32[1040,768]{1,0:T(8,128)} %get-tuple-element.69.refs_0_.refs_7_, ...), custom_call_target="tpu_custom_call", output_to_operand_aliasing={{0}: (6, {})} | custom-call | flops 11041505280 | bytes 37748736 | tf_op jit(solution)/shard_map/leave/pallas_call | solution.py:438
  387.9 42.8 %leave_back.2 = (f32[1040,768]{1,0:T(8,128)}, bf16[1040,768]{1,0:T(8,128)(2,1)}, f32[768,3072]{1,0:T(8,128)}, f32[3072,768]{1,0:T(8,128)}, f32[768,768]{1,0:T(8,128)}, /*index=5*/f32[1,768]{1,0:T(1,128)}) custom-call(bf16[2,1024,768]{2,1,0:T(8,128)(2,1)} %refs_0_.8, f32[1040,768]{1,0:T(8,128)} %get-tuple-element.78.refs_1_, ...), custom_call_target="tpu_custom_call" | custom-call | flops 22083010560 | bytes 62914560 | tf_op jit(solution)/shard_map/leave_back/pallas_call | solution.py:719
  430.7 33.6 %attend_back.2.refs_3_ = bf16[3,1040,768]{2,1,0:T(8,128)(2,1)} custom-call(bf16[3,1040,768]{2,1,0:T(8,128)(2,1)} %get-tuple-element.70.qkv_ref, bf16[1040,768]{1,0:T(8,128)(2,1)} %get-tuple-element.81.grad_ref, bf16[1040,768]{1,0:T(8,128)(2,1)} %get-tuple-element.71.refs_1_.refs_4_.attended_ref, f32[6,1,2176]{2,1,0:T(1,128)} %get-tuple-element.82.log_ref), custom_call_target="tpu_custom_call" | custom-call | flops 8306688000 | bytes 13631488 | tf_op jit(solution)/shard_map/attend_back/pallas_call | solution.py:341
  464.2 33.9 %enter_back.2 = (f32[2,1024,768]{2,1,0:T(8,128)}, f32[16,768]{1,0:T(8,128)}, f32[768,2304]{1,0:T(8,128)}, f32[1,768]{1,0:T(1,128)}, bf16[768,768]{1,0:T(8,128)(2...) custom-call(bf16[2,1024,768]{2,1,0:T(8,128)(2,1)} %refs_0_.9, bf16[16,768]{1,0:T(8,128)(2,1)} %refs_1_.5, ...), custom_call_target="tpu_custom_call" | custom-call | flops 9814671360 | bytes 31457280 | tf_op jit(solution)/shard_map/enter_back/pallas_call | solution.py:916
  498.2 4.6 write_back.1
  502.8 45.6 %leave_back.3 = (f32[1040,768]{1,0:T(8,128)}, bf16[1040,768]{1,0:T(8,128)(2,1)}, bf16[768,3072]{1,0:T(8,128)(2,1)}, bf16[3072,768]{1,0:T(8,128)(2,1)}, bf16[768,768]{1,0:T(8,128)(2,1)}, /*index=5*/f32[1,768]{1,0:T(1,128)}) custom-call(bf16[2,1024,768]{2,1,0:T(8,128)(2,1)} %refs_0_.8, f32[16,768]{1,0:T(8,128)} %get-tuple-element.90.refs_1_, ...), custom_call_target="tpu_custom_call" | custom-call | flops 22083010560 | bytes 62914560 | tf_op jit(solution)/shard_map/leave_back/pallas_call | solution.py:719
  548.4 3.0 convert_element_type.22
  551.4 0.0 reduce-scatter.6.cloned.1.call-start
  551.5 3.4 maximum_convert_fusion
  554.9 0.0 reduce-scatter.8.cloned.1.call-start
  555.0 33.7 %attend_back.3.refs_3_ = bf16[3,1040,768]{2,1,0:T(8,128)(2,1)} custom-call(bf16[3,1040,768]{2,1,0:T(8,128)(2,1)} %get-tuple-element.63.qkv_ref, bf16[1040,768]{1,0:T(8,128)(2,1)} %get-tuple-element.97.grad_ref, bf16[1040,768]{1,0:T(8,128)(2,1)} %get-tuple-element.64.refs_2_.refs_5_.attended_ref, f32[6,1,2176]{2,1,0:T(1,128)} %get-tuple-element.98.log_ref), custom_call_target="tpu_custom_call" | custom-call | flops 8306688000 | bytes 13631488 | tf_op jit(solution)/shard_map/attend_back/pallas_call | solution.py:341
  588.6 19.6 %enter_back.3 = (f32[2,1024,768]{2,1,0:T(8,128)}, f32[16,768]{1,0:T(8,128)}, bf16[768,2304]{1,0:T(8,128)(2,1)}, f32[1,768]{1,0:T(1,128)}) custom-call(bf16[2,1024,768]{2,1,0:T(8,128)(2,1)} %refs_0_.9, bf16[16,768]{1,0:T(8,128)(2,1)} %refs_1_.5, bf16[1040,768]{1,0:T(8,128)(2,1)} %get-tuple-element.74.refs_2_, ...), custom_call_target="tpu_custom_call", output_to_operand_aliasing={{0}: (8, {})} | custom-call | flops 9814671360 | bytes 31457280 | tf_op jit(solution)/shard_map/enter_back/pallas_call | solution.py:916
  608.2 5.5 convert_element_type.21
  613.7 0.0 reduce-scatter.12.cloned.1.call-start
  613.7 7.3 convert_element_type.23
  621.0 0.0 reduce-scatter.14.cloned.1.call-start
  621.1 6.7 convert_element_type.24
  627.9 0.7 copy-done.2
  628.7 39.8 %all-reduce = (f32[16,768]{1,0:T(8,128)}, f32[2,768]{1,0:T(2,128)}, f32[768]{0:T(1024)}) all-reduce(f32[16,768]{1,0:T(8,128)S(1)} %add.22, f32[2,768]{1,0:T(2,128)S(1)} %maximum_add_fusion, f32[768]{0:T(1024)S(1)} %reduce), channel_id=1, replica_groups=mesh['wide'=8,'narrow'=4] {'wide','narrow'}, use_global_device_ids=true, to_apply=%region_5.6 | all-reduce | flops 14592 | bytes 116736 | tf_op jit(solution)/shard_map/psum | solution.py:1013
  668.5 106.3 %reduce-scatter.6.cloned.1.call-done = f32[24,2304]{1,0:T(8,128)} async-done(((f32[768,2304]{1,0:T(8,128)}), f32[24,2304]{1,0:T(8,128)}) %reduce-scatter.6.cloned.1.call-update) | async-done | bytes 221200 | tf_op jit(solution)/shard_map/reduce_scatter | solution.py:938
  774.8 124.7 %reduce-scatter.8.cloned.1.call-done = f32[24,2304]{1,0:T(8,128)} async-done(((f32[768,2304]{1,0:T(8,128)}), f32[24,2304]{1,0:T(8,128)}) %reduce-scatter.8.cloned.1.call-update) | async-done | bytes 221200 | tf_op jit(solution)/shard_map/reduce_scatter | solution.py:938
  899.5 142.4 %reduce-scatter.12.cloned.1.call-done = f32[24,3072]{1,0:T(8,128)} async-done(((f32[768,3072]{1,0:T(8,128)}), f32[24,3072]{1,0:T(8,128)}) %reduce-scatter.12.cloned.1.call-update) | async-done | bytes 294928 | tf_op jit(solution)/shard_map/reduce_scatter | solution.py:938
  1041.8 140.9 %reduce-scatter.14.cloned.1.call-done = f32[96,768]{1,0:T(8,128)} async-done(((f32[3072,768]{1,0:T(8,128)}), f32[96,768]{1,0:T(8,128)}) %reduce-scatter.14.cloned.1.call-update) | async-done | bytes 294928 | tf_op jit(solution)/shard_map/reduce_scatter | solution.py:938
  (26 shorter events, 0.2 us)
Async XLA Ops:
  7.2 66.6 %all-gather.6.cloned.1.call-start = ((), (), s32[]{:S(2)}) async-start(), calls=%async_computation.5 | async-start | bytes 3649536 | tf_op jit(solution)/shard_map/all_gather | solution.py:933
  7.9 121.7 %all-gather.10.cloned.1.call-start = ((), (), s32[]{:S(2)}) async-start(), calls=%async_computation.7 | async-start | bytes 1216512 | tf_op jit(solution)/shard_map/all_gather | solution.py:933
  8.7 186.4 %all-gather.12.cloned.1.call-start = ((), (), s32[]{:S(2)}) async-start(), calls=%async_computation.8 | async-start | bytes 4866048 | tf_op jit(solution)/shard_map/all_gather | solution.py:933
  9.4 250.9 %all-gather.14.cloned.1.call-start = ((), (), s32[]{:S(2)}) async-start(), calls=%async_computation.9 | async-start | bytes 4866048 | tf_op jit(solution)/shard_map/all_gather | solution.py:933
  10.0 312.1 %all-gather.8.cloned.1.call-start = ((), (), s32[]{:S(2)}) async-start(), calls=%async_computation.6 | async-start | bytes 3649536 | tf_op jit(solution)/shard_map/all_gather | solution.py:933
  10.6 658.0 %reduce-scatter.10.cloned.1.call-start = ((), (), s32[]{:S(2)}) async-start(), calls=%async_computation.12 | async-start | bytes 2433024 | tf_op jit(solution)/shard_map/reduce_scatter | solution.py:938
  548.4 3.1 copy-start
  548.4 3.1 copy-start.1
  551.4 223.3 %reduce-scatter.6.cloned.1.call-start = ((), (), s32[]{:S(2)}) async-start(), calls=%async_computation.10 | async-start | bytes 7299072 | tf_op jit(solution)/shard_map/reduce_scatter | solution.py:938
  554.9 344.5 %reduce-scatter.8.cloned.1.call-start = ((), (), s32[]{:S(2)}) async-start(), calls=%async_computation.11 | async-start | bytes 7299072 | tf_op jit(solution)/shard_map/reduce_scatter | solution.py:938
  613.7 428.1 %reduce-scatter.12.cloned.1.call-start = ((), (), s32[]{:S(2)}) async-start(), calls=%async_computation.13 | async-start | bytes 9732096 | tf_op jit(solution)/shard_map/reduce_scatter | solution.py:938
  621.0 561.7 %reduce-scatter.14.cloned.1.call-start = ((), (), s32[]{:S(2)}) async-start(), calls=%async_computation.14 | async-start | bytes 9732096 | tf_op jit(solution)/shard_map/reduce_scatter | solution.py:938
  627.8 0.8 copy-start.2
  627.8 0.8 copy-start.3
  627.8 0.8 copy-start.8
  627.8 0.9 copy-start.4
  627.8 0.9 copy-start.5
  627.8 0.9 copy-start.6
  627.8 0.9 copy-start.7
Sparse Core Ops, SparseCore 0:
  10.9 62.8 all-gather.5
  76.7 52.8 all-gather.9
  132.5 62.5 all-gather.11
  197.9 62.3 all-gather.13
  263.0 58.9 all-gather.7
  551.6 97.8 reduce-scatter.9
  656.6 118.1 reduce-scatter.5
  781.0 118.3 reduce-scatter.7
  907.0 134.8 reduce-scatter.11
  1048.1 134.5 reduce-scatter.13

commit v2 on v1

--- a/solution.py
+++ b/solution.py
@@ -929,6 +929,348 @@
     )(*args)
 
 
+MESH = pl.DeviceIdType.MESH
+DEPTH, SIDE = 4, 2
+GRID = (DEPTH, SIDE, SIDE, SIDE)
+
+
+def my_place():
+    wide = lax.axis_index("wide")
+    narrow = lax.axis_index("narrow")
+    return wide // SIDE, wide % SIDE, narrow // SIDE, narrow % SIDE
+
+
+def device_at(z, x, y, core):
+    return (z * SIDE + x, y * SIDE + core)
+
+
+def partners(z, x, y, core):
+    along = [device_at((z + step) % DEPTH, x, y, core) for step in range(1, DEPTH)]
+    return along, device_at(z, 1 - x, y, core), device_at(z, x, 1 - y, core), device_at(z, x, y, 1 - core)
+
+
+def meet(peers):
+    barrier = pltpu.get_barrier_semaphore()
+    for peer in peers:
+        pl.semaphore_signal(barrier, inc=1, device_id=peer, device_id_type=MESH)
+    pl.semaphore_wait(barrier, len(peers))
+
+
+ORDERS = ("zxy", "zyx", "xyz", "yxz")
+
+
+def remote(source, target, send, recv, peer):
+    return pltpu.make_async_remote_copy(
+        src_ref=source, dst_ref=target, send_sem=send, recv_sem=recv, device_id=peer, device_id_type=MESH
+    )
+
+
+def slab(ref, place, known, at):
+    z, x, y, core = place
+    return ref.at[
+        slice(None) if "z" in known else z,
+        slice(None) if "x" in known else x,
+        slice(None) if "y" in known else y,
+        slice(None) if "c" in known else core,
+        :,
+        at,
+    ]
+
+
+def gather_kernel(groups, lead, count, *refs):
+    shards = refs[:count]
+    fulls = refs[count : 2 * count]
+    own_sem, send_sem, recv_sem = refs[2 * count :]
+    place = my_place()
+    along, x_peer, y_peer, core_peer = partners(*place)
+    meet(along + [x_peer, y_peer, core_peer])
+    peers = {"z": along, "x": [x_peer], "y": [y_peer], "c": [core_peer]}
+    piece_of = {}
+    for group, (a, pieces) in enumerate(groups):
+        for piece in pieces:
+            piece_of[group, piece] = len(piece_of)
+
+    def begin(index, group):
+        a, pieces = groups[group]
+        copies = []
+        for piece in pieces:
+            order, start, size = piece
+            number = piece_of[group, piece]
+            path = order + "c"
+            at = pl.ds(start, size)
+            target = slab(fulls[a], place, path[:index], at)
+            source = shards[a].at[:, at] if index == 0 else target
+            if index == 0:
+                copies.append(pltpu.make_async_copy(source, target, own_sem.at[number]))
+            for step, peer in enumerate(peers[path[index]]):
+                slot = index + step if path[index] == "z" else index + (2 if "z" in path[:index] else 0)
+                copies.append(remote(source, target, send_sem.at[number, slot], recv_sem.at[number, slot], peer))
+        for copy in copies:
+            copy.start()
+        return copies
+
+    flying = {}
+    total = len(groups)
+    for group in range(min(lead, total)):
+        flying[0, group] = begin(0, group)
+    for tick in range(total + 3):
+        for index in (3, 2, 1, 0):
+            group = tick - index
+            if not 0 <= group < total:
+                continue
+            for copy in flying.pop((index, group)):
+                copy.wait()
+            if index < 3:
+                flying[index + 1, group] = begin(index + 1, group)
+            if index == 0 and group + lead < total:
+                flying[0, group + lead] = begin(0, group + lead)
+
+
+def gather_fast(shards, groups, lead):
+    count = len(shards)
+    shapes = [s.shape for s in shards]
+    number = sum(len(pieces) for _, pieces in groups)
+    outs = pl.pallas_call(
+        functools.partial(gather_kernel, groups, lead, count),
+        in_specs=[pl.BlockSpec(memory_space=pl.ANY)] * count,
+        out_specs=[pl.BlockSpec(memory_space=pl.ANY)] * count,
+        out_shape=[shaped(GRID + s, low_type) for s in shapes],
+        scratch_shapes=[
+            pltpu.SemaphoreType.DMA((number,)),
+            pltpu.SemaphoreType.DMA((number, 6)),
+            pltpu.SemaphoreType.DMA((number, 6)),
+        ],
+        compiler_params=pltpu.CompilerParams(collective_id=0, has_side_effects=True),
+        name="gather",
+    )(*shards)
+    return [o.reshape(DEPTH * SIDE**3 * s[0], s[1]) for o, s in zip(outs, shapes)]
+
+
+def cut(cols, shares):
+    unit = cols // 128 // sum(shares)
+    pieces = []
+    at = 0
+    for order, share in zip(ORDERS, shares):
+        if share:
+            pieces.append((order, at, share * unit * 128))
+            at += share * unit * 128
+    return pieces
+
+
+def reduce_kernel(groups, lead, count, outs, *refs):
+    partials = refs[:count]
+    small_ref = refs[count]
+    totals = refs[count + 1 : count + 1 + outs]
+    small_out_ref = refs[count + 1 + outs]
+    scratch = list(refs[count + 2 + outs :])
+    small_recv_ref, small_sum_ref, small_z_ref, small_send, small_recv = scratch[:5]
+    own_sem, core_send, core_recv, send_sem, recv_sem = scratch[5:10]
+    scratch = scratch[10:]
+    place = my_place()
+    z, x, y, core = place
+    along, x_peer, y_peer, core_peer = partners(*place)
+    peers = {"x": x_peer, "y": y_peer, "c": core_peer}
+    index_of = {"x": x, "y": y}
+    buffers = []
+    number = 0
+    for a, _, _, pieces in groups:
+        own, core_in, *scratch = scratch
+        entries = []
+        for order, start, size in pieces:
+            kept, out1, in1, out2, in2, out3, in3, *scratch = scratch
+            entries.append((number, order, start, size, kept, (out1, out2, out3), (in1, in2, in3)))
+            number += 1
+        buffers.append((own, core_in, entries))
+    meet(along + [x_peer, y_peer, core_peer])
+
+    def begin_core(group):
+        a = groups[group][0]
+        own, core_in, _ = buffers[group]
+        copies = [
+            remote(partials[a].at[:, :, :, 1 - core], core_in, core_send.at[group], core_recv.at[group], core_peer),
+            pltpu.make_async_copy(partials[a].at[:, :, :, core], own, own_sem.at[group]),
+        ]
+        for copy in copies:
+            copy.start()
+        return copies
+
+    def pair_stage(entry, index, axis):
+        item, _, _, _, _, outgoing, incoming = entry
+        return remote(outgoing[index], incoming[index], send_sem.at[item, index], recv_sem.at[item, index], peers[axis])
+
+    def after_core(group):
+        own, core_in, entries = buffers[group]
+        copies = []
+        for entry in entries:
+            _, order, start, size, kept, outgoing, _ = entry
+            axis, other = order[2], order[1]
+            at = pl.ds(start, size)
+            mine = index_of[axis]
+            for far in range(DEPTH):
+                for side in range(SIDE):
+                    def pick(ref, where):
+                        spot = (far, side, where) if axis == "y" else (far, where, side)
+                        return ref[spot + (slice(None), at)].astype(f32)
+
+                    kept[far, side] = pick(own, mine) + pick(core_in, mine)
+                    outgoing[0][far, side] = (pick(own, 1 - mine) + pick(core_in, 1 - mine)).astype(low_type)
+            copies.append(pair_stage(entry, 0, axis))
+        for copy in copies:
+            copy.start()
+        return copies
+
+    def after_first(group):
+        copies = []
+        for entry in buffers[group][2]:
+            _, order, _, _, kept, outgoing, incoming = entry
+            axis = order[1]
+            mine = index_of[axis]
+            for far in range(DEPTH):
+                kept[far, mine] = kept[far, mine] + incoming[0][far, mine].astype(f32)
+                outgoing[1][far] = (
+                    kept[far, 1 - mine] + incoming[0][far, 1 - mine].astype(f32)
+                ).astype(low_type)
+            copies.append(pair_stage(entry, 1, axis))
+        for copy in copies:
+            copy.start()
+        return copies
+
+    def after_second(group):
+        copies = []
+        for entry in buffers[group][2]:
+            item, order, _, _, kept, outgoing, incoming = entry
+            mine = index_of[order[1]]
+            kept[z, mine] = kept[z, mine] + incoming[1][z].astype(f32)
+            for step in range(1, DEPTH):
+                target = (z + step) % DEPTH
+                outgoing[2][step - 1] = (
+                    kept[target, mine] + incoming[1][target].astype(f32)
+                ).astype(low_type)
+                copies.append(
+                    remote(
+                        outgoing[2].at[step - 1],
+                        incoming[2].at[step - 1],
+                        send_sem.at[item, 1 + step],
+                        recv_sem.at[item, 1 + step],
+                        along[step - 1],
+                    )
+                )
+        for copy in copies:
+            copy.start()
+        return copies
+
+    def after_third(group):
+        _, out, offset, _ = groups[group]
+        for entry in buffers[group][2]:
+            _, order, start, size, kept, _, incoming = entry
+            mine = index_of[order[1]]
+            total = kept[z, mine]
+            for step in range(DEPTH - 1):
+                total = total + incoming[2][step].astype(f32)
+            totals[out][:, pl.ds(offset + start, size)] = total
+
+    steps = [after_core, after_first, after_second, after_third]
+    flying = {}
+    total = len(groups)
+    for group in range(min(lead, total)):
+        flying[0, group] = begin_core(group)
+
+    def small_pair(index, axis, source):
+        copy = remote(source, small_recv_ref.at[index], small_send.at[index], small_recv.at[index], peers[axis])
+        copy.start()
+        return copy
+
+    def small_stage(tick):
+        if tick == 0:
+            flying["small"] = [small_pair(0, "c", small_ref)]
+            return
+        for copy in flying.pop("small", []):
+            copy.wait()
+        if tick == 1:
+            small_sum_ref[0] = small_ref[...] + small_recv_ref[0]
+            flying["small"] = [small_pair(1, "y", small_sum_ref.at[0])]
+        elif tick == 2:
+            small_sum_ref[1] = small_sum_ref[0] + small_recv_ref[1]
+            flying["small"] = [small_pair(2, "x", small_sum_ref.at[1])]
+        elif tick == 3:
+            small_sum_ref[2] = small_sum_ref[1] + small_recv_ref[2]
+            small_z_ref[z] = small_sum_ref[2]
+            flying["small"] = []
+            for step in range(1, DEPTH):
+                copy = remote(
+                    small_sum_ref.at[2],
+                    small_z_ref.at[z],
+                    small_send.at[2 + step],
+                    small_recv.at[2 + step],
+                    along[step - 1],
+                )
+                copy.start()
+                flying["small"].append(copy)
+        elif tick == 4:
+            value = small_z_ref[0]
+            for far in range(1, DEPTH):
+                value = value + small_z_ref[far]
+            small_out_ref[...] = value
+
+    for tick in range(total + 3):
+        small_stage(tick)
+        for index in (3, 2, 1, 0):
+            group = tick - index
+            if not 0 <= group < total:
+                continue
+            for copy in flying.pop((index, group)):
+                copy.wait()
+            flying[index + 1, group] = steps[index](group)
+            if index == 0 and group + lead < total:
+                flying[0, group + lead] = begin_core(group + lead)
+
+
+def reduce_fast(partials, small, groups, lead, widths):
+    devices = DEPTH * SIDE**3
+    views = [p.reshape(GRID + (p.shape[0] // devices, p.shape[1])) for p in partials]
+    rows = [v.shape[-2] for v in views]
+    scratch = []
+    number = 0
+    for a, _, _, pieces in groups:
+        height = rows[a]
+        cols = views[a].shape[-1]
+        full = (DEPTH, SIDE, SIDE, height, cols)
+        scratch += [pltpu.VMEM(full, low_type), pltpu.VMEM(full, low_type)]
+        for _, _, size in pieces:
+            number += 1
+            scratch.append(pltpu.VMEM((DEPTH, SIDE, height, size), f32))
+            for lead_dims in ((DEPTH, SIDE), (DEPTH,), (DEPTH - 1,)):
+                scratch += [pltpu.VMEM(lead_dims + (height, size), low_type)] * 2
+    total = len(groups)
+    sems = pltpu.SemaphoreType.DMA
+    out_rows = {out: rows[a] for a, out, _, _ in groups}
+    results = pl.pallas_call(
+        functools.partial(reduce_kernel, groups, lead, len(views), len(widths)),
+        in_specs=[pl.BlockSpec(memory_space=pl.ANY)] * len(views) + [pl.BlockSpec(memory_space=pltpu.VMEM)],
+        out_specs=[pl.BlockSpec(memory_space=pltpu.VMEM)] * (len(widths) + 1),
+        out_shape=[shaped((out_rows[i], w), f32) for i, w in enumerate(widths)]
+        + [shaped(small.shape, f32)],
+        scratch_shapes=[
+            pltpu.VMEM((3,) + small.shape, f32),
+            pltpu.VMEM((3,) + small.shape, f32),
+            pltpu.VMEM((DEPTH,) + small.shape, f32),
+            sems((6,)),
+            sems((6,)),
+            sems((total,)),
+            sems((total,)),
+            sems((total,)),
+            sems((number, 5)),
+            sems((number, 5)),
+        ]
+        + scratch,
+        compiler_params=pltpu.CompilerParams(
+            collective_id=1, has_side_effects=True, vmem_limit_bytes=60 * 2**20
+        ),
+        name="reduce",
+    )(*views, small)
+    return results[:-1], results[-1]
+
+
 def gather_weights(shards):
     return [lax.all_gather(shard, AXES, axis=0, tiled=True) for shard in shards]
 
@@ -940,13 +1282,33 @@
     ]
 
 
+def fast_gather_weights(shards):
+    shares = {2304: (8, 8, 1, 1), 768: (3, 3, 0, 0), 3072: (10, 10, 2, 2)}
+    groups = []
+    for a, shard in enumerate(shards):
+        cols = shard.shape[1]
+        tall = shard.shape[0] * 32 > cols
+        groups.append((a, cut(cols, (2, 2, 1, 1) if tall else shares.get(cols, (1, 1)))))
+    return gather_fast(shards, groups, 1)
+
+
+def fast_scatter_sums(query_sum, pair_sum, qkv_sum, out_sum, up_sum, down_sum, small):
+    partials = [query_sum, pair_sum, qkv_sum, out_sum, up_sum, down_sum]
+    cols = [p.shape[1] for p in partials]
+    places = [(0, 0), (0, cols[0]), (1, 0), (2, 0), (3, 0), (4, 0)]
+    order = (5, 4, 0, 1, 3, 2)
+    groups = [(a,) + places[a] + (cut(cols[a], (1, 1)),) for a in order]
+    return reduce_fast(partials, small, groups, 2, [cols[0] + cols[1]] + cols[2:])
+
+
 def on_device(
-    tokens, item_ids, w_mem, w_qkv, w_out, w_up, w_down, mem_tokens, gains, w_beta, out_grad
+    fast, tokens, item_ids, w_mem, w_qkv, w_out, w_up, w_down, mem_tokens, gains, w_beta, out_grad
 ):
     slots, seg_rows, width = tokens.shape
     gains = gains.astype(f32)
     w_beta = w_beta.astype(f32).reshape(1, width)
-    w_qkv, w_out, w_up, w_down, w_mem = gather_weights([w_qkv, w_out, w_up, w_down, w_mem])
+    gather = fast_gather_weights if fast else gather_weights
+    w_qkv, w_out, w_up, w_down, w_mem = gather([w_qkv, w_out, w_up, w_down, w_mem])
     same_item = jnp.where(item_ids[1:] == item_ids[:-1], 1.0, 0.0).astype(f32)
     kept_all = []
     written = [None] * (slots + 1)
@@ -1008,6 +1370,15 @@
             w_query_sum, *pulled = extra
         grad_mem_tokens += grad_mem
         grad_gains += jnp.concatenate([gain_one, gain_two], axis=0)
+    if fast:
+        mems = mem_tokens.shape[0]
+        small = jnp.concatenate([grad_mem_tokens, grad_gains, grad_beta], axis=0)
+        small = jnp.pad(small, ((0, -small.shape[0] % 8), (0, 0)))
+        summed, small = fast_scatter_sums(
+            w_query_sum, w_pair_sum, qkv_sum, sums["out"], sums["up"], sums["down"], small
+        )
+        small = (small[:mems], small[mems : mems + 2], small[mems + 2])
+        return (out, grad_tokens, *summed, *small)
     mem_sum = jnp.concatenate([w_query_sum, w_pair_sum], axis=1)
     summed = scatter_sums([mem_sum, qkv_sum, sums["out"], sums["up"], sums["down"]])
     small = lax.psum((grad_mem_tokens, grad_gains, grad_beta.reshape(width)), AXES)
@@ -1042,6 +1413,7 @@
         P(),
         P(),
     )
+    fast = mesh.shape["wide"] == DEPTH * SIDE and mesh.shape["narrow"] == SIDE * SIDE
     return jax.shard_map(
-        on_device, mesh=mesh, in_specs=in_specs, out_specs=out_specs, check_vma=False
+        functools.partial(on_device, fast), mesh=mesh, in_specs=in_specs, out_specs=out_specs, check_vma=False
     )

time: 1200 us -> 557 us (0.46)
  waiting for transfers between devices: 771 us -> 0 us
  Pallas kernels: 332 us -> 527 us
  blocking collectives: 39.8 us -> 0 us
  other arithmetic: 27.2 us -> 3.44 us
  between operations: 16.1 us -> 2.28 us
    reduce_scatter x5 -> x0, waiting for transfers between devices: 514 us -> none  [scatter_sums(): lax.psum_scatter(total.astype(f32), AXES, scatter_dimension=0, tiled=True)]
    all_gather x5 -> x0, waiting for transfers between devices: 254 us -> none  [gather_weights(): return [lax.all_gather(shard, AXES, axis=0, tiled=True) for shard in shards]]
    pallas_call x0 -> x2, Pallas kernels: none -> 195 us  [the longest x1 101 us: reduce_fast(): pl.pallas_call(functools.partial(reduce_kernel, groups, lead, len(views),...]
    psum x1 -> x0, blocking collectives: 39.8 us -> none  [on_device(): lax.psum((grad_mem_tokens, grad_gains, grad_beta.reshape(width)), AXES)]
    convert_element_type x5 -> x0, other arithmetic: 25.8 us -> none  [scatter_sums(): total.astype(f32)]
  transfers between devices with their start and end apart: 10 -> 0, of which waited for: 9 -> 0; matrix products, arithmetic and copies ran while one was open for 2% -> 0% of each run, Pallas kernels for 9% -> 0%
where the time goes in v2:
time: 557 us; the launch traced here: 547 us
  Pallas kernels  527 us (95%)
  local copies, waits for them, and re-layouts  14.9 us (3%)
    pallas_call x1, Pallas kernels, reduce_fast(): pl.pallas_call(functools.partial(reduce_kernel, groups, lead, len(views),...  101 us
    pallas_call x1, Pallas kernels, gather_fast(): pl.pallas_call(functools.partial(gather_kernel, groups, lead, count), in_...  94.4 us
    pallas_call x2, Pallas kernels, leave_back(): pl.pallas_call(functools.partial(leave_back_kernel, grad_rows is not None...  88.2 us
    pallas_call x2, Pallas kernels, attend_back(): pl.pallas_call(functools.partial(attend_back_kernel, seg_rows), grid=(pai...  67.2 us
    pallas_call x2, Pallas kernels, enter_back(): pl.pallas_call(functools.partial(enter_back_kernel, reads, w_sum is not N...  53.4 us
    pallas_call x2, Pallas kernels, leave_segment(): pl.pallas_call(functools.partial(leave_kernel, reads, earlier is not None...  44.9 us
    pallas_call x2, Pallas kernels, attend(): pl.pallas_call(functools.partial(attend_kernel, seg_rows), grid=(pairs,),...  42.9 us
    pallas_call x2, Pallas kernels, enter_segment(): pl.pallas_call(body, grid=(parts,), in_specs=in_specs, out_specs=out_spec...  27.7 us

profile of v2, /device:TPU:0, one launch (start us, length us, event | category | flops | bytes accessed | tf_op | source)
XLA Modules:
  0.0 547.2 jit_solution(13270480248117369613)
XLA Ops:
  0.6 1.3 fusion
  3.3 1.3 reshape.72.w_beta_ref
  4.5 1.3 convert_element_type.6.gains_ref.refs_3_.refs_2_.refs_5_.refs_6_
  5.8 94.4 %gather.1 = (bf16[4,2,2,2,24,2304]{5,4,3,2,1,0:T(8,128)(2,1)}, bf16[4,2,2,2,24,768]{5,4,3,2,1,0:T(8,128)(2,1)}, bf16[4,2,2,2,24,3072]{5,4,3,2,1,0:T(8,128)(2,1)}...) custom-call(bf16[24,2304]{1,0:T(8,128)(2,1)} %refs_0_.6, bf16[24,768]{1,0:T(8,128)(2,1)} %refs_1_.4, ...), custom_call_target="tpu_custom_call" | custom-call | tf_op jit(solution)/shard_map/gather/pallas_call | solution.py:1033
  100.2 9.1 %enter.1 = (bf16[1040,768]{1,0:T(8,128)(2,1)}, bf16[3,1040,768]{2,1,0:T(8,128)(2,1)}) custom-call(bf16[2,1024,768]{2,1,0:T(8,128)(2,1)} %refs_0_.11, bf16[16,768]{1,0:T(8,128)(2,1)} %refs_1_.7, f32[2,768]{1,0:T(2,128)} %convert_element_type.6.gains_ref.refs_3_.refs_2_.refs_5_.refs_6_, bf16[768,2304]{1,0:T(8,128)(2,1)} %bitcast.31), custom_call_target="tpu_custom_call" | custom-call | flops 3680501760 | bytes 20971520 | tf_op jit(solution)/shard_map/enter/pallas_call | solution.py:202
  109.3 21.4 %attend.2 = (bf16[1040,768]{1,0:T(8,128)(2,1)}, f32[6,1,2176]{2,1,0:T(1,128)}) custom-call(bf16[3,1040,768]{2,1,0:T(8,128)(2,1)} %get-tuple-element.76.qkv_ref), custom_call_target="tpu_custom_call" | custom-call | flops 3322675200 | bytes 7340032 | tf_op jit(solution)/shard_map/attend/pallas_call | solution.py:277
  130.6 22.2 %leave.2 = (bf16[2,1024,768]{2,1,0:T(8,128)(2,1)}, f32[16,768]{1,0:T(8,128)}, f32[1040,768]{1,0:T(8,128)}, bf16[1040,768]{1,0:T(8,128)(2,1)}, f32[1040,3072]{1,0:T(8,128)}) custom-call(bf16[2,1024,768]{2,1,0:T(8,128)(2,1)} %refs_0_.11, bf16[16,768]{1,0:T(8,128)(2,1)} %refs_1_.7, bf16[1040,768]{1,0:T(8,128)(2,1)} %get-tuple-element.77.refs_2_.refs_5_.attended_ref, ...), custom_call_target="tpu_custom_call" | custom-call | flops 11041505280 | bytes 37748736 | tf_op jit(solution)/shard_map/leave/pallas_call | solution.py:438
  152.9 2.8 write.1
  155.7 18.6 %enter_read.1 = (bf16[1040,768]{1,0:T(8,128)(2,1)}, bf16[3,1040,768]{2,1,0:T(8,128)(2,1)}, f32[1040,768]{1,0:T(8,128)}, f32[1040,768]{1,0:T(8,128)}, f32[1040,16]{1,0:T(8,128)}) custom-call(bf16[2,1024,768]{2,1,0:T(8,128)(2,1)} %refs_0_.11, bf16[16,768]{1,0:T(8,128)(2,1)} %refs_1_.7, f32[2,768]{1,0:T(2,128)} %convert_element_type.6.gains_ref.refs_3_.refs_2_.refs_5_.refs_6_, ...), custom_call_target="tpu_custom_call" | custom-call | flops 4907335680 | bytes 20971520 | tf_op jit(solution)/shard_map/enter_read/pallas_call | solution.py:202
  174.3 21.6 %attend.3 = (bf16[1040,768]{1,0:T(8,128)(2,1)}, f32[6,1,2176]{2,1,0:T(1,128)}) custom-call(bf16[3,1040,768]{2,1,0:T(8,128)(2,1)} %get-tuple-element.86.qkv_ref), custom_call_target="tpu_custom_call" | custom-call | flops 3322675200 | bytes 7340032 | tf_op jit(solution)/shard_map/attend/pallas_call | solution.py:277
  195.9 22.6 %leave.3 = (bf16[2,1024,768]{2,1,0:T(8,128)(2,1)}, f32[16,768]{1,0:T(8,128)}, f32[1040,768]{1,0:T(8,128)}, bf16[1040,768]{1,0:T(8,128)(2,1)}, f32[1040,3072]{1,0:T(8,128)}) custom-call(f32[1040,768]{1,0:T(8,128)} %get-tuple-element.85.refs_0_.refs_7_, ...), custom_call_target="tpu_custom_call", output_to_operand_aliasing={{0}: (6, {})} | custom-call | flops 11041505280 | bytes 37748736 | tf_op jit(solution)/shard_map/leave/pallas_call | solution.py:438
  218.5 42.9 %leave_back.2 = (f32[1040,768]{1,0:T(8,128)}, bf16[1040,768]{1,0:T(8,128)(2,1)}, f32[768,3072]{1,0:T(8,128)}, f32[3072,768]{1,0:T(8,128)}, f32[768,768]{1,0:T(8,128)}, /*index=5*/f32[1,768]{1,0:T(1,128)}) custom-call(bf16[2,1024,768]{2,1,0:T(8,128)(2,1)} %refs_0_.10, f32[1040,768]{1,0:T(8,128)} %get-tuple-element.94.refs_1_, ...), custom_call_target="tpu_custom_call" | custom-call | flops 22083010560 | bytes 62914560 | tf_op jit(solution)/shard_map/leave_back/pallas_call | solution.py:719
  261.5 33.6 %attend_back.2.refs_3_ = bf16[3,1040,768]{2,1,0:T(8,128)(2,1)} custom-call(bf16[3,1040,768]{2,1,0:T(8,128)(2,1)} %get-tuple-element.86.qkv_ref, bf16[1040,768]{1,0:T(8,128)(2,1)} %get-tuple-element.97.grad_ref, bf16[1040,768]{1,0:T(8,128)(2,1)} %get-tuple-element.87.refs_1_.refs_4_.attended_ref, f32[6,1,2176]{2,1,0:T(1,128)} %get-tuple-element.98.log_ref), custom_call_target="tpu_custom_call" | custom-call | flops 8306688000 | bytes 13631488 | tf_op jit(solution)/shard_map/attend_back/pallas_call | solution.py:341
  295.1 34.2 %enter_back.2 = (f32[2,1024,768]{2,1,0:T(8,128)}, f32[16,768]{1,0:T(8,128)}, f32[768,2304]{1,0:T(8,128)}, f32[1,768]{1,0:T(1,128)}, bf16[768,768]{1,0:T(8,128)(2...) custom-call(bf16[2,1024,768]{2,1,0:T(8,128)(2,1)} %refs_0_.11, bf16[16,768]{1,0:T(8,128)(2,1)} %refs_1_.7, ...), custom_call_target="tpu_custom_call" | custom-call | flops 9814671360 | bytes 31457280 | tf_op jit(solution)/shard_map/enter_back/pallas_call | solution.py:916
  329.2 4.6 write_back.1
  333.9 45.3 %leave_back.3 = (f32[1040,768]{1,0:T(8,128)}, bf16[1040,768]{1,0:T(8,128)(2,1)}, bf16[768,3072]{1,0:T(8,128)(2,1)}, bf16[3072,768]{1,0:T(8,128)(2,1)}, bf16[768,768]{1,0:T(8,128)(2,1)}, /*index=5*/f32[1,768]{1,0:T(1,128)}) custom-call(bf16[2,1024,768]{2,1,0:T(8,128)(2,1)} %refs_0_.10, f32[16,768]{1,0:T(8,128)} %get-tuple-element.106.refs_1_, ...), custom_call_target="tpu_custom_call" | custom-call | flops 22083010560 | bytes 62914560 | tf_op jit(solution)/shard_map/leave_back/pallas_call | solution.py:719
  379.2 33.5 %attend_back.3.refs_3_ = bf16[3,1040,768]{2,1,0:T(8,128)(2,1)} custom-call(bf16[3,1040,768]{2,1,0:T(8,128)(2,1)} %get-tuple-element.76.qkv_ref, bf16[1040,768]{1,0:T(8,128)(2,1)} %get-tuple-element.113.grad_ref, bf16[1040,768]{1,0:T(8,128)(2,1)} %get-tuple-element.77.refs_2_.refs_5_.attended_ref, f32[6,1,2176]{2,1,0:T(1,128)} %get-tuple-element.114.log_ref), custom_call_target="tpu_custom_call" | custom-call | flops 8306688000 | bytes 13631488 | tf_op jit(solution)/shard_map/attend_back/pallas_call | solution.py:341
  412.7 0.0 copy-start.1
  412.7 0.0 copy-start.2
  412.7 0.0 copy-start.3
  412.7 0.0 copy-start
  412.7 0.0 copy-start.4
  412.7 19.2 %enter_back.3 = (f32[2,1024,768]{2,1,0:T(8,128)}, f32[16,768]{1,0:T(8,128)}, bf16[768,2304]{1,0:T(8,128)(2,1)}, f32[1,768]{1,0:T(1,128)}) custom-call(bf16[2,1024,768]{2,1,0:T(8,128)(2,1)} %refs_0_.11, bf16[16,768]{1,0:T(8,128)(2,1)} %refs_1_.7, bf16[1040,768]{1,0:T(8,128)(2,1)} %get-tuple-element.90.refs_2_, ...), custom_call_target="tpu_custom_call", output_to_operand_aliasing={{0}: (8, {})} | custom-call | flops 9814671360 | bytes 31457280 | tf_op jit(solution)/shard_map/enter_back/pallas_call | solution.py:916
  432.0 0.0 copy-done.1
  432.0 0.0 copy-done.2
  432.0 0.0 copy-done.3
  432.0 0.7 maximum_add_fusion
  432.7 0.0 copy-done
  432.7 0.8 add.8
  433.5 0.0 copy-done.4
  433.5 0.6 select_maximum_fusion.refs_6_
  434.2 100.5 %reduce.3 = (f32[24,2304]{1,0:T(8,128)}, f32[24,2304]{1,0:T(8,128)}, f32[24,768]{1,0:T(8,128)}, f32[24,3072]{1,0:T(8,128)}, f32[96,768]{1,0:T(8,128)}, /*index=5*/f32[24,768]{1,0:T(8,128)}) custom-call(bf16[4,2,2,2,24,768]{5,4,3,2,1,0:T(8,128)(2,1)} %bitcast.21, bf16[4,2,2,2,24,1536]{5,4,3,2,1,0:T(8,128)(2,1)} %bitcast.20, ...), custom_call_target="tpu_custom_call" | custom-call | tf_op jit(solution)/shard_map/reduce/pallas_call | solution.py:1247
  534.7 1.3 slice_reduce_fusion
  536.0 1.3 slice.18
  537.3 1.4 slice.17
  538.8 1.6 copy.30
  540.4 1.6 copy.31
  542.0 1.5 copy.32
  543.6 1.7 copy.33
  545.2 1.7 copy.34
Async XLA Ops:
  412.7 19.2 %copy-start.1 = (f32[1,768]{1,0:T(1,128)S(1)}, f32[1,768]{1,0:T(1,128)}, u32[]{:S(2)}) copy-start(f32[1,768]{1,0:T(1,128)} %get-tuple-element.128) | copy-start | bytes 9220
  412.7 19.3 %copy-start.2 = (f32[1,768]{1,0:T(1,128)S(1)}, f32[1,768]{1,0:T(1,128)}, u32[]{:S(2)}) copy-start(f32[1,768]{1,0:T(1,128)} %get-tuple-element.127) | copy-start | bytes 9220
  412.7 19.3 %copy-start.3 = (f32[1,768]{1,0:T(1,128)S(1)}, f32[1,768]{1,0:T(1,128)}, u32[]{:S(2)}) copy-start(f32[1,768]{1,0:T(1,128)} %get-tuple-element.130) | copy-start | bytes 9220
  412.7 20.0 %copy-start = (f32[16,768]{1,0:T(8,128)S(1)}, f32[16,768]{1,0:T(8,128)}, u32[]{:S(2)}) copy-start(f32[16,768]{1,0:T(8,128)} %get-tuple-element.125) | copy-start | bytes 147460
  412.7 20.8 %copy-start.4 = (f32[1,768]{1,0:T(1,128)S(1)}, f32[1,768]{1,0:T(1,128)}, u32[]{:S(2)}) copy-start(f32[1,768]{1,0:T(1,128)} %get-tuple-element.131) | copy-start | bytes 9220

commit v3 on v1

--- a/solution.py
+++ b/solution.py
@@ -248,13 +248,13 @@
     return jnp.transpose(jnp.broadcast_to(column, (count, 128)))[0:1, :]
 
 
-def attend_kernel(seg_rows, qkv_ref, attended_ref, log_ref):
+def attend_kernel(seg_rows, qkv_ref, attended_ref, log_ref, lanes=slice(None)):
     rows = qkv_ref.shape[1]
     places, _ = packed_lanes(rows, seg_rows)
     for (start, count), place in zip(query_blocks(rows, seg_rows), places):
         reach = start + count
-        queries = stack_heads(qkv_ref[0, start:reach, :] * score_scale)
-        raw = nt(queries, qkv_ref[1, :reach, :])
+        queries = stack_heads(qkv_ref[0, start:reach, lanes] * score_scale)
+        raw = nt(queries, qkv_ref[1, :reach, lanes])
         place_of = lax.broadcasted_iota(jnp.int32, (2 * count, count), 0)
         place_of = jnp.where(place_of < count, place_of, place_of - count)
         allowed = place_of >= lax.broadcasted_iota(jnp.int32, (2 * count, count), 1)
@@ -264,7 +264,7 @@
         grown = jnp.exp(masked - peak)
         total = jnp.sum(grown, axis=1, keepdims=True)
         probs = low(grown * (1.0 / total))
-        mixed = merge_heads(nn(probs, qkv_ref[2, :reach, :]))
+        mixed = merge_heads(nn(probs, qkv_ref[2, :reach, lanes]))
         attended_ref[start:reach, :] = low(mixed)
         log_row = as_row(peak + jnp.log(total))
         log_ref[0, 0:1, place : place + 2 * count] = log_row
@@ -291,7 +291,17 @@
     )(qkv)
 
 
-def attend_back_kernel(seg_rows, qkv_ref, grad_ref, attended_ref, log_ref, out_ref, keys_sum, values_sum):
+def attend_back_kernel(
+    seg_rows,
+    qkv_ref,
+    grad_ref,
+    attended_ref,
+    log_ref,
+    out_ref,
+    keys_sum,
+    values_sum,
+    lanes=slice(None),
+):
     rows = qkv_ref.shape[1]
     places, _ = packed_lanes(rows, seg_rows)
     ones = jnp.ones((8, PAIR), f32)
@@ -328,9 +338,9 @@
         else:
             values_sum[:reach, :] += value_part
             keys_sum[:reach, :] += key_part
-        out_ref[0, start:reach, :] = low(merge_heads(tn(grad_raw, keys)) * score_scale)
-    out_ref[1] = low(keys_sum[...])
-    out_ref[2] = low(values_sum[...])
+        out_ref[0, start:reach, lanes] = low(merge_heads(tn(grad_raw, keys)) * score_scale)
+    out_ref[1, :, lanes] = low(keys_sum[...])
+    out_ref[2, :, lanes] = low(values_sum[...])
 
 
 def attend_back(qkv, grad_attended, attended, logs, seg_rows):
@@ -687,7 +697,7 @@
         grad_out_ref[...] = grad_out.astype(grad_out_ref.dtype)
 
 
-def leave_back(slot, out_grad, grad_rows, kept, gains, w_out, w_up, w_down, sums, grad_type):
+def leave_back(slot, out_grad, grad_rows, kept, gains, w_out, w_up, w_down, sums, grad_type, moved=None):
     _, seg_rows, width = out_grad.shape
     rows = kept["normed_two"].shape[0]
     hidden = w_up.shape[1]
@@ -716,32 +726,57 @@
     if sums is not None:
         args += [sums["up"], sums["down"], sums["out"]]
         in_specs += [up_spec, down_spec, whole((width, width))]
+    body = functools.partial(leave_back_kernel, grad_rows is not None, sums is not None)
+    out_specs = [
+        result((rows, width)),
+        result((rows, width)),
+        up_spec,
+        down_spec,
+        result((width, width)),
+        result((1, width)),
+    ]
+    out_shape = [
+        shaped((rows, width), f32),
+        shaped((rows, width), low_type),
+        shaped((width, hidden), grad_type),
+        shaped((hidden, width), grad_type),
+        shaped((width, width), grad_type),
+        shaped((1, width), f32),
+    ]
+    scratch = [
+        pltpu.VMEM((rows, width), low_type),
+        pltpu.VMEM((rows, width), f32),
+        pltpu.VMEM((rows, width), low_type),
+    ]
+    extra = {}
+    if moved is not None:
+        shapes = [m.shape[-2:] for m in moved]
+        groups = []
+        before = 0
+        for a, (_, cols) in enumerate(shapes):
+            for at in range(0, cols, width):
+                groups.append((a, at, width, 0, before + at, cut(width, (1, 1)), False))
+            before += cols
+        plan = Reduce(groups, shapes)
+        grid = hidden // size
+        schedule = {1: (0,), 2: (1,), 3: (2,), 4: (3,), 5: (4,), grid: (5,)}
+        counts = (len(args), len(moved), len(out_shape), 1, len(scratch))
+        body = functools.partial(carry_kernel, body, plan, counts, schedule, grid)
+        args += moved
+        in_specs += [ANYWHERE] * len(moved)
+        total = (width // DEVICES, before)
+        out_specs.append(result(total))
+        out_shape.append(shaped(total, f32))
+        scratch += plan.scratch()
+        extra = dict(collective_id=1, has_side_effects=True)
     return pl.pallas_call(
-        functools.partial(leave_back_kernel, grad_rows is not None, sums is not None),
+        body,
         grid=(hidden // size,),
         in_specs=in_specs,
-        out_specs=[
-            result((rows, width)),
-            result((rows, width)),
-            up_spec,
-            down_spec,
-            result((width, width)),
-            result((1, width)),
-        ],
-        out_shape=[
-            shaped((rows, width), f32),
-            shaped((rows, width), low_type),
-            shaped((width, hidden), grad_type),
-            shaped((hidden, width), grad_type),
-            shaped((width, width), grad_type),
-            shaped((1, width), f32),
-        ],
-        scratch_shapes=[
-            pltpu.VMEM((rows, width), low_type),
-            pltpu.VMEM((rows, width), f32),
-            pltpu.VMEM((rows, width), low_type),
-        ],
-        compiler_params=params(),
+        out_specs=out_specs,
+        out_shape=out_shape,
+        scratch_shapes=scratch,
+        compiler_params=params(**extra),
         cost_estimate=pl.CostEstimate(
             flops=4 * rows * width * (width + 2 * hidden), bytes_accessed=60 * 2**20, transcendentals=0
         ),
@@ -929,6 +964,393 @@
     )(*args)
 
 
+MESH = pl.DeviceIdType.MESH
+DEPTH, SIDE = 4, 2
+GRID = (DEPTH, SIDE, SIDE, SIDE)
+DEVICES = DEPTH * SIDE**3
+ORDERS = ("zxy", "zyx", "xyz", "yxz")
+sems = pltpu.SemaphoreType.DMA
+
+
+def my_place():
+    wide = lax.axis_index("wide")
+    narrow = lax.axis_index("narrow")
+    return wide // SIDE, wide % SIDE, narrow // SIDE, narrow % SIDE
+
+
+def device_at(z, x, y, core):
+    return (z * SIDE + x, y * SIDE + core)
+
+
+def partners(z, x, y, core):
+    return {
+        "z": [device_at((z + step) % DEPTH, x, y, core) for step in range(1, DEPTH)],
+        "x": [device_at(z, 1 - x, y, core)],
+        "y": [device_at(z, x, 1 - y, core)],
+        "c": [device_at(z, x, y, 1 - core)],
+    }
+
+
+def meet(peers):
+    barrier = pltpu.get_barrier_semaphore()
+    everyone = [peer for group in peers.values() for peer in group]
+    for peer in everyone:
+        pl.semaphore_signal(barrier, inc=1, device_id=peer, device_id_type=MESH)
+    pl.semaphore_wait(barrier, len(everyone))
+
+
+def remote(source, target, send, recv, peer):
+    return pltpu.make_async_remote_copy(
+        src_ref=source,
+        dst_ref=target,
+        send_sem=send,
+        recv_sem=recv,
+        device_id=peer,
+        device_id_type=MESH,
+    )
+
+
+def slab(ref, place, known, at):
+    z, x, y, core = place
+    return ref.at[
+        slice(None) if "z" in known else z,
+        slice(None) if "x" in known else x,
+        slice(None) if "y" in known else y,
+        slice(None) if "c" in known else core,
+        :,
+        at,
+    ]
+
+
+def cut(cols, shares):
+    unit = cols // 128 // sum(shares)
+    pieces = []
+    at = 0
+    for order, share in zip(ORDERS, shares):
+        if share:
+            pieces.append((order, at, share * unit * 128))
+            at += share * unit * 128
+    return pieces
+
+
+class Gather:
+    def __init__(self, groups, lead):
+        self.groups = groups
+        self.lead = lead
+        self.ticks = len(groups) + 3
+        self.numbers = {}
+        for group, (_, pieces) in enumerate(groups):
+            for piece in pieces:
+                self.numbers[group, piece] = len(self.numbers)
+
+    def scratch(self):
+        count = len(self.numbers)
+        return [sems((count,)), sems((count, 6)), sems((count, 6))]
+
+    def bind(self, shards, fulls, scratch):
+        self.shards = shards
+        self.fulls = fulls
+        self.own_sem, self.send_sem, self.recv_sem = scratch
+        self.place = my_place()
+        self.peers = partners(*self.place)
+
+    def copies(self, index, group):
+        a, pieces = self.groups[group]
+        made = []
+        for piece in pieces:
+            order, start, size = piece
+            number = self.numbers[group, piece]
+            path = order + "c"
+            at = pl.ds(start, size)
+            target = slab(self.fulls[a], self.place, path[:index], at)
+            source = self.shards[a].at[:, at] if index == 0 else target
+            if index == 0:
+                made.append(pltpu.make_async_copy(source, target, self.own_sem.at[number]))
+            for step, peer in enumerate(self.peers[path[index]]):
+                slot = index + step if path[index] == "z" else index + 2 * ("z" in path[:index])
+                made.append(
+                    remote(
+                        source,
+                        target,
+                        self.send_sem.at[number, slot],
+                        self.recv_sem.at[number, slot],
+                        peer,
+                    )
+                )
+        return made
+
+    def begin(self, index, group):
+        for copy in self.copies(index, group):
+            copy.start()
+
+    def enter(self):
+        meet(self.peers)
+        for group in range(min(self.lead, len(self.groups))):
+            self.begin(0, group)
+
+    def tick(self, now):
+        total = len(self.groups)
+        for index in (3, 2, 1, 0):
+            group = now - index
+            if not 0 <= group < total:
+                continue
+            for copy in self.copies(index, group):
+                copy.wait()
+            if index < 3:
+                self.begin(index + 1, group)
+            if index == 0 and group + self.lead < total:
+                self.begin(0, group + self.lead)
+
+
+class Reduce:
+    def __init__(self, groups, shapes, ready=None):
+        self.groups = groups
+        self.shapes = shapes
+        self.ready = ready or {}
+        self.ticks = len(groups) + 3
+        self.slots = 2
+        count = 0
+        self.entries = []
+        for *_, pieces, _ in groups:
+            self.entries.append([(count + i, piece) for i, piece in enumerate(pieces)])
+            count += len(pieces)
+        self.count = count
+
+    def scratch(self):
+        total = len(self.groups)
+        made = [sems((total,)), sems((total,)), sems((total,)), sems((self.count, 5)), sems((self.count, 5))]
+        for a, _, cols, _, _, pieces, held in self.groups:
+            height = self.shapes[a][0]
+            full = (DEPTH, SIDE, SIDE, height, cols)
+            made.append(pltpu.VMEM(full, low_type))
+            if not held:
+                made.append(pltpu.VMEM(full, low_type))
+            for _, _, size in pieces:
+                made.append(pltpu.VMEM((DEPTH, SIDE, height, size), f32))
+                made.append(pltpu.VMEM((DEPTH, SIDE, height, size), low_type))
+                made.append(pltpu.VMEM((DEPTH, height, size), low_type))
+                made.append(pltpu.VMEM((DEPTH - 1, height, size), low_type))
+        return made
+
+    def bind(self, partials, totals, scratch):
+        self.partials = partials
+        self.totals = totals
+        self.own_sem, self.core_send, self.core_recv, self.send_sem, self.recv_sem, *scratch = scratch
+        self.place = my_place()
+        self.peers = partners(*self.place)
+        z, x, y, core = self.place
+        self.mine = {"x": x, "y": y}
+        self.core_in, self.own, self.parts = [], [], {}
+        for group, (*_, held) in enumerate(self.groups):
+            core_in, *scratch = scratch
+            self.core_in.append(core_in)
+            if held:
+                self.own.append(None)
+            else:
+                own, *scratch = scratch
+                self.own.append(own)
+            for number, _ in self.entries[group]:
+                self.parts[number] = scratch[:4]
+                scratch = scratch[4:]
+
+    def enter(self):
+        meet(self.peers)
+
+    def core_copies(self, group):
+        a, first, cols, _, _, _, held = self.groups[group]
+        at = pl.ds(first, cols)
+        core = self.place[3]
+        made = [
+            remote(
+                self.partials[a].at[:, :, :, 1 - core, :, at],
+                self.core_in[group],
+                self.core_send.at[group],
+                self.core_recv.at[group],
+                self.peers["c"][0],
+            )
+        ]
+        if not held:
+            made.append(
+                pltpu.make_async_copy(
+                    self.partials[a].at[:, :, :, core, :, at], self.own[group], self.own_sem.at[group]
+                )
+            )
+        return made
+
+    def copies(self, index, group):
+        if index == 0:
+            return self.core_copies(group)
+        made = []
+        z = self.place[0]
+        for number, (order, start, size) in self.entries[group]:
+            kept, in1, in2, in3 = self.parts[number]
+            if index == 1:
+                axis = order[2]
+                far = 1 - self.mine[axis]
+                at = pl.ds(start, size)
+                core_in = self.core_in[group]
+                source = core_in.at[:, :, far, :, at] if axis == "y" else core_in.at[:, far, :, :, at]
+                pairs = [(source, in1, self.peers[axis][0], 0)]
+            elif index == 2:
+                axis = order[1]
+                pairs = [(in1.at[:, 1 - self.mine[axis]], in2, self.peers[axis][0], 1)]
+            else:
+                pairs = [
+                    (in2.at[(z + step) % DEPTH], in3.at[step - 1], self.peers["z"][step - 1], 1 + step)
+                    for step in range(1, DEPTH)
+                ]
+            for source, target, peer, slot in pairs:
+                made.append(
+                    remote(
+                        source,
+                        target,
+                        self.send_sem.at[number, slot],
+                        self.recv_sem.at[number, slot],
+                        peer,
+                    )
+                )
+        return made
+
+    def begin(self, index, group):
+        for copy in self.copies(index, group):
+            copy.start()
+
+    def add(self, index, group):
+        z, x, y, core = self.place
+        a, first, _, out, offset, _, held = self.groups[group]
+        core_in = self.core_in[group]
+        for number, (order, start, size) in self.entries[group]:
+            kept, in1, in2, in3 = self.parts[number]
+            at = pl.ds(start, size)
+            if index == 0:
+                axis = order[2]
+                mine = self.mine[axis]
+
+                def spot(step, where):
+                    far, side = step // SIDE, step % SIDE
+                    return (far, side, where) if axis == "y" else (far, where, side)
+
+                def own_at(place):
+                    if held:
+                        inside = pl.ds(first + start, size)
+                        return self.partials[a][place + (core, slice(None), inside)].astype(f32)
+                    return self.own[group][place + (slice(None), at)].astype(f32)
+
+                @pl.loop(0, DEPTH * SIDE)
+                def _(step):
+                    near = spot(step, mine)
+                    away = spot(step, 1 - mine)
+                    kept[step // SIDE, step % SIDE] = own_at(near) + core_in[near + (slice(None), at)].astype(f32)
+                    moved = own_at(away) + core_in[away + (slice(None), at)].astype(f32)
+                    core_in[away + (slice(None), at)] = low(moved)
+            elif index == 1:
+                mine = self.mine[order[1]]
+
+                @pl.loop(0, DEPTH)
+                def _(far):
+                    kept[far, mine] += in1[far, mine].astype(f32)
+                    in1[far, 1 - mine] = low(kept[far, 1 - mine] + in1[far, 1 - mine].astype(f32))
+            elif index == 2:
+                mine = self.mine[order[1]]
+                kept[z, mine] += in2[z].astype(f32)
+                for step in range(1, DEPTH):
+                    target = (z + step) % DEPTH
+                    in2[target] = low(kept[target, mine] + in2[target].astype(f32))
+            else:
+                mine = self.mine[order[1]]
+                total = kept[z, mine]
+                for step in range(DEPTH - 1):
+                    total = total + in3[step].astype(f32)
+                self.totals[out][:, pl.ds(offset + start, size)] = total
+
+    def tick(self, now):
+        total = len(self.groups)
+        for index in (3, 2, 1, 0):
+            group = now - index
+            if not 0 <= group < total:
+                continue
+            for copy in self.copies(index, group):
+                copy.wait()
+            self.add(index, group)
+            if index < 3:
+                self.begin(index + 1, group)
+
+
+class SmallSum:
+    def __init__(self, shape):
+        self.shape = shape
+        self.ticks = 4
+
+    def scratch(self):
+        return [
+            pltpu.VMEM((4,) + self.shape, f32),
+            pltpu.VMEM((3,) + self.shape, f32),
+            pltpu.VMEM((DEPTH,) + self.shape, f32),
+            sems((6,)),
+            sems((6,)),
+        ]
+
+    def bind(self, out, scratch):
+        self.out = out
+        self.sums, self.arrived, self.along, self.send_sem, self.recv_sem = scratch
+        self.place = my_place()
+        self.peers = partners(*self.place)
+
+    def copies(self, index):
+        if index < 3:
+            return [
+                remote(
+                    self.sums.at[index],
+                    self.arrived.at[index],
+                    self.send_sem.at[index],
+                    self.recv_sem.at[index],
+                    self.peers["cyx"[index]][0],
+                )
+            ]
+        return [
+            remote(
+                self.sums.at[3],
+                self.along.at[self.place[0]],
+                self.send_sem.at[3 + step],
+                self.recv_sem.at[3 + step],
+                self.peers["z"][step],
+            )
+            for step in range(DEPTH - 1)
+        ]
+
+    def enter(self, value):
+        self.sums[0] = value
+        for copy in self.copies(0):
+            copy.start()
+
+    def tick(self, index):
+        for copy in self.copies(index):
+            copy.wait()
+        if index < 3:
+            self.sums[index + 1] = self.sums[index] + self.arrived[index]
+            if index == 2:
+                self.along[self.place[0]] = self.sums[3]
+            for copy in self.copies(index + 1):
+                copy.start()
+        else:
+            total = self.along[0]
+            for far in range(1, DEPTH):
+                total = total + self.along[far]
+            self.out[...] = total
+
+
+def slabs(array):
+    rows, cols = array.shape
+    return array.reshape(GRID + (rows // DEVICES, cols))
+
+
+def flat(array):
+    return array.reshape(DEVICES * array.shape[-2], array.shape[-1])
+
+
+ANYWHERE = pl.BlockSpec(memory_space=pl.ANY)
+
+
 def gather_weights(shards):
     return [lax.all_gather(shard, AXES, axis=0, tiled=True) for shard in shards]
 
@@ -940,26 +1362,388 @@
     ]
 
 
-def on_device(
-    tokens, item_ids, w_mem, w_qkv, w_out, w_up, w_down, mem_tokens, gains, w_beta, out_grad
+def at_chunk(step, size):
+    return pl.ds(pl.multiple_of(step * size, size), size)
+
+
+def at_step(step, when):
+    return lambda body: pl.when(step == when)(body)
+
+
+def arrive_kernel(plan, seg_rows, schedule, *refs):
+    count = len(plan.groups)
+    tokens_ref, mem_ref, gains_ref, *refs = refs
+    shards, refs = refs[:count], refs[count:]
+    normed_ref, qkv_ref, attended_ref, log_ref, *refs = refs
+    fulls, refs = refs[:count], refs[count:]
+    first_ref, w_ref, w_sem, *refs = refs
+    plan.bind(shards, fulls, refs)
+    parts, rows, width = qkv_ref.shape
+    step = pl.program_id(0)
+
+    @pl.when(step == 0)
+    def _():
+        plan.enter()
+        load_first(tokens_ref, mem_ref, first_ref)
+
+        def chunk(at):
+            unit, _ = normal_form(first_ref[at, :].astype(f32))
+            normed_ref[at, :] = low(unit * gains_ref[0:1, :])
+
+        over_rows(rows, chunk)
+
+    for when, ticks in schedule.items():
+
+        @pl.when(step == when)
+        def _():
+            for now in ticks:
+                plan.tick(now)
+
+    @pl.when(step == 0)
+    def _():
+        copy = pltpu.make_async_copy(fulls[0], w_ref, w_sem)
+        copy.start()
+        copy.wait()
+
+    @pl.when(step < parts)
+    def _():
+        block = w_ref[..., at_chunk(step, width)].astype(f32).reshape(width, width)
+        qkv_ref[step] = low(nn(normed_ref[...], low(block)))
+
+    @pl.when(step >= parts)
+    def _():
+        attend_kernel(seg_rows, qkv_ref, attended_ref, log_ref, at_chunk(step - parts, PAIR))
+
+
+def arrive(tokens, mem_tokens, gains, shards, plan, schedule):
+    slots, seg_rows, width = tokens.shape
+    mems = mem_tokens.shape[0]
+    rows = seg_rows + mems
+    parts = shards[0].shape[1] // width
+    pairs = width // PAIR
+    _, lanes = packed_lanes(rows, seg_rows)
+
+    def pair(step):
+        return jnp.maximum(step - parts, 0)
+
+    outs = pl.pallas_call(
+        functools.partial(arrive_kernel, plan, seg_rows, schedule),
+        grid=(parts + pairs,),
+        in_specs=[
+            pl.BlockSpec((None, seg_rows, width), lambda j: (0, 0, 0), pipeline_mode=pl.Buffered(1)),
+            whole((mems, width)),
+            whole(gains.shape),
+        ]
+        + [ANYWHERE] * len(shards),
+        out_specs=[
+            result((rows, width)),
+            result((parts, rows, width)),
+            pl.BlockSpec((rows, PAIR), lambda j: (0, pair(j))),
+            pl.BlockSpec((1, 1, lanes), lambda j: (pair(j), 0, 0)),
+        ]
+        + [ANYWHERE] * len(shards),
+        out_shape=[
+            shaped((rows, width), low_type),
+            shaped((parts, rows, width), low_type),
+            shaped((rows, width), low_type),
+            shaped((pairs, 1, lanes), f32),
+        ]
+        + [shaped(GRID + shard.shape, low_type) for shard in shards],
+        scratch_shapes=[
+            pltpu.VMEM((rows, width), low_type),
+            pltpu.VMEM(GRID + shards[0].shape, low_type),
+            sems,
+        ]
+        + plan.scratch(),
+        compiler_params=params(collective_id=0, has_side_effects=True),
+        name="arrive",
+    )(tokens, mem_tokens, gains, *shards)
+    return outs[:4], [flat(o) for o in outs[4:]]
+
+
+def carry_kernel(body, plan, counts, schedule, grid, *refs):
+    ins, moved, outs, totals, scratch = counts
+    parts = []
+    for count in (ins, moved, outs, totals, scratch):
+        parts.append(refs[:count])
+        refs = refs[count:]
+    own_in, partials, own_out, total_refs, own_scratch = parts
+    plan.bind(partials, total_refs, refs)
+    step = pl.program_id(0)
+
+    @pl.when(step == 0)
+    def _():
+        plan.enter()
+        for group in range(len(plan.groups)):
+            plan.begin(0, group)
+
+    for when, ticks in schedule.items():
+        if when < grid:
+
+            @pl.when(step == when)
+            def _():
+                for now in ticks:
+                    plan.tick(now)
+
+    body(*own_in, *own_out, *own_scratch)
+
+    if grid in schedule:
+
+        @pl.when(step == grid - 1)
+        def _():
+            for now in schedule[grid]:
+                plan.tick(now)
+
+
+def finish_kernel(plan, small, seg_rows, schedule, counts, *refs):
+    (
+        qkv_ref,
+        grad_ref,
+        attended_ref,
+        log_ref,
+        tokens_ref,
+        mem_ref,
+        normed_ref,
+        gains_ref,
+        w_ref,
+        w_in_ref,
+        small_in_ref,
+        grad_states_ref,
+        *refs,
+    ) = refs
+    moved, totals = counts
+    partials, refs = refs[:moved], refs[moved:]
+    first_ref, *refs = refs
+    total_refs, refs = refs[:totals], refs[totals:]
+    small_out_ref, keys_sum, values_sum, grad_qkv_ref, w_grad_ref, sum_ref, states_sem, *refs = refs
+    kept = len(small.scratch())
+    small.bind(small_out_ref, refs[:kept])
+    plan.bind(list(partials) + [w_grad_ref], total_refs, refs[kept:])
+    rows, width = normed_ref.shape
+    parts = grad_qkv_ref.shape[0]
+    pairs = width // PAIR
+    step = pl.program_id(0)
+    late = [g for g, group in enumerate(plan.groups) if group[-1]]
+    early = [g for g, group in enumerate(plan.groups) if not group[-1]]
+    states_copy = pltpu.make_async_copy(grad_states_ref, first_ref, states_sem)
+
+    @pl.when(step == 0)
+    def _():
+        plan.enter()
+        for group in early:
+            plan.begin(0, group)
+        states_copy.start()
+        sum_ref[...] = jnp.zeros_like(sum_ref)
+
+    for when, ticks in schedule.items():
+
+        @pl.when(step == when)
+        def _():
+            for now in ticks:
+                plan.tick(now)
+
+    @pl.when(step < pairs)
+    def _():
+        attend_back_kernel(
+            seg_rows,
+            qkv_ref,
+            grad_ref,
+            attended_ref,
+            log_ref,
+            grad_qkv_ref,
+            keys_sum,
+            values_sum,
+            at_chunk(step, PAIR),
+        )
+
+    @pl.when((step >= pairs) & (step < pairs + parts))
+    def _():
+        part = step - pairs
+        grad_w = tn(normed_ref[...], grad_qkv_ref[part]) + w_in_ref[...]
+        w_grad_ref[..., at_chunk(part, width)] = low(grad_w.reshape(GRID + (width // DEVICES, width)))
+        for index, group in enumerate(late):
+
+            @pl.when(part == index)
+            def _():
+                plan.begin(0, group)
+
+    @pl.when(step >= pairs + parts)
+    def _():
+        sum_ref[...] += nt(grad_qkv_ref[step - pairs - parts], w_ref[...])
+
+    @pl.when(step == pairs + 2 * parts - 1)
+    def _():
+        gain = gains_ref[0:1, :]
+        states_copy.wait()
+        small_out_ref[...] = small_in_ref[...]
+        mems = rows - seg_rows
+
+        def back(first, at):
+            unit, inverse = normal_form(first)
+            grad = sum_ref[at, :]
+            small_out_ref[mems : mems + 1, :] += jnp.sum(grad * unit, axis=0, keepdims=True)
+            first_ref[at, :] += norm_back(grad, unit, inverse, gain)
+
+        def chunk(at):
+            back(tokens_ref[at, :].astype(f32), at)
+
+        over_rows(seg_rows, chunk)
+        last = pl.ds(seg_rows, mems)
+        back(mem_ref[...].astype(f32), last)
+        small_out_ref[:mems, :] += first_ref[last, :]
+        small.enter(small_out_ref[...])
+        rest = list(range(sum(len(t) for t in schedule.values()), plan.ticks))
+        for index in range(max(len(rest), small.ticks)):
+            if index < len(rest):
+                plan.tick(rest[index])
+            if index < small.ticks:
+                small.tick(index)
+
+
+def finish(
+    tokens, mem_tokens, kept, grad_attended, grad_states, gains, w_qkv, w_in, small_in, partials, plan, schedule, widths
 ):
     slots, seg_rows, width = tokens.shape
+    mems = mem_tokens.shape[0]
+    rows = seg_rows + mems
+    qkv = kept["qkv"]
+    parts = qkv.shape[0]
+    pairs = width // PAIR
+    small = SmallSum(small_in.shape)
+    logs = kept["logs"]
+
+    def pair(step):
+        return jnp.minimum(step, pairs - 1)
+
+    def part(step, start):
+        return jnp.clip(step - start, 0, parts - 1)
+
+    column = pl.BlockSpec((rows, PAIR), lambda j: (0, pair(j)))
+    outs = pl.pallas_call(
+        functools.partial(finish_kernel, plan, small, seg_rows, schedule, (len(partials), len(widths))),
+        grid=(pairs + 2 * parts,),
+        in_specs=[
+            pl.BlockSpec((parts, rows, PAIR), lambda j: (0, 0, pair(j))),
+            column,
+            column,
+            pl.BlockSpec((1,) + logs.shape[1:], lambda j: (pair(j), 0, 0)),
+            pl.BlockSpec((None, seg_rows, width), lambda j: (0, 0, 0), pipeline_mode=pl.Buffered(1)),
+            whole((mems, width)),
+            whole((rows, width)),
+            whole(gains.shape),
+            pl.BlockSpec((width, width), lambda j: (0, part(j, pairs + parts))),
+            pl.BlockSpec((width, width), lambda j: (0, part(j, pairs))),
+            whole(small_in.shape),
+            ANYWHERE,
+        ]
+        + [ANYWHERE] * len(partials),
+        out_specs=[whole((rows, width))] + [whole(s) for s in widths] + [whole(small_in.shape)],
+        out_shape=[shaped((rows, width), f32)]
+        + [shaped(s, f32) for s in widths]
+        + [shaped(small_in.shape, f32)],
+        scratch_shapes=[
+            pltpu.VMEM((rows, PAIR), f32),
+            pltpu.VMEM((rows, PAIR), f32),
+            pltpu.VMEM((parts, rows, width), low_type),
+            pltpu.VMEM(GRID + (width // DEVICES, parts * width), low_type),
+            pltpu.VMEM((rows, width), f32),
+            sems,
+        ]
+        + small.scratch()
+        + plan.scratch(),
+        compiler_params=params(collective_id=2, has_side_effects=True),
+        name="finish",
+    )(
+        qkv,
+        grad_attended,
+        kept["attended"],
+        logs,
+        tokens,
+        mem_tokens,
+        kept["normed_one"],
+        gains,
+        w_qkv,
+        w_in,
+        small_in,
+        grad_states,
+        *partials,
+    )
+    return outs[0], outs[1:-1], outs[-1]
+
+
+def settle_kernel(count, first_ref, *refs):
+    small_ref, *refs = refs
+    sums, refs = refs[:count], refs[count + 1 :]
+    tokens_ref, mem_ref, gains_ref, beta_ref, *outs = refs
+    tokens_ref[...] = first_ref[...]
+
+    @pl.when(pl.program_id(0) == 0)
+    def _():
+        mems = mem_ref.shape[0]
+        mem_ref[...] = small_ref[:mems, :]
+        gains_ref[...] = small_ref[mems : mems + 2, :]
+        beta_ref[...] = small_ref[mems + 2 : mems + 3, :]
+        for source, target in zip(sums, outs):
+            target[...] = source[...]
+
+
+def settle(first, small, sums, grad_tokens, mems):
+    slots, seg_rows, width = grad_tokens.shape
+    size = 256
+    shapes = [(mems, width), (2, width), (1, width)] + [s.shape for s in sums]
+    return pl.pallas_call(
+        functools.partial(settle_kernel, len(sums)),
+        grid=(seg_rows // size,),
+        in_specs=[pl.BlockSpec((size, width), lambda j: (j, 0)), whole(small.shape)]
+        + [whole(s.shape) for s in sums]
+        + [ANYWHERE],
+        out_specs=[pl.BlockSpec((None, size, width), lambda j: (0, j, 0))] + [result(s) for s in shapes],
+        out_shape=[shaped(grad_tokens.shape, f32)] + [shaped(s, f32) for s in shapes],
+        input_output_aliases={2 + len(sums): 0},
+        compiler_params=params(),
+        name="settle",
+    )(first, small, *sums, grad_tokens)
+
+
+def fast_gather(shards):
+    shares = {2304: (8, 8, 1, 1), 768: (3, 3, 0, 0), 3072: (10, 10, 2, 2)}
+    groups = []
+    for a, shard in enumerate(shards):
+        rows, cols = shard.shape
+        groups.append((a, cut(cols, (2, 2, 1, 1) if rows > 48 else shares.get(cols, (1, 1)))))
+    return Gather(groups, 1)
+
+
+def on_device(
+    fast, tokens, item_ids, w_mem, w_qkv, w_out, w_up, w_down, mem_tokens, gains, w_beta, out_grad
+):
+    slots, seg_rows, width = tokens.shape
+    mems = mem_tokens.shape[0]
     gains = gains.astype(f32)
     w_beta = w_beta.astype(f32).reshape(1, width)
-    w_qkv, w_out, w_up, w_down, w_mem = gather_weights([w_qkv, w_out, w_up, w_down, w_mem])
+    shards = [w_qkv, w_out, w_up, w_down, w_mem]
+    if fast:
+        schedule = {0: (0, 1, 2, 3), 4: (4,), 6: (5,), 8: (6, 7)}
+        arrived, fulls = arrive(tokens, mem_tokens, gains, shards, fast_gather(shards), schedule)
+    else:
+        fulls = gather_weights(shards)
+    w_qkv, w_out, w_up, w_down, w_mem = fulls
     same_item = jnp.where(item_ids[1:] == item_ids[:-1], 1.0, 0.0).astype(f32)
     kept_all = []
     written = [None] * (slots + 1)
     out = None
     for slot in range(slots):
         kept = {}
-        entered = enter_segment(slot, tokens, mem_tokens, gains, w_qkv, w_mem, written[slot])
-        kept["normed_one"], kept["qkv"] = entered[:2]
         start = (tokens, mem_tokens)
-        if written[slot] is not None:
-            kept["states_one"], kept["query"], kept["match"] = entered[2:]
-            start = kept["states_one"]
-        kept["attended"], kept["logs"] = attend(kept["qkv"], seg_rows)
+        if fast and slot == 0:
+            kept["normed_one"], kept["qkv"], kept["attended"], kept["logs"] = arrived
+        else:
+            entered = enter_segment(slot, tokens, mem_tokens, gains, w_qkv, w_mem, written[slot])
+            kept["normed_one"], kept["qkv"] = entered[:2]
+            if written[slot] is not None:
+                kept["states_one"], kept["query"], kept["match"] = entered[2:]
+                start = kept["states_one"]
+            kept["attended"], kept["logs"] = attend(kept["qkv"], seg_rows)
         out, mem_out, kept["states_two"], kept["normed_two"], kept["upward"] = leave_segment(
             slot, slots, seg_rows, start, kept["attended"], gains, w_out, w_up, w_down, out
         )
@@ -972,22 +1756,31 @@
     qkv_sum = None
     grad_tokens = None
     grad_mem_tokens = 0.0
-    grad_gains = 0.0
+    gain_one_sum = 0.0
+    gain_two_sum = 0.0
     grad_beta = 0.0
     pulled = None
     for slot in reversed(range(slots)):
         kept = kept_all[slot]
-        grad_type = f32 if slot else low_type
+        last = slot == 0
+        grad_type = low_type if last else f32
         grad_rows = None
+        mem_plan = None
         if slot + 1 < slots:
             grad_rows, w_pair_sum, grad_beta_part = write_back(
                 same_item[slot : slot + 1], kept["mem_out"], w_mem, w_beta, written[slot + 1], *pulled
             )
             grad_beta += grad_beta_part
-        grad_states, grad_attended, up_sum, down_sum, out_sum, gain_two = leave_back(
-            slot, out_grad, grad_rows, kept, gains, w_out, w_up, w_down, sums, grad_type
+            if fast and last:
+                mem_plan = [slabs(w_query_sum), slabs(w_pair_sum)]
+        left = leave_back(
+            slot, out_grad, grad_rows, kept, gains, w_out, w_up, w_down, sums, grad_type, mem_plan
         )
+        grad_states, grad_attended, up_sum, down_sum, out_sum, gain_two, *mem_total = left
+        gain_two_sum += gain_two
         sums = {"up": up_sum, "down": down_sum, "out": out_sum}
+        if fast and last:
+            break
         grad_qkv = attend_back(kept["qkv"], grad_attended, kept["attended"], kept["logs"], seg_rows)
         grad_tokens, grad_mem, qkv_sum, gain_one, *extra = enter_back(
             slot,
@@ -1007,8 +1800,43 @@
         if written[slot] is not None:
             w_query_sum, *pulled = extra
         grad_mem_tokens += grad_mem
-        grad_gains += jnp.concatenate([gain_one, gain_two], axis=0)
+        gain_one_sum += gain_one
+    if fast:
+        small = jnp.concatenate([grad_mem_tokens, gain_one_sum, gain_two_sum, grad_beta], axis=0)
+        small = jnp.pad(small, ((0, -small.shape[0] % 8), (0, 0)))
+        partials = [slabs(down_sum), slabs(up_sum), slabs(out_sum)]
+        shapes = [p.shape[-2:] for p in partials] + [(width // DEVICES, w_qkv.shape[1])]
+        half = shapes[1][1] // 2
+        groups = [(0, 0, width, 0, 0, cut(width, (1, 1)), False)]
+        groups += [(1, at, half, 1, at, cut(half, (1, 1)), False) for at in (0, half)]
+        groups += [(2, 0, width, 2, 0, cut(width, (1, 1)), False)]
+        groups += [
+            (3, at, width, 3, at, cut(width, (1, 1)), True) for at in range(0, shapes[3][1], width)
+        ]
+        plan = Reduce(groups, shapes)
+        schedule = {1: (0,), 4: (1,), 6: (2,), 9: (3,)}
+        first, (down_total, up_total, out_total, qkv_total), small = finish(
+            tokens,
+            mem_tokens,
+            kept,
+            grad_attended,
+            grad_states,
+            gains,
+            w_qkv,
+            qkv_sum,
+            small,
+            partials,
+            plan,
+            schedule,
+            shapes,
+        )
+        totals = [mem_total[0], qkv_total, out_total, up_total, down_total]
+        grad_tokens, grad_mem_tokens, grad_gains, grad_beta, *totals = settle(
+            first, small, totals, grad_tokens, mems
+        )
+        return (out, grad_tokens, *totals, grad_mem_tokens, grad_gains, grad_beta.reshape(width))
     mem_sum = jnp.concatenate([w_query_sum, w_pair_sum], axis=1)
+    grad_gains = jnp.concatenate([gain_one_sum, gain_two_sum], axis=0)
     summed = scatter_sums([mem_sum, qkv_sum, sums["out"], sums["up"], sums["down"]])
     small = lax.psum((grad_mem_tokens, grad_gains, grad_beta.reshape(width)), AXES)
     return (out, grad_tokens, *summed, *small)
@@ -1042,6 +1870,7 @@
         P(),
         P(),
     )
+    fast = mesh.shape["wide"] == DEPTH * SIDE and mesh.shape["narrow"] == SIDE * SIDE
     return jax.shard_map(
-        on_device, mesh=mesh, in_specs=in_specs, out_specs=out_specs, check_vma=False
+        functools.partial(on_device, fast), mesh=mesh, in_specs=in_specs, out_specs=out_specs, check_vma=False
     )

time: 1200 us -> 475 us (0.40)
  waiting for transfers between devices: 771 us -> 0 us
  Pallas kernels: 332 us -> 459 us
  blocking collectives: 39.8 us -> 0 us
  other arithmetic: 27.2 us -> 3.89 us
  between operations: 16.1 us -> 2.21 us
    reduce_scatter x5 -> x0, waiting for transfers between devices: 514 us -> none  [scatter_sums(): lax.psum_scatter(total.astype(f32), AXES, scatter_dimension=0, tiled=True)]
    all_gather x5 -> x0, waiting for transfers between devices: 254 us -> none  [gather_weights(): return [lax.all_gather(shard, AXES, axis=0, tiled=True) for shard in shards]]
    pallas_call x2 -> x5, Pallas kernels: 88.4 us -> 298 us  [the longest x1 102 us: arrive(): pl.pallas_call(functools.partial(arrive_kernel, plan, seg_rows, schedule)...]
    psum x1 -> x0, blocking collectives: 39.8 us -> none  [on_device(): lax.psum((grad_mem_tokens, grad_gains, grad_beta.reshape(width)), AXES)]
    pallas_call x2 -> x1, Pallas kernels: 67.2 us -> 33.4 us  [attend_back(): pl.pallas_call(functools.partial(attend_back_kernel, seg_rows), grid=(pai...]
    convert_element_type x5 -> x0, other arithmetic: 25.8 us -> none  [scatter_sums(): total.astype(f32)]
    pallas_call x2 -> x1, Pallas kernels: 43.2 us -> 21.4 us  [attend(): pl.pallas_call(functools.partial(attend_kernel, seg_rows), grid=(pairs,),...]
    pallas_call x2 -> x1, Pallas kernels: 53.5 us -> 34.1 us  [enter_back(): pl.pallas_call(functools.partial(enter_back_kernel, reads, w_sum is not N...]
  transfers between devices with their start and end apart: 10 -> 0, of which waited for: 9 -> 0; matrix products, arithmetic and copies ran while one was open for 2% -> 0% of each run, Pallas kernels for 9% -> 0%
where the time goes in v3:
time: 475 us; the launch traced here: 467 us
  Pallas kernels  459 us (97%)
    pallas_call x1, Pallas kernels, arrive(): pl.pallas_call(functools.partial(arrive_kernel, plan, seg_rows, schedule)...  102 us
    pallas_call x2, Pallas kernels, leave_back(): pl.pallas_call(body, grid=(hidden // size,), in_specs=in_specs, out_specs...  97.2 us
    pallas_call x1, Pallas kernels, finish(): pl.pallas_call(functools.partial(finish_kernel, plan, small, seg_rows, sc...  94.2 us
    pallas_call x2, Pallas kernels, leave_segment(): pl.pallas_call(functools.partial(leave_kernel, reads, earlier is not None...  44.9 us
    pallas_call x1, Pallas kernels, enter_back(): pl.pallas_call(functools.partial(enter_back_kernel, reads, w_sum is not N...  34.1 us
    pallas_call x1, Pallas kernels, attend_back(): pl.pallas_call(functools.partial(attend_back_kernel, seg_rows), grid=(pai...  33.4 us
    pallas_call x1, Pallas kernels, attend(): pl.pallas_call(functools.partial(attend_kernel, seg_rows), grid=(pairs,),...  21.4 us
    pallas_call x1, Pallas kernels, enter_segment(): pl.pallas_call(body, grid=(parts,), in_specs=in_specs, out_specs=out_spec...  19.1 us

profile of v3, /device:TPU:0, one launch (start us, length us, event | category | flops | bytes accessed | tf_op | source)
XLA Modules:
  0.0 467.3 jit_solution(9627626026624902120)
XLA Ops:
  0.6 1.3 fusion
  3.3 1.3 reshape.72.w_beta_ref
  4.5 1.3 convert_element_type.6.refs_2_.refs_3_.gains_ref.refs_5_.refs_6_.refs_7_
  5.8 102.0 %arrive.1 = (bf16[1040,768]{1,0:T(8,128)(2,1)}, bf16[3,1040,768]{2,1,0:T(8,128)(2,1)}, bf16[1040,768]{1,0:T(8,128)(2,1)}, f32[6,1,2176]{2,1,0:T(1,128)}, bf16[4,...) custom-call(bf16[2,1024,768]{2,1,0:T(8,128)(2,1)} %refs_4_.3, ...), custom_call_target="tpu_custom_call" | custom-call | tf_op jit(solution)/shard_map/arrive/pallas_call | solution.py:1429
  107.8 22.2 %leave.2 = (bf16[2,1024,768]{2,1,0:T(8,128)(2,1)}, f32[16,768]{1,0:T(8,128)}, f32[1040,768]{1,0:T(8,128)}, bf16[1040,768]{1,0:T(8,128)(2,1)}, f32[1040,3072]{1,0:T(8,128)}) custom-call(bf16[2,1024,768]{2,1,0:T(8,128)(2,1)} %refs_4_.3, bf16[16,768]{1,0:T(8,128)(2,1)} %refs_5_.3, bf16[1040,768]{1,0:T(8,128)(2,1)} %get-tuple-element.82.refs_2_.refs_5_, ...), custom_call_target="tpu_custom_call" | custom-call | flops 11041505280 | bytes 37748736 | tf_op jit(solution)/shard_map/leave/pallas_call | solution.py:448
  130.0 2.8 write.1
  132.8 19.1 %enter_read.1 = (bf16[1040,768]{1,0:T(8,128)(2,1)}, bf16[3,1040,768]{2,1,0:T(8,128)(2,1)}, f32[1040,768]{1,0:T(8,128)}, f32[1040,768]{1,0:T(8,128)}, f32[1040,16]{1,0:T(8,128)}) custom-call(bf16[2,1024,768]{2,1,0:T(8,128)(2,1)} %refs_4_.3, bf16[16,768]{1,0:T(8,128)(2,1)} %refs_5_.3, ...), custom_call_target="tpu_custom_call" | custom-call | flops 4907335680 | bytes 20971520 | tf_op jit(solution)/shard_map/enter_read/pallas_call | solution.py:202
  151.9 21.4 %attend.1 = (bf16[1040,768]{1,0:T(8,128)(2,1)}, f32[6,1,2176]{2,1,0:T(1,128)}) custom-call(bf16[3,1040,768]{2,1,0:T(8,128)(2,1)} %get-tuple-element.91.qkv_ref), custom_call_target="tpu_custom_call" | custom-call | flops 3322675200 | bytes 7340032 | tf_op jit(solution)/shard_map/attend/pallas_call | solution.py:277
  173.3 22.6 %leave.3 = (bf16[2,1024,768]{2,1,0:T(8,128)(2,1)}, f32[16,768]{1,0:T(8,128)}, f32[1040,768]{1,0:T(8,128)}, bf16[1040,768]{1,0:T(8,128)(2,1)}, f32[1040,3072]{1,0:T(8,128)}) custom-call(f32[1040,768]{1,0:T(8,128)} %get-tuple-element.90.refs_0_.refs_7_, ...), custom_call_target="tpu_custom_call", output_to_operand_aliasing={{0}: (6, {})} | custom-call | flops 11041505280 | bytes 37748736 | tf_op jit(solution)/shard_map/leave/pallas_call | solution.py:448
  195.9 43.0 %leave_back.2 = (f32[1040,768]{1,0:T(8,128)}, bf16[1040,768]{1,0:T(8,128)(2,1)}, f32[768,3072]{1,0:T(8,128)}, f32[3072,768]{1,0:T(8,128)}, f32[768,768]{1,0:T(8,128)}, /*index=5*/f32[1,768]{1,0:T(1,128)}) custom-call(bf16[2,1024,768]{2,1,0:T(8,128)(2,1)} %refs_0_.9, f32[1040,768]{1,0:T(8,128)} %get-tuple-element.99.refs_1_, ...), custom_call_target="tpu_custom_call" | custom-call | flops 22083010560 | bytes 62914560 | tf_op jit(solution)/shard_map/leave_back/pallas_call | solution.py:772
  238.8 33.4 %attend_back.1.refs_3_ = bf16[3,1040,768]{2,1,0:T(8,128)(2,1)} custom-call(bf16[3,1040,768]{2,1,0:T(8,128)(2,1)} %get-tuple-element.91.qkv_ref, bf16[1040,768]{1,0:T(8,128)(2,1)} %get-tuple-element.102.grad_ref, bf16[1040,768]{1,0:T(8,128)(2,1)} %get-tuple-element.92.refs_1_.refs_4_.attended_ref, f32[6,1,2176]{2,1,0:T(1,128)} %get-tuple-element.103.log_ref), custom_call_target="tpu_custom_call" | custom-call | flops 8306688000 | bytes 13631488 | tf_op jit(solution)/shard_map/attend_back/pallas_call | solution.py:351
  272.2 34.1 %enter_back.1 = (f32[2,1024,768]{2,1,0:T(8,128)}, f32[16,768]{1,0:T(8,128)}, f32[768,2304]{1,0:T(8,128)}, f32[1,768]{1,0:T(1,128)}, bf16[768,768]{1,0:T(8,128)(2...) custom-call(bf16[2,1024,768]{2,1,0:T(8,128)(2,1)} %refs_4_.3, bf16[16,768]{1,0:T(8,128)(2,1)} %refs_5_.3, ...), custom_call_target="tpu_custom_call" | custom-call | flops 9814671360 | bytes 31457280 | tf_op jit(solution)/shard_map/enter_back/pallas_call | solution.py:951
  306.4 4.6 write_back.1
  311.0 0.0 copy-start.1
  311.0 0.0 copy-start
  311.0 0.0 copy-start.2
  311.0 0.0 copy-start.3
  311.0 54.2 %leave_back.3 = (f32[1040,768]{1,0:T(8,128)}, bf16[1040,768]{1,0:T(8,128)(2,1)}, bf16[768,3072]{1,0:T(8,128)(2,1)}, bf16[3072,768]{1,0:T(8,128)(2,1)}, bf16[768,...) custom-call(bf16[2,1024,768]{2,1,0:T(8,128)(2,1)} %refs_0_.9, f32[16,768]{1,0:T(8,128)} %get-tuple-element.111.refs_1_, ...), custom_call_target="tpu_custom_call" | custom-call | flops 22083010560 | bytes 62914560 | tf_op jit(solution)/shard_map/leave_back/pallas_call | solution.py:772
  365.2 0.0 copy-done.1
  365.3 0.7 add.5
  365.9 0.0 copy-done
  365.9 0.0 copy-done.2
  365.9 0.0 copy-done.3
  365.9 0.7 select_maximum_fusion.refs_10_
  366.6 94.2 %finish.1 = (f32[1040,768]{1,0:T(8,128)}, f32[96,768]{1,0:T(8,128)}, f32[24,3072]{1,0:T(8,128)}, f32[24,768]{1,0:T(8,128)}, f32[24,2304]{1,0:T(8,128)}, /*index=5*/f32[24,768]{1,0:T(8,128)}) custom-call(bf16[3,1040,768]{2,1,0:T(8,128)(2,1)} %get-tuple-element.95.refs_0_, bf16[1040,768]{1,0:T(8,128)(2,1)} %get-tuple-element.120.refs_1_, ...), custom_call_target="tpu_custom_call" | custom-call | tf_op jit(solution)/shard_map/finish/pallas_call | solution.py:1622
  460.8 5.0 %settle.1 = (f32[2,1024,768]{2,1,0:T(8,128)}, f32[16,768]{1,0:T(8,128)}, f32[2,768]{1,0:T(2,128)}, f32[1,768]{1,0:T(1,128)}, f32[24,2304]{1,0:T(8,128)}, /*index...) custom-call(f32[1040,768]{1,0:T(8,128)} %get-tuple-element.133.first, ...), custom_call_target="tpu_custom_call", output_to_operand_aliasing={{0}: (7, {})} | custom-call | tf_op jit(solution)/shard_map/settle/pallas_call | solution.py:1694
  465.8 1.3 reduce
Async XLA Ops:
  311.0 54.2 %copy-start.1 = (f32[1,768]{1,0:T(1,128)S(1)}, f32[1,768]{1,0:T(1,128)}, u32[]{:S(2)}) copy-start(f32[1,768]{1,0:T(1,128)} %get-tuple-element.126) | copy-start | bytes 9220
  311.0 54.9 %copy-start = (f32[16,768]{1,0:T(8,128)S(1)}, f32[16,768]{1,0:T(8,128)}, u32[]{:S(2)}) copy-start(f32[16,768]{1,0:T(8,128)} %get-tuple-element.124) | copy-start | bytes 147460
  311.0 54.9 %copy-start.2 = (f32[1,768]{1,0:T(1,128)S(1)}, f32[1,768]{1,0:T(1,128)}, u32[]{:S(2)}) copy-start(f32[1,768]{1,0:T(1,128)} %get-tuple-element.125) | copy-start | bytes 9220
  311.0 54.9 %copy-start.3 = (f32[1,768]{1,0:T(1,128)S(1)}, f32[1,768]{1,0:T(1,128)}, u32[]{:S(2)}) copy-start(f32[1,768]{1,0:T(1,128)} %get-tuple-element.128) | copy-start | bytes 9220

commit v4 on v3

--- a/solution.py
+++ b/solution.py
@@ -16,7 +16,8 @@
 gelu_a = 0.044715
 f32 = jnp.float32
 low_type = jnp.bfloat16
-VMEM_BYTES = 60 * 2**20
+MIB = 2**20
+ANYWHERE = pl.BlockSpec(memory_space=pl.ANY)
 
 
 def nn(left, right):
@@ -97,8 +98,8 @@
     return pl.BlockSpec(shape, lambda *_: zeros)
 
 
-def params(**extra):
-    return pltpu.CompilerParams(vmem_limit_bytes=VMEM_BYTES, **extra)
+def params(mib=60, **extra):
+    return pltpu.CompilerParams(vmem_limit_bytes=mib * MIB, **extra)
 
 
 def shaped(shape, dtype):
@@ -206,7 +207,7 @@
         out_specs=out_specs,
         out_shape=out_shape,
         scratch_shapes=[pltpu.VMEM((rows, width), low_type)],
-        compiler_params=params(),
+        compiler_params=params(24),
         cost_estimate=pl.CostEstimate(
             flops=2 * macs, bytes_accessed=20 * 2**20, transcendentals=0
         ),
@@ -283,7 +284,7 @@
             pl.BlockSpec((1, 1, lanes), lambda h: (h, 0, 0)),
         ],
         out_shape=[shaped((rows, width), low_type), shaped((pairs, 1, lanes), f32)],
-        compiler_params=params(),
+        compiler_params=params(10),
         cost_estimate=pl.CostEstimate(
             flops=4 * rows * rows * width, bytes_accessed=7 * 2**20, transcendentals=0
         ),
@@ -360,7 +361,7 @@
         out_specs=three,
         out_shape=shaped((parts, rows, width), low_type),
         scratch_shapes=[pltpu.VMEM((rows, PAIR), f32), pltpu.VMEM((rows, PAIR), f32)],
-        compiler_params=params(),
+        compiler_params=params(12),
         cost_estimate=pl.CostEstimate(
             flops=10 * rows * rows * width, bytes_accessed=13 * 2**20, transcendentals=0
         ),
@@ -465,7 +466,7 @@
         ],
         scratch_shapes=scratch,
         input_output_aliases=aliases,
-        compiler_params=params(),
+        compiler_params=params(40),
         cost_estimate=pl.CostEstimate(
             flops=2 * rows * width * (width + 2 * hidden), bytes_accessed=36 * 2**20, transcendentals=0
         ),
@@ -538,7 +539,7 @@
         ],
         out_specs=[result(s.shape) for s in out_shape],
         out_shape=out_shape,
-        compiler_params=params(),
+        compiler_params=params(10),
         name="write",
     )(flag, mem_out, w_mem, w_mem, w_beta)
     return dict(zip(names, outs))
@@ -609,7 +610,7 @@
         + [whole(a.shape) for a in args[4:]],
         out_specs=[result(s.shape) for s in out_shape],
         out_shape=out_shape,
-        compiler_params=params(),
+        compiler_params=params(12),
         name="write_back",
     )(*args)
 
@@ -784,6 +785,169 @@
     )(*args)
 
 
+def leave_both_kernel(reads, adds, *refs):
+    if reads:
+        (states_one_ref, *refs) = refs
+    else:
+        (tokens_ref, mem_ref, *refs) = refs
+    (attended_ref, out_grad_ref, gains_ref, w_out_ref, w_up_ref, w_down_ref, *refs) = refs
+    if adds:
+        refs = refs[1:]
+    (
+        out_ref,
+        grad_states_ref,
+        grad_attended_ref,
+        grad_up_ref,
+        grad_down_ref,
+        grad_out_ref,
+        grad_gain_ref,
+        states_two_ref,
+        normed_ref,
+        forward_ref,
+        backward_ref,
+        grad_low_ref,
+        *scratch,
+    ) = refs
+    rows, width = attended_ref.shape
+    seg_rows = out_grad_ref.shape[0]
+    step = pl.program_id(0)
+
+    @pl.when(step == 0)
+    def _():
+        if not reads:
+            load_first(tokens_ref, mem_ref, scratch[0])
+        grad_low_ref[:seg_rows, :] = out_grad_ref[...]
+        grad_low_ref[seg_rows:, :] = jnp.zeros((rows - seg_rows, width), low_type)
+
+        def chunk(at):
+            source = states_one_ref if reads else scratch[0]
+            states = source[at, :].astype(f32) + nn(attended_ref[at, :], w_out_ref[...])
+            states_two_ref[at, :] = states
+            unit, _ = normal_form(states)
+            normed_ref[at, :] = low(unit * gains_ref[1:2, :])
+            forward_ref[at, :] = states
+            backward_ref[at, :] = jnp.zeros_like(states)
+
+        over_rows(rows, chunk)
+
+    normed = normed_ref[...]
+    grad_low = grad_low_ref[...]
+    upward = nn(normed, w_up_ref[...])
+    grad_active = nt(grad_low, w_down_ref[...])
+    active, slope = gelu_parts(upward)
+    active = low(active)
+    grad_upward = low(grad_active * slope)
+    forward_ref[...] += nn(active, w_down_ref[...])
+    backward_ref[...] += nt(grad_upward, w_up_ref[...])
+    grad_down = tn(active, grad_low)
+    grad_up = tn(normed, grad_upward)
+    grad_down_ref[...] = grad_down.astype(grad_down_ref.dtype)
+    grad_up_ref[...] = grad_up.astype(grad_up_ref.dtype)
+
+    @pl.when(step == pl.num_programs(0) - 1)
+    def _():
+        gain = gains_ref[1:2, :]
+        grad_gain_ref[...] = jnp.zeros_like(grad_gain_ref)
+
+        def chunk(at):
+            unit, inverse = normal_form(states_two_ref[at, :])
+            grad = backward_ref[at, :]
+            grad_gain_ref[...] += jnp.sum(grad * unit, axis=0, keepdims=True)
+            total = grad_low_ref[at, :].astype(f32) + norm_back(grad, unit, inverse, gain)
+            grad_states_ref[at, :] = total
+            total_low = low(total)
+            normed_ref[at, :] = total_low
+            grad_attended_ref[at, :] = low(nt(total_low, w_out_ref[...]))
+
+        over_rows(rows, chunk)
+        grad_out = tn(attended_ref[...], normed_ref[...])
+        grad_out_ref[...] = grad_out.astype(grad_out_ref.dtype)
+        out_ref[...] = low(forward_ref[:seg_rows, :])
+
+
+def gelu_parts(upward):
+    square = upward * upward
+    bent = jnp.tanh(upward * (gelu_c + gelu_c * gelu_a * square))
+    half = 0.5 + 0.5 * bent
+    active = upward * half
+    slope = half + (active - active * half) * (2.0 * gelu_c + 6.0 * gelu_c * gelu_a * square)
+    return active, slope
+
+
+def leave_both(slot, start, attended, out_grad, gains, w_out, w_up, w_down, earlier, grad_type):
+    slots, seg_rows, width = out_grad.shape
+    rows = attended.shape[0]
+    mems = rows - seg_rows
+    hidden = w_up.shape[1]
+    size = 512 if hidden % 512 == 0 else hidden
+    reads = not isinstance(start, tuple)
+    args = []
+    in_specs = []
+    scratch = [
+        pltpu.VMEM((rows, width), f32),
+        pltpu.VMEM((rows, width), low_type),
+        pltpu.VMEM((rows, width), f32),
+        pltpu.VMEM((rows, width), f32),
+        pltpu.VMEM((rows, width), low_type),
+    ]
+    segment = pl.BlockSpec((None, seg_rows, width), lambda j: (slot, 0, 0), pipeline_mode=pl.Buffered(1))
+    if reads:
+        args.append(start)
+        in_specs.append(whole((rows, width)))
+    else:
+        args += list(start)
+        in_specs += [segment, whole((mems, width))]
+        scratch.append(pltpu.VMEM((rows, width), low_type))
+    up_spec = pl.BlockSpec((width, size), lambda j: (0, j))
+    down_spec = pl.BlockSpec((size, width), lambda j: (j, 0))
+    args += [attended, out_grad, gains, w_out, w_up, w_down]
+    in_specs += [
+        whole((rows, width)),
+        segment,
+        whole(gains.shape),
+        whole((width, width)),
+        up_spec,
+        down_spec,
+    ]
+    aliases = {}
+    if earlier is not None:
+        args.append(earlier)
+        in_specs.append(ANYWHERE)
+        aliases = {len(args) - 1: 0}
+    outs = pl.pallas_call(
+        functools.partial(leave_both_kernel, reads, earlier is not None),
+        grid=(hidden // size,),
+        in_specs=in_specs,
+        out_specs=[
+            segment,
+            whole((rows, width)),
+            whole((rows, width)),
+            up_spec,
+            down_spec,
+            whole((width, width)),
+            whole((1, width)),
+        ],
+        out_shape=[
+            shaped((slots, seg_rows, width), low_type),
+            shaped((rows, width), f32),
+            shaped((rows, width), low_type),
+            shaped((width, hidden), grad_type),
+            shaped((hidden, width), grad_type),
+            shaped((width, width), grad_type),
+            shaped((1, width), f32),
+        ],
+        scratch_shapes=scratch,
+        input_output_aliases=aliases,
+        compiler_params=params(50),
+        cost_estimate=pl.CostEstimate(
+            flops=6 * rows * width * (width + 2 * hidden), bytes_accessed=60 * 2**20, transcendentals=0
+        ),
+        name="leave_both",
+    )(*args)
+    names = ("block_out", "grad_states", "grad_attended", "up", "down", "out", "gain_two")
+    return dict(zip(names, outs))
+
+
 def enter_back_kernel(reads, adds, earlier, *refs):
     (tokens_ref, mem_ref, normed_ref, grad_qkv_ref, grad_states_ref, gains_ref, w_ref, *refs) = refs
     if reads:
@@ -956,7 +1120,7 @@
         out_shape=out_shape,
         scratch_shapes=scratch,
         input_output_aliases=aliases,
-        compiler_params=params(),
+        compiler_params=params(36),
         cost_estimate=pl.CostEstimate(
             flops=4 * rows * width * width * (parts + 1), bytes_accessed=30 * 2**20, transcendentals=0
         ),
@@ -1346,9 +1510,6 @@
 
 def flat(array):
     return array.reshape(DEVICES * array.shape[-2], array.shape[-1])
-
-
-ANYWHERE = pl.BlockSpec(memory_space=pl.ANY)
 
 
 def gather_weights(shards):
@@ -1700,7 +1861,7 @@
         out_specs=[pl.BlockSpec((None, size, width), lambda j: (0, j, 0))] + [result(s) for s in shapes],
         out_shape=[shaped(grad_tokens.shape, f32)] + [shaped(s, f32) for s in shapes],
         input_output_aliases={2 + len(sums): 0},
-        compiler_params=params(),
+        compiler_params=params(10),
         name="settle",
     )(first, small, *sums, grad_tokens)
 
@@ -1744,11 +1905,14 @@
                 kept["states_one"], kept["query"], kept["match"] = entered[2:]
                 start = kept["states_one"]
             kept["attended"], kept["logs"] = attend(kept["qkv"], seg_rows)
-        out, mem_out, kept["states_two"], kept["normed_two"], kept["upward"] = leave_segment(
-            slot, slots, seg_rows, start, kept["attended"], gains, w_out, w_up, w_down, out
-        )
-        kept["mem_out"] = mem_out
-        if slot + 1 < slots:
+        if slot + 1 == slots:
+            both = leave_both(slot, start, kept["attended"], out_grad, gains, w_out, w_up, w_down, out, f32)
+            out = both["block_out"]
+        else:
+            out, mem_out, kept["states_two"], kept["normed_two"], kept["upward"] = leave_segment(
+                slot, slots, seg_rows, start, kept["attended"], gains, w_out, w_up, w_down, out
+            )
+            kept["mem_out"] = mem_out
             written[slot + 1] = write_memory(same_item[slot : slot + 1], mem_out, w_mem, w_beta)
         kept_all.append(kept)
 
@@ -1773,9 +1937,11 @@
             grad_beta += grad_beta_part
             if fast and last:
                 mem_plan = [slabs(w_query_sum), slabs(w_pair_sum)]
-        left = leave_back(
-            slot, out_grad, grad_rows, kept, gains, w_out, w_up, w_down, sums, grad_type, mem_plan
-        )
+            left = leave_back(
+                slot, out_grad, grad_rows, kept, gains, w_out, w_up, w_down, sums, grad_type, mem_plan
+            )
+        else:
+            left = [both[name] for name in ("grad_states", "grad_attended", "up", "down", "out", "gain_two")]
         grad_states, grad_attended, up_sum, down_sum, out_sum, gain_two, *mem_total = left
         gain_two_sum += gain_two
         sums = {"up": up_sum, "down": down_sum, "out": out_sum}

time: 475 us -> 458 us (0.964)
  Pallas kernels: 459 us -> 424 us
  local copies, waits for them, and re-layouts: 2.59 us -> 21.1 us
    pallas_call x0 -> x1, Pallas kernels: none -> 52.4 us  [leave_both(): pl.pallas_call(functools.partial(leave_both_kernel, reads, earlier is not...]
    pallas_call x2 -> x1, Pallas kernels: 97.2 us -> 54 us  [leave_back(): pl.pallas_call(body, grid=(hidden // size,), in_specs=in_specs, out_specs...]
    pallas_call x2 -> x1, Pallas kernels: 44.9 us -> 19.5 us  [leave_segment(): pl.pallas_call(functools.partial(leave_kernel, reads, earlier is not None...]
    unnamed x8 -> x66, local copies, waits for them, and re-layouts: 0.02 us -> 19 us
    pallas_call x1, Pallas kernels: 19.1 us -> 13.8 us  [enter_segment(): pl.pallas_call(body, grid=(parts,), in_specs=in_specs, out_specs=out_spec...]
    pallas_call x1, Pallas kernels: 34.1 us -> 29.2 us  [enter_back(): pl.pallas_call(functools.partial(enter_back_kernel, reads, w_sum is not N...]
where the time goes in v4:
time: 458 us; the launch traced here: 451 us
  Pallas kernels  424 us (93%)
  local copies, waits for them, and re-layouts  21.1 us (5%)
    pallas_call x1, Pallas kernels, arrive(): pl.pallas_call(functools.partial(arrive_kernel, plan, seg_rows, schedule)...  102 us
    pallas_call x1, Pallas kernels, finish(): pl.pallas_call(functools.partial(finish_kernel, plan, small, seg_rows, sc...  94.3 us
    pallas_call x1, Pallas kernels, leave_back(): pl.pallas_call(body, grid=(hidden // size,), in_specs=in_specs, out_specs...  54 us
    pallas_call x1, Pallas kernels, leave_both(): pl.pallas_call(functools.partial(leave_both_kernel, reads, earlier is not...  52.4 us
    pallas_call x1, Pallas kernels, attend_back(): pl.pallas_call(functools.partial(attend_back_kernel, seg_rows), grid=(pai...  33.4 us
    pallas_call x1, Pallas kernels, enter_back(): pl.pallas_call(functools.partial(enter_back_kernel, reads, w_sum is not N...  29.2 us
    pallas_call x1, Pallas kernels, attend(): pl.pallas_call(functools.partial(attend_kernel, seg_rows), grid=(pairs,),...  20.4 us
    pallas_call x1, Pallas kernels, leave_segment(): pl.pallas_call(functools.partial(leave_kernel, reads, earlier is not None...  19.5 us

profile of v4, /device:TPU:0, one launch (start us, length us, event | category | flops | bytes accessed | tf_op | source)
XLA Modules:
  0.0 450.7 jit_solution(13449189735269138562)
XLA Ops:
  0.6 0.0 copy-start.10
  0.7 0.0 copy-start.2
  0.7 1.4 fusion
  3.4 0.7 reshape.72.w_beta_ref
  4.1 1.3 convert_element_type.6.refs_2_.refs_3_.gains_ref.refs_5_.refs_6_.refs_7_
  5.3 102.0 %arrive.1 = (bf16[1040,768]{1,0:T(8,128)(2,1)}, bf16[3,1040,768]{2,1,0:T(8,128)(2,1)}, bf16[1040,768]{1,0:T(8,128)(2,1)}, f32[6,1,2176]{2,1,0:T(1,128)}, bf16[4,...) custom-call(bf16[2,1024,768]{2,1,0:T(8,128)(2,1)} %refs_4_.3, ...), custom_call_target="tpu_custom_call" | custom-call | tf_op jit(solution)/shard_map/arrive/pallas_call | solution.py:1590
  107.3 0.0 copy-done.10
  107.3 0.0 copy-done.2
  107.3 1.4 copy-done.5
  108.8 1.3 copy-done.15
  110.0 19.5 %leave.1 = (bf16[2,1024,768]{2,1,0:T(8,128)(2,1)}, f32[16,768]{1,0:T(8,128)S(1)}, f32[1040,768]{1,0:T(8,128)S(1)}, bf16[1040,768]{1,0:T(8,128)(2,1)S(1)}, f32[1040,3072]{1,0:T(8,128)}) custom-call(bf16[2,1024,768]{2,1,0:T(8,128)(2,1)S(1)} %copy-done.2, bf16[16,768]{1,0:T(8,128)(2,1)S(1)} %copy-done.10, bf16[1040,768]{1,0:T(8,128)(2,1)S(1)} %copy-done.5, ...), custom_call_target="tpu_custom_call" | custom-call | flops 11041505280 | bytes 37748736 | tf_op jit(solution)/shard_map/leave/pallas_call | solution.py:449
  129.6 0.5 write.1
  130.1 1.1 copy-done.31
  131.2 0.8 copy-done.32
  132.0 1.3 copy-done.3
  133.3 13.8 %enter_read.1 = (bf16[1040,768]{1,0:T(8,128)(2,1)S(1)}, bf16[3,1040,768]{2,1,0:T(8,128)(2,1)S(1)}, f32[1040,768]{1,0:T(8,128)S(1)}, f32[1040,768]{1,0:T(8,128)S(1)}, f32[1040,16]{1,0:T(8,128)S(1)}) custom-call(bf16[2,1024,768]{2,1,0:T(8,128)(2,1)S(1)} %copy-done.2, bf16[16,768]{1,0:T(8,128)(2,1)S(1)} %copy-done.10, f32[2,768]{1,0:T(2,128)S(1)} %copy-done.13, ...), custom_call_target="tpu_custom_call" | custom-call | flops 4907335680 | bytes 20971520 | tf_op jit(solution)/shard_map/enter_read/pallas_call | solution.py:203
  147.1 0.0 copy-start.29
  147.2 1.2 copy-done.29
  148.3 20.4 %attend.1 = (bf16[1040,768]{1,0:T(8,128)(2,1)S(1)}, f32[6,1,2176]{2,1,0:T(1,128)S(1)}) custom-call(bf16[3,1040,768]{2,1,0:T(8,128)(2,1)S(1)} %get-tuple-element.88.qkv_ref), custom_call_target="tpu_custom_call" | custom-call | flops 3322675200 | bytes 7340032 | tf_op jit(solution)/shard_map/attend/pallas_call | solution.py:278
  168.8 1.1 copy-done.27
  170.0 52.4 %leave_both.1 = (bf16[2,1024,768]{2,1,0:T(8,128)(2,1)}, f32[1040,768]{1,0:T(8,128)}, bf16[1040,768]{1,0:T(8,128)(2,1)S(1)}, f32[768,3072]{1,0:T(8,128)}, f32[307...) custom-call(f32[1040,768]{1,0:T(8,128)} %copy-done.22, ...), custom_call_target="tpu_custom_call", output_to_operand_aliasing={{0}: (7, {})} | custom-call | flops 33124515840 | bytes 62914560 | tf_op jit(solution)/shard_map/leave_both/pallas_call | solution.py:917
  222.4 0.0 copy-done.20
  222.4 0.0 copy-done.28
  222.4 0.0 copy-start.23
  222.4 0.0 copy-start.25
  222.4 0.0 copy-start.26
  222.5 0.0 copy-start.30
  222.5 33.4 %attend_back.1.refs_3_ = bf16[3,1040,768]{2,1,0:T(8,128)(2,1)S(1)} custom-call(bf16[3,1040,768]{2,1,0:T(8,128)(2,1)S(1)} %copy-done.20, bf16[1040,768]{1,0:T(8,128)(2,1)S(1)} %get-tuple-element.96.grad_ref, bf16[1040,768]{1,0:T(8,128)(2,1)S(1)} %copy-done.28, f32[6,1,2176]{2,1,0:T(1,128)S(1)} %get-tuple-element.97.log_ref), custom_call_target="tpu_custom_call" | custom-call | flops 8306688000 | bytes 13631488 | tf_op jit(solution)/shard_map/attend_back/pallas_call | solution.py:352
  255.8 0.0 copy-start.21
  255.9 2.1 copy-done.21
  258.0 29.2 %enter_back.1 = (f32[2,1024,768]{2,1,0:T(8,128)}, f32[16,768]{1,0:T(8,128)S(1)}, f32[768,2304]{1,0:T(8,128)}, f32[1,768]{1,0:T(1,128)S(1)}, bf16[768,768]{1,0:T(...) custom-call(bf16[2,1024,768]{2,1,0:T(8,128)(2,1)S(1)} %copy-done.2, ...), custom_call_target="tpu_custom_call" | custom-call | flops 9814671360 | bytes 31457280 | tf_op jit(solution)/shard_map/enter_back/pallas_call | solution.py:1115
  287.3 1.5 write_back.1
  288.8 0.0 copy-done.18
  288.8 0.0 copy-start.14
  288.8 1.4 copy-done.14
  290.2 0.6 copy-done.17
  290.8 54.0 %leave_back.1 = (f32[1040,768]{1,0:T(8,128)}, bf16[1040,768]{1,0:T(8,128)(2,1)}, bf16[768,3072]{1,0:T(8,128)(2,1)}, bf16[3072,768]{1,0:T(8,128)(2,1)}, bf16[768,...) custom-call(bf16[2,1024,768]{2,1,0:T(8,128)(2,1)} %refs_0_.7, f32[16,768]{1,0:T(8,128)} %copy-done.17, ...), custom_call_target="tpu_custom_call" | custom-call | flops 22083010560 | bytes 62914560 | tf_op jit(solution)/shard_map/leave_back/pallas_call | solution.py:773
  344.9 0.7 add.5
  345.6 0.7 select_maximum_fusion.refs_10_
  346.2 94.3 %finish.1 = (f32[1040,768]{1,0:T(8,128)}, f32[96,768]{1,0:T(8,128)}, f32[24,3072]{1,0:T(8,128)}, f32[24,768]{1,0:T(8,128)}, f32[24,2304]{1,0:T(8,128)}, /*index=5*/f32[24,768]{1,0:T(8,128)}) custom-call(bf16[3,1040,768]{2,1,0:T(8,128)(2,1)} %get-tuple-element.92.refs_0_, bf16[1040,768]{1,0:T(8,128)(2,1)} %get-tuple-element.114.refs_1_, ...), custom_call_target="tpu_custom_call" | custom-call | tf_op jit(solution)/shard_map/finish/pallas_call | solution.py:1783
  440.5 1.9 copy-done.4
  442.4 1.0 copy-done.6
  443.4 1.0 copy-done.7
  444.3 0.9 copy-done.9
  445.3 0.9 copy-done.11
  446.2 0.9 copy-done.12
  447.0 2.6 settle.1
  449.6 0.6 reduce
  (36 shorter events, 0.1 us)
Async XLA Ops:
  0.6 106.7 %copy-start.10 = (bf16[16,768]{1,0:T(8,128)(2,1)S(1)}, bf16[16,768]{1,0:T(8,128)(2,1)}, u32[]{:S(2)}) copy-start(bf16[16,768]{1,0:T(8,128)(2,1)} %refs_5_.3) | copy-start | bytes 73732
  0.7 106.7 %copy-start.2 = (bf16[2,1024,768]{2,1,0:T(8,128)(2,1)S(1)}, bf16[2,1024,768]{2,1,0:T(8,128)(2,1)}, u32[]{:S(2)}) copy-start(bf16[2,1024,768]{2,1,0:T(8,128)(2,1)} %refs_4_.3) | copy-start | bytes 9437188
  5.3 102.0 %copy-start.13 = (f32[2,768]{1,0:T(2,128)S(1)}, f32[2,768]{1,0:T(2,128)}, u32[]{:S(2)}) copy-start(f32[2,768]{1,0:T(2,128)} %convert_element_type.6.refs_2_.refs_3_.gains_ref.refs_5_.refs_6_.refs_7_) | copy-start | bytes 18436
  107.3 1.4 copy-start.5
  108.8 1.3 copy-start.15
  110.0 19.5 %copy-start = (bf16[4,2,2,2,24,2304]{5,4,3,2,1,0:T(8,128)(2,1)S(1)}, bf16[4,2,2,2,24,2304]{5,4,3,2,1,0:T(8,128)(2,1)}, u32[]{:S(2)}) copy-start(bf16[4,2,2,2,24,2304]{5,4,3,2,1,0:T(8,128)(2,1)} %get-tuple-element.78) | copy-start | bytes 10616836
  129.6 1.6 copy-start.31
  129.6 2.4 copy-start.32
  129.6 3.7 copy-start.3
  147.1 1.2 copy-start.29
  148.3 20.5 %copy-start.19 = (bf16[3,1040,768]{2,1,0:T(8,128)(2,1)}, bf16[3,1040,768]{2,1,0:T(8,128)(2,1)S(1)}, u32[]{:S(2)}) copy-start(bf16[3,1040,768]{2,1,0:T(8,128)(2,1)S(1)} %get-tuple-element.88.qkv_ref) | copy-start | bytes 14376964
  148.3 20.5 %copy-start.22 = (f32[1040,768]{1,0:T(8,128)}, f32[1040,768]{1,0:T(8,128)S(1)}, u32[]{:S(2)}) copy-start(f32[1040,768]{1,0:T(8,128)S(1)} %get-tuple-element.87.refs_0_.refs_7_) | copy-start | bytes 9584644
  148.3 20.5 %copy-start.24 = (f32[1040,768]{1,0:T(8,128)}, f32[1040,768]{1,0:T(8,128)S(1)}, u32[]{:S(2)}) copy-start(f32[1040,768]{1,0:T(8,128)S(1)} %get-tuple-element.99.refs_8_) | copy-start | bytes 9584644
  148.3 21.6 %copy-start.16 = (bf16[4,2,2,2,24,768]{5,4,3,2,1,0:T(8,128)(2,1)S(1)}, bf16[4,2,2,2,24,768]{5,4,3,2,1,0:T(8,128)(2,1)}, u32[]{:S(2)}) copy-start(bf16[4,2,2,2,24,768]{5,4,3,2,1,0:T(8,128)(2,1)} %get-tuple-element.80) | copy-start | bytes 3538948
  168.8 1.1 copy-start.27
  170.0 52.4 %copy-start.20 = (bf16[3,1040,768]{2,1,0:T(8,128)(2,1)S(1)}, bf16[3,1040,768]{2,1,0:T(8,128)(2,1)}, u32[]{:S(2)}) copy-start(bf16[3,1040,768]{2,1,0:T(8,128)(2,1)} %copy-done.19) | copy-start | bytes 14376964
  170.0 52.5 %copy-start.28 = (bf16[1040,768]{1,0:T(8,128)(2,1)S(1)}, bf16[1040,768]{1,0:T(8,128)(2,1)}, u32[]{:S(2)}) copy-start(bf16[1040,768]{1,0:T(8,128)(2,1)} %copy-done.27) | copy-start | bytes 4792324
  222.4 35.6 %copy-start.23 = (f32[1040,768]{1,0:T(8,128)S(1)}, f32[1040,768]{1,0:T(8,128)}, u32[]{:S(2)}) copy-start(f32[1040,768]{1,0:T(8,128)} %copy-done.22) | copy-start | bytes 9584644
  222.4 35.6 %copy-start.25 = (f32[1040,768]{1,0:T(8,128)S(1)}, f32[1040,768]{1,0:T(8,128)}, u32[]{:S(2)}) copy-start(f32[1040,768]{1,0:T(8,128)} %copy-done.24) | copy-start | bytes 9584644
  222.4 35.6 %copy-start.26 = (f32[1040,768]{1,0:T(8,128)S(1)}, f32[1040,768]{1,0:T(8,128)}, u32[]{:S(2)}) copy-start(f32[1040,768]{1,0:T(8,128)} %get-tuple-element.98.refs_4_) | copy-start | bytes 9584644
  222.5 35.6 %copy-start.30 = (bf16[1040,768]{1,0:T(8,128)(2,1)S(1)}, bf16[1040,768]{1,0:T(8,128)(2,1)}, u32[]{:S(2)}) copy-start(bf16[1040,768]{1,0:T(8,128)(2,1)} %copy-done.29) | copy-start | bytes 4792324
  255.8 2.2 copy-start.21
  258.0 29.3 %copy-start.1 = (bf16[4,2,2,2,24,2304]{5,4,3,2,1,0:T(8,128)(2,1)S(1)}, bf16[4,2,2,2,24,2304]{5,4,3,2,1,0:T(8,128)(2,1)}, u32[]{:S(2)}) copy-start(bf16[4,2,2,2,24,2304]{5,4,3,2,1,0:T(8,128)(2,1)} %get-tuple-element.78) | copy-start | bytes 10616836
  287.3 1.5 copy-start.18
  288.8 1.4 copy-start.14
  290.2 0.6 copy-start.17
  346.2 94.3 %copy-start.8 = (f32[24,2304]{1,0:T(8,128)S(1)}, f32[24,2304]{1,0:T(8,128)}, u32[]{:S(2)}) copy-start(f32[24,2304]{1,0:T(8,128)} %get-tuple-element.129.refs_1_) | copy-start | bytes 663556
  440.5 1.9 copy-start.4
  442.4 1.0 copy-start.6
  443.4 1.0 copy-start.7
  444.3 0.9 copy-start.9
  445.3 0.9 copy-start.11
  446.2 0.9 copy-start.12

commit v5 on v4

--- a/solution.py
+++ b/solution.py
@@ -48,7 +48,10 @@
     return rows
 
 
-def over_rows(rows, body):
+def over_rows(rows, body, at_once=True):
+    if at_once:
+        body(pl.ds(0, rows))
+        return
     count = row_chunk(rows)
 
     @pl.loop(0, rows // count)
@@ -119,7 +122,7 @@
 
         def chunk(at):
             unit, _ = normal_form(first_ref[at, :].astype(f32))
-            normed_ref[at, :] = low(unit * gains_ref[0:1, :])
+            normed_ref[at, :] = low(unit * gains_ref[0:1, :].astype(f32))
 
         over_rows(first_ref.shape[0], chunk)
 
@@ -163,7 +166,7 @@
             states = first.astype(f32) + numerator / below
             states_ref[at, :] = states
             unit, _ = normal_form(states)
-            normed_ref[at, :] = low(unit * gains_ref[0:1, :])
+            normed_ref[at, :] = low(unit * gains_ref[0:1, :].astype(f32))
 
         over_rows(first_ref.shape[0], chunk)
 
@@ -249,7 +252,9 @@
     return jnp.transpose(jnp.broadcast_to(column, (count, 128)))[0:1, :]
 
 
-def attend_kernel(seg_rows, qkv_ref, attended_ref, log_ref, lanes=slice(None)):
+def attend_kernel(
+    seg_rows, qkv_ref, attended_ref, log_ref, lanes=slice(None), pair=0
+):
     rows = qkv_ref.shape[1]
     places, _ = packed_lanes(rows, seg_rows)
     for (start, count), place in zip(query_blocks(rows, seg_rows), places):
@@ -266,9 +271,9 @@
         total = jnp.sum(grown, axis=1, keepdims=True)
         probs = low(grown * (1.0 / total))
         mixed = merge_heads(nn(probs, qkv_ref[2, :reach, lanes]))
-        attended_ref[start:reach, :] = low(mixed)
+        attended_ref[start:reach, lanes] = low(mixed)
         log_row = as_row(peak + jnp.log(total))
-        log_ref[0, 0:1, place : place + 2 * count] = log_row
+        log_ref[pair, 0:1, place : place + 2 * count] = log_row
 
 
 def attend(qkv, seg_rows):
@@ -394,7 +399,7 @@
             states = source[at, :].astype(f32) + nn(attended_ref[at, :], w_out_ref[...])
             states_two_ref[at, :] = states
             unit, _ = normal_form(states)
-            normed_ref[at, :] = low(unit * gains_ref[1:2, :])
+            normed_ref[at, :] = low(unit * gains_ref[1:2, :].astype(f32))
             sum_ref[at, :] = states
 
         over_rows(rows, chunk)
@@ -487,6 +492,7 @@
 
 
 def write_kernel(
+    slot,
     flag_ref,
     mem_out_ref,
     w_key_ref,
@@ -499,7 +505,7 @@
     delta_ref,
     beta_row_ref,
 ):
-    flag = flag_ref[0]
+    flag = jnp.where(flag_ref[slot + 1] == flag_ref[slot], 1.0, 0.0).astype(f32)
     width = key_ref.shape[1]
     mem_out = mem_out_ref[...]
     mem_low = low(mem_out)
@@ -511,12 +517,12 @@
         high, rest = split(part)
         phi_ref[:, index * width : (index + 1) * width] = high
         phi_rest_ref[:, index * width : (index + 1) * width] = rest
-    beta, beta_row = beta_parts(mem_out, w_beta_ref[...])
+    beta, beta_row = beta_parts(mem_out, w_beta_ref[...].astype(f32))
     delta_ref[...] = low(low(beta * value).astype(f32) * flag)
     beta_row_ref[...] = beta_row * flag
 
 
-def write_memory(flag, mem_out, w_mem, w_beta):
+def write_memory(slot, flag, mem_out, w_mem, w_beta):
     mems, width = mem_out.shape
     names = ("key", "value", "phi_keys_low", "phi_keys_rest", "delta_low", "beta_row")
     out_shape = [
@@ -528,7 +534,7 @@
         shaped((1, mems), f32),
     ]
     outs = pl.pallas_call(
-        write_kernel,
+        functools.partial(write_kernel, slot),
         grid=(1,),
         in_specs=[
             pl.BlockSpec(memory_space=pltpu.SMEM),
@@ -546,6 +552,7 @@
 
 
 def write_back_kernel(
+    slot,
     flag_ref,
     mem_out_ref,
     w_key_ref,
@@ -560,11 +567,11 @@
     grad_w_ref,
     grad_beta_ref,
 ):
-    flag = flag_ref[0]
+    flag = jnp.where(flag_ref[slot + 1] == flag_ref[slot], 1.0, 0.0).astype(f32)
     width = key_ref.shape[1]
     mem_out = mem_out_ref[...]
     mem_low = low(mem_out)
-    w_beta = w_beta_ref[...]
+    w_beta = w_beta_ref[...].astype(f32)
     key = key_ref[...]
     value = value_ref[...]
     beta, _ = beta_parts(mem_out, w_beta)
@@ -589,7 +596,7 @@
     grad_w_ref[:, width:] = low(tn(mem_low, grad_value))
 
 
-def write_back(flag, mem_out, w_mem, w_beta, written, grad_delta, grad_phi, grad_normal):
+def write_back(slot, flag, mem_out, w_mem, w_beta, written, grad_delta, grad_phi, grad_normal):
     mems, width = mem_out.shape
     args = [flag, mem_out, w_mem, w_mem, w_beta, written["key"], written["value"]]
     args += [grad_delta, grad_phi, grad_normal]
@@ -599,7 +606,7 @@
         shaped((1, width), f32),
     ]
     return pl.pallas_call(
-        write_back_kernel,
+        functools.partial(write_back_kernel, slot),
         grid=(1,),
         in_specs=[
             pl.BlockSpec(memory_space=pltpu.SMEM),
@@ -678,7 +685,7 @@
 
     @pl.when(step == pl.num_programs(0) - 1)
     def _():
-        gain = gains_ref[1:2, :]
+        gain = gains_ref[1:2, :].astype(f32)
         grad_gain_ref[...] = jnp.zeros_like(grad_gain_ref)
 
         def chunk(at):
@@ -758,9 +765,9 @@
             for at in range(0, cols, width):
                 groups.append((a, at, width, 0, before + at, cut(width, (1, 1)), False))
             before += cols
-        plan = Reduce(groups, shapes)
+        plan = Reduce(groups, shapes, event_order(len(groups), 2))
         grid = hidden // size
-        schedule = {1: (0,), 2: (1,), 3: (2,), 4: (3,), 5: (4,), grid: (5,)}
+        schedule = spread(plan.order, {1: (0, 1), 2: (1, 0), 3: (1, 1), 4: (1, 2), 5: (2, 2), grid: (3, 2)})
         counts = (len(args), len(moved), len(out_shape), 1, len(scratch))
         body = functools.partial(carry_kernel, body, plan, counts, schedule, grid)
         args += moved
@@ -824,7 +831,7 @@
             states = source[at, :].astype(f32) + nn(attended_ref[at, :], w_out_ref[...])
             states_two_ref[at, :] = states
             unit, _ = normal_form(states)
-            normed_ref[at, :] = low(unit * gains_ref[1:2, :])
+            normed_ref[at, :] = low(unit * gains_ref[1:2, :].astype(f32))
             forward_ref[at, :] = states
             backward_ref[at, :] = jnp.zeros_like(states)
 
@@ -846,7 +853,7 @@
 
     @pl.when(step == pl.num_programs(0) - 1)
     def _():
-        gain = gains_ref[1:2, :]
+        gain = gains_ref[1:2, :].astype(f32)
         grad_gain_ref[...] = jnp.zeros_like(grad_gain_ref)
 
         def chunk(at):
@@ -988,7 +995,7 @@
 
     @pl.when(step == pl.num_programs(0) - 1)
     def _():
-        gain = gains_ref[0:1, :]
+        gain = gains_ref[0:1, :].astype(f32)
         grad_gain_ref[...] = jnp.zeros_like(grad_gain_ref)
         if reads:
             (grad_query_ref, packed_sum_ref, delta_sum_ref) = refs
@@ -1040,7 +1047,7 @@
                 total += nt(grad_query, w_query_ref[...])
             sum_ref[at, :] = total
 
-        over_rows(rows, chunk)
+        over_rows(rows, chunk, False)
         grad_tokens_ref[...] = sum_ref[:seg_rows, :]
         grad_mem_ref[...] = sum_ref[seg_rows:, :]
         if reads:
@@ -1130,6 +1137,27 @@
 
 MESH = pl.DeviceIdType.MESH
 DEPTH, SIDE = 4, 2
+
+
+def events(*numbers):
+    return [divmod(number, 10) if number >= 0 else -1 - number for number in numbers]
+
+
+ARRIVE_ORDER = events(
+    0, 1, 10, 11, 20, 21, 2, 3, 30, 31, 12, 4, 13, 5, 22, 14, 23, 15, 32, 24, 6, 33, 25, 7, 34,
+    35, 16, 17, 26, 27, 36, 37
+)
+ARRIVE_STEPS = {0: (3, 1), 1: (0, 4), 2: (0, 5), 3: (1, 4), 4: (1, 5), 6: (0, 6), 8: (0, 7)}
+ARRIVE_STEPS.update({9: (3, 5), 10: (1, 7), 11: (2, 7), 12: (3, 6)})
+FINISH_ORDER = events(
+    0, 1, 10, 2, 11, 3, 20, 12, 4, 21, 13, 5, 30, 22, 14, 31, 23, 15, 6, 32, 24, 7, 33, 25, 8,
+    16, 34, 17, 35, 18, 26, 36, 27, 37, 28, 38
+)
+FINISH_STEPS = {1: (0, 1), 2: (0, 2), 3: (0, 3), 4: (0, 4), 5: (0, 5), 6: (1, 4)}
+FINISH_STEPS.update({7: (0, 6), 8: (0, 7), 9: (0, 8), 10: (3, 4), 11: (3, 5)})
+FINISH_TAIL = events(
+    -1, 18, 26, -2, 36, 27, -3, 37, 28, -4, 38
+)
 GRID = (DEPTH, SIDE, SIDE, SIDE)
 DEVICES = DEPTH * SIDE**3
 ORDERS = ("zxy", "zyx", "xyz", "yxz")
@@ -1197,11 +1225,33 @@
     return pieces
 
 
+def event_order(total, lanes):
+    order = []
+    for now in range(-(-total // lanes) + 3):
+        for lane in range(lanes):
+            for index in (3, 2, 1, 0):
+                group = (now - index) * lanes + lane
+                if now >= index and group < total:
+                    order.append((index, group))
+    return order
+
+
+def spread(order, last):
+    schedule = {}
+    done = 0
+    for step, event in last.items():
+        until = order.index(event) + 1
+        schedule[step] = tuple(range(done, until))
+        done = until
+    return schedule
+
+
 class Gather:
-    def __init__(self, groups, lead):
+    def __init__(self, groups, order, lead):
         self.groups = groups
         self.lead = lead
-        self.ticks = len(groups) + 3
+        self.order = order
+        self.ticks = len(self.order)
         self.numbers = {}
         for group, (_, pieces) in enumerate(groups):
             for piece in pieces:
@@ -1253,26 +1303,21 @@
             self.begin(0, group)
 
     def tick(self, now):
-        total = len(self.groups)
-        for index in (3, 2, 1, 0):
-            group = now - index
-            if not 0 <= group < total:
-                continue
-            for copy in self.copies(index, group):
-                copy.wait()
-            if index < 3:
-                self.begin(index + 1, group)
-            if index == 0 and group + self.lead < total:
-                self.begin(0, group + self.lead)
+        index, group = self.order[now]
+        for copy in self.copies(index, group):
+            copy.wait()
+        if index < 3:
+            self.begin(index + 1, group)
+        if index == 0 and group + self.lead < len(self.groups):
+            self.begin(0, group + self.lead)
 
 
 class Reduce:
-    def __init__(self, groups, shapes, ready=None):
+    def __init__(self, groups, shapes, order):
         self.groups = groups
         self.shapes = shapes
-        self.ready = ready or {}
-        self.ticks = len(groups) + 3
-        self.slots = 2
+        self.order = order
+        self.ticks = len(self.order)
         count = 0
         self.entries = []
         for *_, pieces, _ in groups:
@@ -1428,16 +1473,12 @@
                 self.totals[out][:, pl.ds(offset + start, size)] = total
 
     def tick(self, now):
-        total = len(self.groups)
-        for index in (3, 2, 1, 0):
-            group = now - index
-            if not 0 <= group < total:
-                continue
-            for copy in self.copies(index, group):
-                copy.wait()
-            self.add(index, group)
-            if index < 3:
-                self.begin(index + 1, group)
+        index, group = self.order[now]
+        for copy in self.copies(index, group):
+            copy.wait()
+        self.add(index, group)
+        if index < 3:
+            self.begin(index + 1, group)
 
 
 class SmallSum:
@@ -1531,16 +1572,47 @@
     return lambda body: pl.when(step == when)(body)
 
 
-def arrive_kernel(plan, seg_rows, schedule, *refs):
-    count = len(plan.groups)
+def slab_rows(values):
+    return low(values.astype(f32).reshape(-1, values.shape[-1]))
+
+
+def arrive_kernel(plan, seg_rows, schedule, hidden_size, *refs):
+    count = 5
     tokens_ref, mem_ref, gains_ref, *refs = refs
     shards, refs = refs[:count], refs[count:]
-    normed_ref, qkv_ref, attended_ref, log_ref, *refs = refs
+    (
+        normed_ref,
+        qkv_ref,
+        attended_ref,
+        log_ref,
+        out_ref,
+        mem_out_ref,
+        states_two_ref,
+        normed_two_ref,
+        upward_ref,
+        *refs,
+    ) = refs
     fulls, refs = refs[:count], refs[count:]
-    first_ref, w_ref, w_sem, *refs = refs
+    w_qkv_full, w_out_full, w_up_full, w_down_full, _ = fulls
+    (
+        first_ref,
+        w_ref,
+        w_out_slabs,
+        w_out_ref,
+        w_up_ref,
+        w_down_ref,
+        sum_ref,
+        w_sem,
+        up_sem,
+        down_sem,
+        *refs,
+    ) = refs
     plan.bind(shards, fulls, refs)
     parts, rows, width = qkv_ref.shape
+    pairs = width // PAIR
+    leave_at = parts + pairs
     step = pl.program_id(0)
+    chunk_now = step - leave_at
 
     @pl.when(step == 0)
     def _():
@@ -1549,7 +1621,7 @@
 
         def chunk(at):
             unit, _ = normal_form(first_ref[at, :].astype(f32))
-            normed_ref[at, :] = low(unit * gains_ref[0:1, :])
+            normed_ref[at, :] = low(unit * gains_ref[0:1, :].astype(f32))
 
         over_rows(rows, chunk)
 
@@ -1562,18 +1634,72 @@
 
     @pl.when(step == 0)
     def _():
-        copy = pltpu.make_async_copy(fulls[0], w_ref, w_sem)
+        copy = pltpu.make_async_copy(w_qkv_full, w_ref, w_sem)
         copy.start()
         copy.wait()
 
     @pl.when(step < parts)
     def _():
-        block = w_ref[..., at_chunk(step, width)].astype(f32).reshape(width, width)
-        qkv_ref[step] = low(nn(normed_ref[...], low(block)))
-
-    @pl.when(step >= parts)
-    def _():
-        attend_kernel(seg_rows, qkv_ref, attended_ref, log_ref, at_chunk(step - parts, PAIR))
+        block = slab_rows(w_ref[..., at_chunk(step, width)])
+        qkv_ref[step] = low(nn(normed_ref[...], block))
+
+    @pl.when((step >= parts) & (step < leave_at))
+    def _():
+        attend_kernel(
+            seg_rows, qkv_ref, attended_ref, log_ref, at_chunk(step - parts, PAIR), step - parts
+        )
+
+    def hidden_copies(index):
+        slot = lax.rem(index, 2)
+        return [
+            pltpu.make_async_copy(
+                w_up_full.at[..., at_chunk(index, hidden_size)], w_up_ref.at[slot], up_sem.at[slot]
+            ),
+            pltpu.make_async_copy(w_down_full.at[index], w_down_ref.at[slot], down_sem.at[slot]),
+        ]
+
+    @pl.when(step == leave_at)
+    def _():
+        copy = pltpu.make_async_copy(w_out_full, w_out_slabs, w_sem)
+        copy.start()
+        for other in hidden_copies(chunk_now):
+            other.start()
+        copy.wait()
+        w_out_ref[...] = slab_rows(w_out_slabs[...])
+
+        def chunk(at):
+            states = first_ref[at, :].astype(f32) + nn(attended_ref[at, :], w_out_ref[...])
+            states_two_ref[at, :] = states
+            unit, _ = normal_form(states)
+            normed_two_ref[at, :] = low(unit * gains_ref[1:2, :].astype(f32))
+            sum_ref[at, :] = states
+
+        over_rows(rows, chunk)
+
+    @pl.when(step >= leave_at)
+    def _():
+        for copy in hidden_copies(chunk_now):
+            copy.wait()
+
+        @pl.when(step + 1 < pl.num_programs(0))
+        def _():
+            for copy in hidden_copies(chunk_now + 1):
+                copy.start()
+
+        slot = lax.rem(chunk_now, 2)
+        upward = nn(normed_two_ref[...], slab_rows(w_up_ref[slot]))
+        upward_ref[...] = upward
+        bent = jnp.tanh(upward * (gelu_c + gelu_c * gelu_a * (upward * upward)))
+        active = low(upward * (0.5 + 0.5 * bent))
+        down = w_down_ref[slot]
+        sum_ref[...] += nn(active, down.reshape(hidden_size, width))
+
+    @pl.when(step == pl.num_programs(0) - 1)
+    def _():
+        out_ref[...] = low(sum_ref[:seg_rows, :])
+        mem_out_ref[...] = sum_ref[seg_rows:, :]
+        for now in range(sum(len(t) for t in schedule.values()), plan.ticks):
+            plan.tick(now)
 
 
 def arrive(tokens, mem_tokens, gains, shards, plan, schedule):
@@ -1582,25 +1708,25 @@
     rows = seg_rows + mems
     parts = shards[0].shape[1] // width
     pairs = width // PAIR
-    _, lanes = packed_lanes(rows, seg_rows)
-
-    def pair(step):
-        return jnp.maximum(step - parts, 0)
-
+    hidden = shards[2].shape[1]
+    size = hidden // DEPTH
+    lanes = packed_lanes(rows, seg_rows)[1]
+    tall = shards[3].shape[0]
+    segment = pl.BlockSpec((None, seg_rows, width), lambda j: (0, 0, 0), pipeline_mode=pl.Buffered(1))
     outs = pl.pallas_call(
-        functools.partial(arrive_kernel, plan, seg_rows, schedule),
-        grid=(parts + pairs,),
-        in_specs=[
-            pl.BlockSpec((None, seg_rows, width), lambda j: (0, 0, 0), pipeline_mode=pl.Buffered(1)),
+        functools.partial(arrive_kernel, plan, seg_rows, schedule, size),
+        grid=(parts + pairs + DEPTH,),
+        in_specs=[segment, whole((mems, width)), whole(gains.shape)] + [ANYWHERE] * len(shards),
+        out_specs=[
+            whole((rows, width)),
+            whole((parts, rows, width)),
+            whole((rows, width)),
+            whole((pairs, 1, lanes)),
+            segment,
             whole((mems, width)),
-            whole(gains.shape),
-        ]
-        + [ANYWHERE] * len(shards),
-        out_specs=[
-            result((rows, width)),
-            result((parts, rows, width)),
-            pl.BlockSpec((rows, PAIR), lambda j: (0, pair(j))),
-            pl.BlockSpec((1, 1, lanes), lambda j: (pair(j), 0, 0)),
+            whole((rows, width)),
+            whole((rows, width)),
+            pl.BlockSpec((rows, size), lambda j: (0, jnp.maximum(j - parts - pairs, 0))),
         ]
         + [ANYWHERE] * len(shards),
         out_shape=[
@@ -1608,18 +1734,30 @@
             shaped((parts, rows, width), low_type),
             shaped((rows, width), low_type),
             shaped((pairs, 1, lanes), f32),
+            shaped((slots, seg_rows, width), low_type),
+            shaped((mems, width), f32),
+            shaped((rows, width), f32),
+            shaped((rows, width), low_type),
+            shaped((rows, hidden), f32),
         ]
         + [shaped(GRID + shard.shape, low_type) for shard in shards],
         scratch_shapes=[
             pltpu.VMEM((rows, width), low_type),
             pltpu.VMEM(GRID + shards[0].shape, low_type),
+            pltpu.VMEM(GRID + shards[1].shape, low_type),
+            pltpu.VMEM((width, width), low_type),
+            pltpu.VMEM((2,) + GRID + (shards[2].shape[0], size), low_type),
+            pltpu.VMEM((2,) + GRID[1:] + (tall, width), low_type),
+            pltpu.VMEM((rows, width), f32),
             sems,
+            sems((2,)),
+            sems((2,)),
         ]
         + plan.scratch(),
         compiler_params=params(collective_id=0, has_side_effects=True),
         name="arrive",
     )(tokens, mem_tokens, gains, *shards)
-    return outs[:4], [flat(o) for o in outs[4:]]
+    return outs[:9], [flat(o) for o in outs[9:]]
 
 
 def carry_kernel(body, plan, counts, schedule, grid, *refs):
@@ -1734,7 +1872,7 @@
 
     @pl.when(step == pairs + 2 * parts - 1)
     def _():
-        gain = gains_ref[0:1, :]
+        gain = gains_ref[0:1, :].astype(f32)
         states_copy.wait()
         small_out_ref[...] = small_in_ref[...]
         mems = rows - seg_rows
@@ -1748,17 +1886,16 @@
         def chunk(at):
             back(tokens_ref[at, :].astype(f32), at)
 
-        over_rows(seg_rows, chunk)
+        over_rows(seg_rows, chunk, False)
         last = pl.ds(seg_rows, mems)
         back(mem_ref[...].astype(f32), last)
         small_out_ref[:mems, :] += first_ref[last, :]
         small.enter(small_out_ref[...])
-        rest = list(range(sum(len(t) for t in schedule.values()), plan.ticks))
-        for index in range(max(len(rest), small.ticks)):
-            if index < len(rest):
-                plan.tick(rest[index])
-            if index < small.ticks:
-                small.tick(index)
+        for event in FINISH_TAIL:
+            if isinstance(event, int):
+                small.tick(event)
+            else:
+                plan.tick(plan.order.index(event))
 
 
 def finish(
@@ -1861,18 +1998,24 @@
         out_specs=[pl.BlockSpec((None, size, width), lambda j: (0, j, 0))] + [result(s) for s in shapes],
         out_shape=[shaped(grad_tokens.shape, f32)] + [shaped(s, f32) for s in shapes],
         input_output_aliases={2 + len(sums): 0},
-        compiler_params=params(10),
+        compiler_params=params(),
         name="settle",
     )(first, small, *sums, grad_tokens)
 
 
 def fast_gather(shards):
-    shares = {2304: (8, 8, 1, 1), 768: (3, 3, 0, 0), 3072: (10, 10, 2, 2)}
     groups = []
     for a, shard in enumerate(shards):
         rows, cols = shard.shape
-        groups.append((a, cut(cols, (2, 2, 1, 1) if rows > 48 else shares.get(cols, (1, 1)))))
-    return Gather(groups, 1)
+        if cols < 2048:
+            bounds = [(0, cols, (2, 2, 1, 1) if rows > 48 else (1, 1))]
+        elif cols % 1024 == 256:
+            bounds = [(0, 1280, (4, 4, 1, 1)), (1280, cols - 1280, (1, 1))]
+        else:
+            bounds = [(0, cols // 2, (5, 5, 1, 1)), (cols // 2, cols // 2, (5, 5, 1, 1))]
+        for at, size, shares in bounds:
+            groups.append((a, [(order, at + start, n) for order, start, n in cut(size, shares)]))
+    return Gather(groups, ARRIVE_ORDER, 2)
 
 
 def on_device(
@@ -1880,16 +2023,15 @@
 ):
     slots, seg_rows, width = tokens.shape
     mems = mem_tokens.shape[0]
-    gains = gains.astype(f32)
-    w_beta = w_beta.astype(f32).reshape(1, width)
+    w_beta = w_beta.reshape(1, width)
     shards = [w_qkv, w_out, w_up, w_down, w_mem]
     if fast:
-        schedule = {0: (0, 1, 2, 3), 4: (4,), 6: (5,), 8: (6, 7)}
-        arrived, fulls = arrive(tokens, mem_tokens, gains, shards, fast_gather(shards), schedule)
+        plan = fast_gather(shards)
+        schedule = spread(plan.order, ARRIVE_STEPS)
+        arrived, fulls = arrive(tokens, mem_tokens, gains, shards, plan, schedule)
     else:
         fulls = gather_weights(shards)
     w_qkv, w_out, w_up, w_down, w_mem = fulls
-    same_item = jnp.where(item_ids[1:] == item_ids[:-1], 1.0, 0.0).astype(f32)
     kept_all = []
     written = [None] * (slots + 1)
     out = None
@@ -1897,7 +2039,9 @@
         kept = {}
         start = (tokens, mem_tokens)
         if fast and slot == 0:
-            kept["normed_one"], kept["qkv"], kept["attended"], kept["logs"] = arrived
+            names = ("normed_one", "qkv", "attended", "logs", "out", "mem_out", "states_two")
+            kept = dict(zip(names + ("normed_two", "upward"), arrived))
+            out, mem_out = kept["out"], kept["mem_out"]
         else:
             entered = enter_segment(slot, tokens, mem_tokens, gains, w_qkv, w_mem, written[slot])
             kept["normed_one"], kept["qkv"] = entered[:2]
@@ -1908,12 +2052,13 @@
         if slot + 1 == slots:
             both = leave_both(slot, start, kept["attended"], out_grad, gains, w_out, w_up, w_down, out, f32)
             out = both["block_out"]
-        else:
+        elif not fast:
             out, mem_out, kept["states_two"], kept["normed_two"], kept["upward"] = leave_segment(
                 slot, slots, seg_rows, start, kept["attended"], gains, w_out, w_up, w_down, out
             )
             kept["mem_out"] = mem_out
-            written[slot + 1] = write_memory(same_item[slot : slot + 1], mem_out, w_mem, w_beta)
+        if slot + 1 < slots:
+            written[slot + 1] = write_memory(slot, item_ids, mem_out, w_mem, w_beta)
         kept_all.append(kept)
 
     sums = None
@@ -1932,7 +2077,7 @@
         mem_plan = None
         if slot + 1 < slots:
             grad_rows, w_pair_sum, grad_beta_part = write_back(
-                same_item[slot : slot + 1], kept["mem_out"], w_mem, w_beta, written[slot + 1], *pulled
+                slot, item_ids, kept["mem_out"], w_mem, w_beta, written[slot + 1], *pulled
             )
             grad_beta += grad_beta_part
             if fast and last:
@@ -1972,15 +2117,14 @@
         small = jnp.pad(small, ((0, -small.shape[0] % 8), (0, 0)))
         partials = [slabs(down_sum), slabs(up_sum), slabs(out_sum)]
         shapes = [p.shape[-2:] for p in partials] + [(width // DEVICES, w_qkv.shape[1])]
-        half = shapes[1][1] // 2
-        groups = [(0, 0, width, 0, 0, cut(width, (1, 1)), False)]
-        groups += [(1, at, half, 1, at, cut(half, (1, 1)), False) for at in (0, half)]
-        groups += [(2, 0, width, 2, 0, cut(width, (1, 1)), False)]
-        groups += [
-            (3, at, width, 3, at, cut(width, (1, 1)), True) for at in range(0, shapes[3][1], width)
-        ]
-        plan = Reduce(groups, shapes)
-        schedule = {1: (0,), 4: (1,), 6: (2,), 9: (3,)}
+        third = shapes[1][1] // 3
+        places = [(0, 0, 256), (0, 256, width - 256)]
+        places += [(1, at, third) for at in range(0, shapes[1][1], third)]
+        places += [(2, 0, width)]
+        places += [(3, at, width) for at in range(0, shapes[3][1], width)]
+        groups = [(a, at, size, a, at, cut(size, (1, 1)), a == 3) for a, at, size in places]
+        plan = Reduce(groups, shapes, FINISH_ORDER)
+        schedule = spread(plan.order, FINISH_STEPS)
         first, (down_total, up_total, out_total, qkv_total), small = finish(
             tokens,
             mem_tokens,

time: 458 us -> 440 us (0.961)
  Pallas kernels: 424 us -> 411 us
  local copies, waits for them, and re-layouts: 21.1 us -> 15.6 us
    pallas_call x4 -> x3, Pallas kernels: 123 us -> 117 us  [the longest x1 114 us: arrive(): pl.pallas_call(functools.partial(arrive_kernel, plan, seg_rows, schedule,...]
    unnamed x66 -> x55, local copies, waits for them, and re-layouts: 19 us -> 14.9 us
where the time goes in v5:
time: 440 us; the launch traced here: 431 us
  Pallas kernels  411 us (93%)
  local copies, waits for them, and re-layouts  15.6 us (4%)
    pallas_call x1, Pallas kernels, arrive(): pl.pallas_call(functools.partial(arrive_kernel, plan, seg_rows, schedule,...  114 us
    pallas_call x1, Pallas kernels, finish(): pl.pallas_call(functools.partial(finish_kernel, plan, small, seg_rows, sc...  93.7 us
    pallas_call x1, Pallas kernels, leave_back(): pl.pallas_call(body, grid=(hidden // size,), in_specs=in_specs, out_specs...  51.4 us
    pallas_call x1, Pallas kernels, leave_both(): pl.pallas_call(functools.partial(leave_both_kernel, reads, earlier is not...  49.4 us
    pallas_call x1, Pallas kernels, attend_back(): pl.pallas_call(functools.partial(attend_back_kernel, seg_rows), grid=(pai...  33.4 us
    pallas_call x1, Pallas kernels, enter_back(): pl.pallas_call(functools.partial(enter_back_kernel, reads, w_sum is not N...  29.4 us
    pallas_call x1, Pallas kernels, attend(): pl.pallas_call(functools.partial(attend_kernel, seg_rows), grid=(pairs,),...  20.4 us
    unnamed x55, local copies, waits for them, and re-layouts  14.9 us

profile of v5, /device:TPU:0, one launch (start us, length us, event | category | flops | bytes accessed | tf_op | source)
XLA Modules:
  0.0 430.9 jit_solution(16158157768333385694)
XLA Ops:
  0.6 0.0 copy-start.9
  0.7 0.7 reshape.58.w_beta_ref
  1.3 114.0 %arrive.1 = (bf16[1040,768]{1,0:T(8,128)(2,1)}, bf16[3,1040,768]{2,1,0:T(8,128)(2,1)}, bf16[1040,768]{1,0:T(8,128)(2,1)}, f32[6,1,2176]{2,1,0:T(1,128)}, bf16[2,...) custom-call(bf16[2,1024,768]{2,1,0:T(8,128)(2,1)} %refs_4_.3, ...), custom_call_target="tpu_custom_call" | custom-call | tf_op jit(solution)/shard_map/arrive/pallas_call | solution.py:1716
  115.4 0.0 copy-done.9
  115.4 0.0 copy-start
  115.4 2.0 copy-done
  117.4 0.8 copy-done.5
  118.2 1.0 write.1
  119.2 1.0 copy-done.1
  120.2 1.0 copy-done.3
  121.2 0.0 copy-done.7
  121.2 0.0 copy-done.8
  121.2 2.0 copy-done.4
  123.2 11.3 %enter_read.1 = (bf16[1040,768]{1,0:T(8,128)(2,1)S(1)}, bf16[3,1040,768]{2,1,0:T(8,128)(2,1)S(1)}, f32[1040,768]{1,0:T(8,128)S(1)}, f32[1040,768]{1,0:T(8,128)S(1)}, f32[1040,16]{1,0:T(8,128)S(1)}) custom-call(bf16[2,1024,768]{2,1,0:T(8,128)(2,1)S(1)} %copy-done.3, bf16[16,768]{1,0:T(8,128)(2,1)S(1)} %copy-done.7, bf16[2,768]{1,0:T(2,128)(2,1)S(1)} %copy-done.8, ...), custom_call_target="tpu_custom_call" | custom-call | flops 4907335680 | bytes 20971520 | tf_op jit(solution)/shard_map/enter_read/pallas_call | solution.py:206
  134.4 0.0 copy-start.24
  134.5 1.1 copy-done.24
  135.6 20.4 %attend.1 = (bf16[1040,768]{1,0:T(8,128)(2,1)S(1)}, f32[6,1,2176]{2,1,0:T(1,128)S(1)}) custom-call(bf16[3,1040,768]{2,1,0:T(8,128)(2,1)S(1)} %get-tuple-element.84.qkv_ref), custom_call_target="tpu_custom_call" | custom-call | flops 3322675200 | bytes 7340032 | tf_op jit(solution)/shard_map/attend/pallas_call | solution.py:283
  156.1 0.0 copy-done.14
  156.1 0.0 copy-done.17
  156.1 0.0 copy-done.19
  156.1 0.0 copy-start.22
  156.1 1.1 copy-done.22
  157.2 0.0 copy-done.11
  157.2 49.4 %leave_both.1 = (bf16[2,1024,768]{2,1,0:T(8,128)(2,1)}, f32[1040,768]{1,0:T(8,128)}, bf16[1040,768]{1,0:T(8,128)(2,1)S(1)}, f32[768,3072]{1,0:T(8,128)}, f32[307...) custom-call(f32[1040,768]{1,0:T(8,128)} %copy-done.17, ...), custom_call_target="tpu_custom_call", output_to_operand_aliasing={{0}: (7, {})} | custom-call | flops 33124515840 | bytes 62914560 | tf_op jit(solution)/shard_map/leave_both/pallas_call | solution.py:924
  206.6 0.0 copy-done.15
  206.6 0.0 copy-done.23
  206.6 0.0 copy-start.18
  206.7 0.0 copy-start.20
  206.7 0.0 copy-start.21
  206.7 0.0 copy-start.25
  206.7 33.4 %attend_back.1.refs_3_ = bf16[3,1040,768]{2,1,0:T(8,128)(2,1)S(1)} custom-call(bf16[3,1040,768]{2,1,0:T(8,128)(2,1)S(1)} %copy-done.15, bf16[1040,768]{1,0:T(8,128)(2,1)S(1)} %get-tuple-element.95.grad_ref, bf16[1040,768]{1,0:T(8,128)(2,1)S(1)} %copy-done.23, f32[6,1,2176]{2,1,0:T(1,128)S(1)} %get-tuple-element.96.log_ref), custom_call_target="tpu_custom_call" | custom-call | flops 8306688000 | bytes 13631488 | tf_op jit(solution)/shard_map/attend_back/pallas_call | solution.py:357
  240.1 0.0 copy-start.16
  240.1 2.2 copy-done.16
  242.3 0.0 copy-done.18
  242.3 0.0 copy-done.20
  242.3 0.0 copy-done.21
  242.3 29.4 %enter_back.1 = (f32[2,1024,768]{2,1,0:T(8,128)}, f32[16,768]{1,0:T(8,128)S(1)}, f32[768,2304]{1,0:T(8,128)}, f32[1,768]{1,0:T(1,128)S(1)}, bf16[768,768]{1,0:T(...) custom-call(bf16[2,1024,768]{2,1,0:T(8,128)(2,1)S(1)} %copy-done.3, ...), custom_call_target="tpu_custom_call" | custom-call | flops 9814671360 | bytes 31457280 | tf_op jit(solution)/shard_map/enter_back/pallas_call | solution.py:1122
  271.8 2.0 write_back.1
  273.8 1.4 copy-done.10
  275.2 0.6 copy-done.12
  275.8 51.4 %leave_back.1 = (f32[1040,768]{1,0:T(8,128)}, bf16[1040,768]{1,0:T(8,128)(2,1)}, bf16[768,3072]{1,0:T(8,128)(2,1)}, bf16[3072,768]{1,0:T(8,128)(2,1)}, bf16[768,...) custom-call(bf16[2,1024,768]{2,1,0:T(8,128)(2,1)} %refs_0_.5, f32[16,768]{1,0:T(8,128)} %copy-done.12, ...), custom_call_target="tpu_custom_call" | custom-call | flops 22083010560 | bytes 62914560 | tf_op jit(solution)/shard_map/leave_back/pallas_call | solution.py:780
  327.2 0.7 add.5
  327.9 0.6 select_maximum_fusion.refs_10_
  328.6 93.7 %finish.1 = (f32[1040,768]{1,0:T(8,128)}, f32[96,768]{1,0:T(8,128)}, f32[24,3072]{1,0:T(8,128)}, f32[24,768]{1,0:T(8,128)}, f32[24,2304]{1,0:T(8,128)}, /*index=5*/f32[24,768]{1,0:T(8,128)}) custom-call(bf16[3,1040,768]{2,1,0:T(8,128)(2,1)} %get-tuple-element.91.refs_0_, bf16[1040,768]{1,0:T(8,128)(2,1)} %get-tuple-element.114.refs_1_, ...), custom_call_target="tpu_custom_call" | custom-call | tf_op jit(solution)/shard_map/finish/pallas_call | solution.py:1920
  422.3 5.2 %settle.1 = (f32[2,1024,768]{2,1,0:T(8,128)}, f32[16,768]{1,0:T(8,128)}, f32[2,768]{1,0:T(2,128)}, f32[1,768]{1,0:T(1,128)}, f32[24,2304]{1,0:T(8,128)}, /*index...) custom-call(f32[1040,768]{1,0:T(8,128)} %get-tuple-element.127.first, ...), custom_call_target="tpu_custom_call", output_to_operand_aliasing={{0}: (7, {})} | custom-call | tf_op jit(solution)/shard_map/settle/pallas_call | solution.py:1992
  427.5 1.3 reduce
  428.8 0.0 copy-done.26
  428.8 1.7 copy.26
  (22 shorter events, 0.0 us)
Async XLA Ops:
  0.6 114.7 %copy-start.9 = (s32[2]{0:T(128)S(1)}, s32[2]{0:T(128)}, u32[]{:S(2)}) copy-start(s32[2]{0:T(128)} %flag_ref.3) | copy-start | bytes 28
  115.4 2.0 copy-start
  117.4 0.8 copy-start.5
  118.2 2.0 copy-start.1
  118.2 3.0 copy-start.3
  118.2 3.0 copy-start.7
  118.2 3.0 copy-start.8
  121.2 2.0 copy-start.4
  134.4 1.2 copy-start.24
  135.6 20.5 %copy-start.14 = (bf16[3,1040,768]{2,1,0:T(8,128)(2,1)}, bf16[3,1040,768]{2,1,0:T(8,128)(2,1)S(1)}, u32[]{:S(2)}) copy-start(bf16[3,1040,768]{2,1,0:T(8,128)(2,1)S(1)} %get-tuple-element.84.qkv_ref) | copy-start | bytes 14376964
  135.6 20.5 %copy-start.17 = (f32[1040,768]{1,0:T(8,128)}, f32[1040,768]{1,0:T(8,128)S(1)}, u32[]{:S(2)}) copy-start(f32[1040,768]{1,0:T(8,128)S(1)} %get-tuple-element.83.refs_0_.refs_7_) | copy-start | bytes 9584644
  135.6 20.5 %copy-start.19 = (f32[1040,768]{1,0:T(8,128)}, f32[1040,768]{1,0:T(8,128)S(1)}, u32[]{:S(2)}) copy-start(f32[1040,768]{1,0:T(8,128)S(1)} %get-tuple-element.98.refs_8_) | copy-start | bytes 9584644
  135.6 21.6 %copy-start.11 = (bf16[4,2,2,2,24,768]{5,4,3,2,1,0:T(8,128)(2,1)S(1)}, bf16[4,2,2,2,24,768]{5,4,3,2,1,0:T(8,128)(2,1)}, u32[]{:S(2)}) copy-start(bf16[4,2,2,2,24,768]{5,4,3,2,1,0:T(8,128)(2,1)} %get-tuple-element.86) | copy-start | bytes 3538948
  156.1 1.1 copy-start.22
  157.2 49.4 %copy-start.15 = (bf16[3,1040,768]{2,1,0:T(8,128)(2,1)S(1)}, bf16[3,1040,768]{2,1,0:T(8,128)(2,1)}, u32[]{:S(2)}) copy-start(bf16[3,1040,768]{2,1,0:T(8,128)(2,1)} %copy-done.14) | copy-start | bytes 14376964
  157.2 49.4 %copy-start.23 = (bf16[1040,768]{1,0:T(8,128)(2,1)S(1)}, bf16[1040,768]{1,0:T(8,128)(2,1)}, u32[]{:S(2)}) copy-start(bf16[1040,768]{1,0:T(8,128)(2,1)} %copy-done.22) | copy-start | bytes 4792324
  206.6 35.7 %copy-start.18 = (f32[1040,768]{1,0:T(8,128)S(1)}, f32[1040,768]{1,0:T(8,128)}, u32[]{:S(2)}) copy-start(f32[1040,768]{1,0:T(8,128)} %copy-done.17) | copy-start | bytes 9584644
  206.7 35.7 %copy-start.20 = (f32[1040,768]{1,0:T(8,128)S(1)}, f32[1040,768]{1,0:T(8,128)}, u32[]{:S(2)}) copy-start(f32[1040,768]{1,0:T(8,128)} %copy-done.19) | copy-start | bytes 9584644
  206.7 35.7 %copy-start.21 = (f32[1040,768]{1,0:T(8,128)S(1)}, f32[1040,768]{1,0:T(8,128)}, u32[]{:S(2)}) copy-start(f32[1040,768]{1,0:T(8,128)} %get-tuple-element.97.refs_4_) | copy-start | bytes 9584644
  206.7 35.6 %copy-start.25 = (bf16[1040,768]{1,0:T(8,128)(2,1)S(1)}, bf16[1040,768]{1,0:T(8,128)(2,1)}, u32[]{:S(2)}) copy-start(bf16[1040,768]{1,0:T(8,128)(2,1)} %copy-done.24) | copy-start | bytes 4792324
  240.1 2.2 copy-start.16
  242.3 29.4 %copy-start.2 = (bf16[4,2,2,2,24,2304]{5,4,3,2,1,0:T(8,128)(2,1)S(1)}, bf16[4,2,2,2,24,2304]{5,4,3,2,1,0:T(8,128)(2,1)}, u32[]{:S(2)}) copy-start(bf16[4,2,2,2,24,2304]{5,4,3,2,1,0:T(8,128)(2,1)} %get-tuple-element.78) | copy-start | bytes 10616836
  242.3 29.4 %copy-start.6 = (f32[16,768]{1,0:T(8,128)S(1)}, f32[16,768]{1,0:T(8,128)}, u32[]{:S(2)}) copy-start(f32[16,768]{1,0:T(8,128)} %get-tuple-element.79.mem_out_ref) | copy-start | bytes 147460
  271.7 2.1 copy-start.13
  273.8 1.4 copy-start.10
  275.2 0.6 copy-start.12
  422.3 6.5 %copy-start.26 = (bf16[2,1024,768]{2,1,0:T(8,128)(2,1)S(1)}, bf16[2,1024,768]{2,1,0:T(8,128)(2,1)}, u32[]{:S(2)}) copy-start(bf16[2,1024,768]{2,1,0:T(8,128)(2,1)} %get-tuple-element.154) | copy-start | bytes 9437188

commit v6 on v5

--- a/solution.py
+++ b/solution.py
@@ -792,14 +792,14 @@
     )(*args)
 
 
-def leave_both_kernel(reads, adds, *refs):
+def leave_both_kernel(reads, adds, slot, *refs):
     if reads:
         (states_one_ref, *refs) = refs
     else:
         (tokens_ref, mem_ref, *refs) = refs
     (attended_ref, out_grad_ref, gains_ref, w_out_ref, w_up_ref, w_down_ref, *refs) = refs
     if adds:
-        refs = refs[1:]
+        (earlier_ref, *refs) = refs
     (
         out_ref,
         grad_states_ref,
@@ -817,10 +817,20 @@
     ) = refs
     rows, width = attended_ref.shape
     seg_rows = out_grad_ref.shape[0]
+    copies = []
+    if adds == "rows":
+        both_ref = out_ref
+        out_ref, first_sem, last_sem, *scratch = scratch
+        copies = [
+            pltpu.make_async_copy(earlier_ref, both_ref.at[0], first_sem),
+            pltpu.make_async_copy(out_ref, both_ref.at[slot], last_sem),
+        ]
     step = pl.program_id(0)
 
     @pl.when(step == 0)
     def _():
+        if copies:
+            copies[0].start()
         if not reads:
             load_first(tokens_ref, mem_ref, scratch[0])
         grad_low_ref[:seg_rows, :] = out_grad_ref[...]
@@ -870,6 +880,10 @@
         grad_out = tn(attended_ref[...], normed_ref[...])
         grad_out_ref[...] = grad_out.astype(grad_out_ref.dtype)
         out_ref[...] = low(forward_ref[:seg_rows, :])
+        if copies:
+            copies[1].start()
+            copies[0].wait()
+            copies[1].wait()
 
 
 def gelu_parts(upward):
@@ -917,16 +931,22 @@
         down_spec,
     ]
     aliases = {}
+    adds = earlier is not None
+    if adds and earlier.ndim == 2:
+        adds = "rows"
     if earlier is not None:
         args.append(earlier)
-        in_specs.append(ANYWHERE)
-        aliases = {len(args) - 1: 0}
+        in_specs.append(whole(earlier.shape) if adds == "rows" else ANYWHERE)
+        aliases = {} if adds == "rows" else {len(args) - 1: 0}
+        if adds == "rows":
+            place = 5 if reads else 6
+            scratch[place:place] = [pltpu.VMEM((seg_rows, width), low_type), sems, sems]
     outs = pl.pallas_call(
-        functools.partial(leave_both_kernel, reads, earlier is not None),
+        functools.partial(leave_both_kernel, reads, adds, slot),
         grid=(hidden // size,),
         in_specs=in_specs,
         out_specs=[
-            segment,
+            ANYWHERE if adds == "rows" else segment,
             whole((rows, width)),
             whole((rows, width)),
             up_spec,
@@ -1156,7 +1176,7 @@
 FINISH_STEPS = {1: (0, 1), 2: (0, 2), 3: (0, 3), 4: (0, 4), 5: (0, 5), 6: (1, 4)}
 FINISH_STEPS.update({7: (0, 6), 8: (0, 7), 9: (0, 8), 10: (3, 4), 11: (3, 5)})
 FINISH_TAIL = events(
-    -1, 18, 26, -2, 36, 27, -3, 37, 28, -4, 38
+    18, 26, -1, 36, 27, -2, 37, 28, -3, 38, -4
 )
 GRID = (DEPTH, SIDE, SIDE, SIDE)
 DEVICES = DEPTH * SIDE**3
@@ -1716,13 +1736,14 @@
     outs = pl.pallas_call(
         functools.partial(arrive_kernel, plan, seg_rows, schedule, size),
         grid=(parts + pairs + DEPTH,),
-        in_specs=[segment, whole((mems, width)), whole(gains.shape)] + [ANYWHERE] * len(shards),
+        in_specs=[segment, whole((mems, width)), whole(gains.shape)]
+        + [whole(shard.shape) for shard in shards],
         out_specs=[
             whole((rows, width)),
             whole((parts, rows, width)),
             whole((rows, width)),
             whole((pairs, 1, lanes)),
-            segment,
+            whole((seg_rows, width)),
             whole((mems, width)),
             whole((rows, width)),
             whole((rows, width)),
@@ -1734,7 +1755,7 @@
             shaped((parts, rows, width), low_type),
             shaped((rows, width), low_type),
             shaped((pairs, 1, lanes), f32),
-            shaped((slots, seg_rows, width), low_type),
+            shaped((seg_rows, width), low_type),
             shaped((mems, width), f32),
             shaped((rows, width), f32),
             shaped((rows, width), low_type),
@@ -1980,7 +2001,7 @@
         mems = mem_ref.shape[0]
         mem_ref[...] = small_ref[:mems, :]
         gains_ref[...] = small_ref[mems : mems + 2, :]
-        beta_ref[...] = small_ref[mems + 2 : mems + 3, :]
+        beta_ref[...] = small_ref[mems + 2, :]
         for source, target in zip(sums, outs):
             target[...] = source[...]
 
@@ -1988,7 +2009,7 @@
 def settle(first, small, sums, grad_tokens, mems):
     slots, seg_rows, width = grad_tokens.shape
     size = 256
-    shapes = [(mems, width), (2, width), (1, width)] + [s.shape for s in sums]
+    shapes = [(mems, width), (2, width), (width,)] + [s.shape for s in sums]
     return pl.pallas_call(
         functools.partial(settle_kernel, len(sums)),
         grid=(seg_rows // size,),
@@ -2144,7 +2165,7 @@
         grad_tokens, grad_mem_tokens, grad_gains, grad_beta, *totals = settle(
             first, small, totals, grad_tokens, mems
         )
-        return (out, grad_tokens, *totals, grad_mem_tokens, grad_gains, grad_beta.reshape(width))
+        return (out, grad_tokens, *totals, grad_mem_tokens, grad_gains, grad_beta)
     mem_sum = jnp.concatenate([w_query_sum, w_pair_sum], axis=1)
     grad_gains = jnp.concatenate([gain_one_sum, gain_two_sum], axis=0)
     summed = scatter_sums([mem_sum, qkv_sum, sums["out"], sums["up"], sums["down"]])

time: 440 us -> 437 us (level)
    unnamed x55 -> x56, local copies, waits for them, and re-layouts: 14.9 us -> 14.7 us
where the time goes in v6:
time: 437 us; the launch traced here: 428 us
  Pallas kernels  410 us (94%)
  local copies, waits for them, and re-layouts  15.4 us (4%)
    pallas_call x1, Pallas kernels, arrive(): pl.pallas_call(functools.partial(arrive_kernel, plan, seg_rows, schedule,...  114 us
    pallas_call x1, Pallas kernels, finish(): pl.pallas_call(functools.partial(finish_kernel, plan, small, seg_rows, sc...  91.7 us
    pallas_call x1, Pallas kernels, leave_back(): pl.pallas_call(body, grid=(hidden // size,), in_specs=in_specs, out_specs...  51 us
    pallas_call x1, Pallas kernels, leave_both(): pl.pallas_call(functools.partial(leave_both_kernel, reads, adds, slot), g...  50.7 us
    pallas_call x1, Pallas kernels, attend_back(): pl.pallas_call(functools.partial(attend_back_kernel, seg_rows), grid=(pai...  33.4 us
    pallas_call x1, Pallas kernels, enter_back(): pl.pallas_call(functools.partial(enter_back_kernel, reads, w_sum is not N...  29.4 us
    pallas_call x1, Pallas kernels, attend(): pl.pallas_call(functools.partial(attend_kernel, seg_rows), grid=(pairs,),...  20.4 us
    unnamed x56, local copies, waits for them, and re-layouts  14.7 us

profile of v6, /device:TPU:0, one launch (start us, length us, event | category | flops | bytes accessed | tf_op | source)
XLA Modules:
  0.0 428.3 jit_solution(11303045567386830803)
XLA Ops:
  0.6 0.0 copy-start.9
  0.7 0.7 reshape.55.w_beta_ref
  1.3 114.3 %arrive.1 = (bf16[1040,768]{1,0:T(8,128)(2,1)}, bf16[3,1040,768]{2,1,0:T(8,128)(2,1)}, bf16[1040,768]{1,0:T(8,128)(2,1)}, f32[6,1,2176]{2,1,0:T(1,128)}, bf16[10...) custom-call(bf16[2,1024,768]{2,1,0:T(8,128)(2,1)} %refs_4_.3, ...), custom_call_target="tpu_custom_call" | custom-call | tf_op jit(solution)/shard_map/arrive/pallas_call | solution.py:1736
  115.6 0.0 copy-done.9
  115.6 0.0 copy-start
  115.6 2.0 copy-done
  117.6 0.8 copy-done.5
  118.4 1.0 write.1
  119.5 1.0 copy-done.1
  120.4 1.0 copy-done.3
  121.4 0.0 copy-done.7
  121.4 0.0 copy-done.8
  121.4 2.0 copy-done.4
  123.4 11.3 %enter_read.1 = (bf16[1040,768]{1,0:T(8,128)(2,1)S(1)}, bf16[3,1040,768]{2,1,0:T(8,128)(2,1)S(1)}, f32[1040,768]{1,0:T(8,128)S(1)}, f32[1040,768]{1,0:T(8,128)S(1)}, f32[1040,16]{1,0:T(8,128)S(1)}) custom-call(bf16[2,1024,768]{2,1,0:T(8,128)(2,1)S(1)} %copy-done.3, bf16[16,768]{1,0:T(8,128)(2,1)S(1)} %copy-done.7, bf16[2,768]{1,0:T(2,128)(2,1)S(1)} %copy-done.8, ...), custom_call_target="tpu_custom_call" | custom-call | flops 4907335680 | bytes 20971520 | tf_op jit(solution)/shard_map/enter_read/pallas_call | solution.py:206
  134.7 0.0 copy-start.25
  134.7 1.1 copy-done.25
  135.8 0.0 copy-start.12
  135.9 20.4 %attend.1 = (bf16[1040,768]{1,0:T(8,128)(2,1)S(1)}, f32[6,1,2176]{2,1,0:T(1,128)S(1)}) custom-call(bf16[3,1040,768]{2,1,0:T(8,128)(2,1)S(1)} %get-tuple-element.84.qkv_ref), custom_call_target="tpu_custom_call" | custom-call | flops 3322675200 | bytes 7340032 | tf_op jit(solution)/shard_map/attend/pallas_call | solution.py:283
  156.3 0.0 copy-done.15
  156.3 0.0 copy-done.18
  156.3 0.0 copy-done.20
  156.3 0.0 copy-start.23
  156.3 1.2 copy-done.23
  157.6 0.0 copy-done.11
  157.6 0.0 copy-done.12
  157.6 50.7 %leave_both.1 = (bf16[2,1024,768]{2,1,0:T(8,128)(2,1)}, f32[1040,768]{1,0:T(8,128)}, bf16[1040,768]{1,0:T(8,128)(2,1)}, f32[768,3072]{1,0:T(8,128)}, f32[3072,76...) custom-call(f32[1040,768]{1,0:T(8,128)} %copy-done.18, bf16[1040,768]{1,0:T(8,128)(2,1)} %copy-done.23, ...), custom_call_target="tpu_custom_call" | custom-call | flops 33124515840 | bytes 62914560 | tf_op jit(solution)/shard_map/leave_both/pallas_call | solution.py:944
  208.2 0.0 copy-done.16
  208.2 0.0 copy-done.24
  208.3 0.0 copy-start.27
  208.3 1.4 copy-done.27
  209.7 33.4 %attend_back.1.refs_3_ = bf16[3,1040,768]{2,1,0:T(8,128)(2,1)S(1)} custom-call(bf16[3,1040,768]{2,1,0:T(8,128)(2,1)S(1)} %copy-done.16, bf16[1040,768]{1,0:T(8,128)(2,1)S(1)} %copy-done.27, bf16[1040,768]{1,0:T(8,128)(2,1)S(1)} %copy-done.24, f32[6,1,2176]{2,1,0:T(1,128)S(1)} %get-tuple-element.96.log_ref), custom_call_target="tpu_custom_call" | custom-call | flops 8306688000 | bytes 13631488 | tf_op jit(solution)/shard_map/attend_back/pallas_call | solution.py:357
  243.1 0.0 copy-start.17
  243.1 2.1 copy-done.17
  245.2 0.0 copy-done.19
  245.2 0.0 copy-done.21
  245.2 0.0 copy-done.22
  245.2 0.0 copy-done.26
  245.2 0.0 copy-start.2
  245.2 0.0 copy-start.6
  245.3 29.4 %enter_back.1 = (f32[2,1024,768]{2,1,0:T(8,128)}, f32[16,768]{1,0:T(8,128)S(1)}, f32[768,2304]{1,0:T(8,128)}, f32[1,768]{1,0:T(1,128)S(1)}, bf16[768,768]{1,0:T(...) custom-call(bf16[2,1024,768]{2,1,0:T(8,128)(2,1)S(1)} %copy-done.3, ...), custom_call_target="tpu_custom_call" | custom-call | flops 9814671360 | bytes 31457280 | tf_op jit(solution)/shard_map/enter_back/pallas_call | solution.py:1142
  274.6 2.0 write_back.1
  276.7 1.4 copy-done.10
  278.1 0.6 copy-done.13
  278.7 51.0 %leave_back.1 = (f32[1040,768]{1,0:T(8,128)}, bf16[1040,768]{1,0:T(8,128)(2,1)}, bf16[768,3072]{1,0:T(8,128)(2,1)}, bf16[3072,768]{1,0:T(8,128)(2,1)}, bf16[768,...) custom-call(bf16[2,1024,768]{2,1,0:T(8,128)(2,1)} %refs_0_.5, f32[16,768]{1,0:T(8,128)} %copy-done.13, ...), custom_call_target="tpu_custom_call" | custom-call | flops 22083010560 | bytes 62914560 | tf_op jit(solution)/shard_map/leave_back/pallas_call | solution.py:780
  329.7 0.7 add.5
  330.4 0.6 select_maximum_fusion.refs_10_
  331.1 91.7 %finish.1 = (f32[1040,768]{1,0:T(8,128)}, f32[96,768]{1,0:T(8,128)}, f32[24,3072]{1,0:T(8,128)}, f32[24,768]{1,0:T(8,128)}, f32[24,2304]{1,0:T(8,128)}, /*index=5*/f32[24,768]{1,0:T(8,128)}) custom-call(bf16[3,1040,768]{2,1,0:T(8,128)(2,1)} %get-tuple-element.91.refs_0_, bf16[1040,768]{1,0:T(8,128)(2,1)} %get-tuple-element.114.refs_1_, ...), custom_call_target="tpu_custom_call" | custom-call | tf_op jit(solution)/shard_map/finish/pallas_call | solution.py:1941
  422.8 5.0 %settle.1 = (f32[2,1024,768]{2,1,0:T(8,128)}, f32[16,768]{1,0:T(8,128)}, f32[2,768]{1,0:T(2,128)}, f32[768]{0:T(1024)}, f32[24,2304]{1,0:T(8,128)}, /*index=5*/f...) custom-call(f32[1040,768]{1,0:T(8,128)} %get-tuple-element.127.first, ...), custom_call_target="tpu_custom_call", output_to_operand_aliasing={{0}: (7, {})} | custom-call | tf_op jit(solution)/shard_map/settle/pallas_call | solution.py:2013
  (22 shorter events, 0.0 us)
Async XLA Ops:
  0.6 115.0 %copy-start.9 = (s32[2]{0:T(128)S(1)}, s32[2]{0:T(128)}, u32[]{:S(2)}) copy-start(s32[2]{0:T(128)} %flag_ref.3) | copy-start | bytes 28
  115.6 2.0 copy-start
  117.6 0.8 copy-start.5
  118.4 2.0 copy-start.1
  118.4 3.0 copy-start.3
  118.4 3.0 copy-start.7
  118.4 3.0 copy-start.8
  121.4 2.0 copy-start.4
  134.7 1.1 copy-start.25
  135.8 20.5 %copy-start.15 = (bf16[3,1040,768]{2,1,0:T(8,128)(2,1)}, bf16[3,1040,768]{2,1,0:T(8,128)(2,1)S(1)}, u32[]{:S(2)}) copy-start(bf16[3,1040,768]{2,1,0:T(8,128)(2,1)S(1)} %get-tuple-element.84.qkv_ref) | copy-start | bytes 14376964
  135.8 20.5 %copy-start.18 = (f32[1040,768]{1,0:T(8,128)}, f32[1040,768]{1,0:T(8,128)S(1)}, u32[]{:S(2)}) copy-start(f32[1040,768]{1,0:T(8,128)S(1)} %get-tuple-element.83.refs_0_.refs_7_) | copy-start | bytes 9584644
  135.8 20.5 %copy-start.20 = (f32[1040,768]{1,0:T(8,128)}, f32[1040,768]{1,0:T(8,128)S(1)}, u32[]{:S(2)}) copy-start(f32[1040,768]{1,0:T(8,128)S(1)} %get-tuple-element.98.refs_8_) | copy-start | bytes 9584644
  135.8 21.7 %copy-start.11 = (bf16[1024,768]{1,0:T(8,128)(2,1)S(1)}, bf16[1024,768]{1,0:T(8,128)(2,1)}, u32[]{:S(2)}) copy-start(bf16[1024,768]{1,0:T(8,128)(2,1)} %get-tuple-element.89.refs_7_) | copy-start | bytes 4718596
  135.8 21.7 %copy-start.12 = (bf16[4,2,2,2,24,768]{5,4,3,2,1,0:T(8,128)(2,1)S(1)}, bf16[4,2,2,2,24,768]{5,4,3,2,1,0:T(8,128)(2,1)}, u32[]{:S(2)}) copy-start(bf16[4,2,2,2,24,768]{5,4,3,2,1,0:T(8,128)(2,1)} %get-tuple-element.86) | copy-start | bytes 3538948
  156.3 1.2 copy-start.23
  157.6 50.7 %copy-start.16 = (bf16[3,1040,768]{2,1,0:T(8,128)(2,1)S(1)}, bf16[3,1040,768]{2,1,0:T(8,128)(2,1)}, u32[]{:S(2)}) copy-start(bf16[3,1040,768]{2,1,0:T(8,128)(2,1)} %copy-done.15) | copy-start | bytes 14376964
  157.6 50.7 %copy-start.24 = (bf16[1040,768]{1,0:T(8,128)(2,1)S(1)}, bf16[1040,768]{1,0:T(8,128)(2,1)}, u32[]{:S(2)}) copy-start(bf16[1040,768]{1,0:T(8,128)(2,1)} %copy-done.23) | copy-start | bytes 4792324
  208.3 1.4 copy-start.27
  209.7 35.5 %copy-start.19 = (f32[1040,768]{1,0:T(8,128)S(1)}, f32[1040,768]{1,0:T(8,128)}, u32[]{:S(2)}) copy-start(f32[1040,768]{1,0:T(8,128)} %copy-done.18) | copy-start | bytes 9584644
  209.7 35.5 %copy-start.21 = (f32[1040,768]{1,0:T(8,128)S(1)}, f32[1040,768]{1,0:T(8,128)}, u32[]{:S(2)}) copy-start(f32[1040,768]{1,0:T(8,128)} %copy-done.20) | copy-start | bytes 9584644
  209.7 35.5 %copy-start.22 = (f32[1040,768]{1,0:T(8,128)S(1)}, f32[1040,768]{1,0:T(8,128)}, u32[]{:S(2)}) copy-start(f32[1040,768]{1,0:T(8,128)} %get-tuple-element.97.refs_4_) | copy-start | bytes 9584644
  209.7 35.5 %copy-start.26 = (bf16[1040,768]{1,0:T(8,128)(2,1)S(1)}, bf16[1040,768]{1,0:T(8,128)(2,1)}, u32[]{:S(2)}) copy-start(bf16[1040,768]{1,0:T(8,128)(2,1)} %copy-done.25) | copy-start | bytes 4792324
  243.1 2.2 copy-start.17
  245.2 29.4 %copy-start.2 = (bf16[4,2,2,2,24,2304]{5,4,3,2,1,0:T(8,128)(2,1)S(1)}, bf16[4,2,2,2,24,2304]{5,4,3,2,1,0:T(8,128)(2,1)}, u32[]{:S(2)}) copy-start(bf16[4,2,2,2,24,2304]{5,4,3,2,1,0:T(8,128)(2,1)} %get-tuple-element.78) | copy-start | bytes 10616836
  245.2 29.4 %copy-start.6 = (f32[16,768]{1,0:T(8,128)S(1)}, f32[16,768]{1,0:T(8,128)}, u32[]{:S(2)}) copy-start(f32[16,768]{1,0:T(8,128)} %get-tuple-element.79.mem_out_ref) | copy-start | bytes 147460
  274.6 2.1 copy-start.14
  276.7 1.4 copy-start.10
  278.1 0.6 copy-start.13
